TPU v7x, 32 devices: a whole 2x2x4 slice. The times are simulated.
32 devices in a mesh: pole: 2 (over x), prow: 16 (over z, y, core).
Axes of the slice: x: 2, y: 2, z: 4, core: 2. Of those that a mesh axis runs over, the one named last changes fastest.
Arguments:
- inverse_window: bfloat16 [8192, 4096], P(('pole', 'prow')), parts along dimension 0, may hold values from -8 to 8, as said below
- panel_one: bfloat16 [8192, 256], P(('pole', 'prow')), parts along dimension 0, may hold values from -0.09375 to 0.09375
- panel_two: bfloat16 [8192, 256], P(('pole', 'prow')), parts along dimension 0, may hold values from -0.09375 to 0.09375
- cross_block: bfloat16 [512, 256], P('pole'), parts along dimension 0, may hold values from -0.375 to 0.375
- diag_one: float32 [512, 256], P('pole'), parts along dimension 0, may hold values from -6 to 6
- diag_two: float32 [512, 256], P('pole'), parts along dimension 0, may hold values from -6 to 6
- row_super: int32 [4096], P('prow'), may hold values from 0 to 15, as said below
- struct_mask: int32 [2, 16], replicated, may hold values from 0 to 1, as said below
Outputs:
- column_one: bfloat16 [8192, 256], P(('pole', 'prow')), parts along dimension 0
- block_one: float32 [512, 256], P('pole'), parts along dimension 0
- column_two: bfloat16 [8192, 256], P(('pole', 'prow')), parts along dimension 0
- edge_block: float32 [512, 256], P('pole'), parts along dimension 0
- block_two: float32 [512, 256], P('pole'), parts along dimension 0
There are 2 independent parts, one for each index of `pole`. A program takes and returns all parts, laid end to end along the dimension named above; an argument that names none is the same for every part. Nothing has to cross between parts.
Inputs may be any that keep to these rules, and one draw needn't show every extreme that they name: `inverse_window`: symmetric. `row_super`: never falling; each ancestor supernode covers 256 // 2 to 384 consecutive rows, and one covers exactly 384. `struct_mask`: each aligned block of 256 window rows holds a row whose supernode lies in both structures.
All inputs are finite; a program needn't handle non-finite values.
Results may differ from a plain program's by a relative error of at most 0.0041.
Values may be sent and summed in bfloat16 or wider, within the bound.
No kernel may reach another device: no remote copies, remote signals or barrier semaphores. Data moves between devices by JAX's collectives and lax.ppermute only.
A program may use at most 128 MiB of HBM per device.

v0:
```python
import jax
import jax.numpy as jnp
from jax import lax
from jax.sharding import PartitionSpec as P


def row_weight(row_super, table):
    count = table.shape[0]
    equal = row_super[:, None] == jnp.arange(count, dtype=jnp.int32)[None, :]
    return jnp.sum(jnp.where(equal, table[None, :], 0), axis=1).astype(jnp.float32)


def transpose_dot(left, right):
    return lax.dot_general(
        left, right, (((0,), (0,)), ((), ())), preferred_element_type=jnp.float32
    )


def wide_transpose_dot(left, right):
    return lax.dot_general(
        left.astype(jnp.float32),
        right,
        (((0,), (0,)), ((), ())),
        precision=lax.Precision.HIGHEST,
        preferred_element_type=jnp.float32,
    )


def local(
    inverse_window, panel_one, panel_two, cross_block, diag_one, diag_two, row_super, struct_mask
):
    highest = lax.Precision.HIGHEST
    weight_one = row_weight(row_super, struct_mask[0])
    weight_two = row_weight(row_super, struct_mask[1])
    masked_one = (panel_one.astype(jnp.float32) * weight_one[:, None]).astype(jnp.bfloat16)
    masked_two = (panel_two.astype(jnp.float32) * weight_two[:, None]).astype(jnp.bfloat16)

    def add_piece(piece):
        return jnp.dot(inverse_window, piece, preferred_element_type=jnp.float32)

    image_one = add_piece(lax.all_gather(masked_one, "prow", axis=0, tiled=True))
    exact_one = -(weight_one[:, None] * image_one)
    schur_term = wide_transpose_dot(masked_one, exact_one)
    column_one = exact_one.astype(jnp.bfloat16)
    block_one = diag_one - lax.psum(schur_term, "prow")
    image_two = add_piece(lax.all_gather(masked_two, "prow", axis=0, tiled=True))
    carried = jnp.dot(column_one, cross_block, preferred_element_type=jnp.float32)
    exact_two = -(weight_two[:, None] * (image_two + carried))
    cross_term = transpose_dot(masked_two, column_one)
    cross_wide = cross_block.astype(jnp.float32)
    cross_sum = lax.psum(cross_term, "prow")
    edge_block = -(cross_sum.T + jnp.dot(block_one, cross_wide, precision=highest))
    schur_two = lax.psum(wide_transpose_dot(masked_two, exact_two), "prow")
    block_two = diag_two - schur_two - jnp.dot(cross_wide.T, edge_block, precision=highest)
    return (column_one, block_one, exact_two.astype(jnp.bfloat16), edge_block, block_two)


def solution(mesh):
    return jax.shard_map(
        local,
        mesh=mesh,
        in_specs=(
            P(("pole", "prow"), None),
            P(("pole", "prow"), None),
            P(("pole", "prow"), None),
            P("pole", None),
            P("pole", None),
            P("pole", None),
            P("prow"),
            P(),
        ),
        out_specs=(
            P(("pole", "prow"), None),
            P("pole", None),
            P(("pole", "prow"), None),
            P("pole", None),
            P("pole", None),
        ),
        check_vma=False,
    )
```

profile of v0, /device:TPU:0, one launch (start us, length us, event | category | flops | bytes accessed | tf_op | source)
XLA Modules:
  0.0 204.4 jit_solution(9440027859091282718)
XLA Ops:
  7.2 0.0 copy-start
  7.2 0.0 all-gather.3.cloned.1.call-start
  7.2 0.8 slice_bitcast_fusion.1
  8.1 0.8 select_reduce_fusion
  8.8 1.7 multiply_convert_fusion.1
  10.5 0.0 all-gather.3.cloned.1.call-update
  10.5 0.0 all-gather.5.cloned.1.call-start
  10.6 1.0 copy.18
  11.6 0.7 multiply_convert_fusion
  12.3 0.0 all-gather.5.cloned.1.call-update
  12.3 0.0 copy-start.1
  12.3 0.0 copy-start.3
  12.3 0.0 all-reduce.3.cloned.1.call-start
  12.4 42.5 %all-gather.3.cloned.1.call-done = bf16[4096,256]{1,0:T(8,128)(2,1)} async-done(((bf16[256,256]{1,0:T(8,128)(2,1)}), bf16[4096,256]{1,0:T(8,128)(2,1)}) %all-gather.3.cloned.1.call-update) | async-done | bytes 2097168 | tf_op jit(solution)/shard_map/all_gather | solution.py:41
  54.9 0.0 copy-done
  54.9 2.3 %fusion.4 = f32[256,256]{1,0:T(8,128)S(1)} fusion(bf16[4096,256]{1,0:T(8,128)(2,1)} %all-gather.3.cloned.1.call-done, bf16[256,4096]{1,0:T(8,128)(2,1)S(1)} %copy-done, f32[256]{0:T(256)S(1)} %convert_element_type.38), kind=kOutput, calls=%fused_computation.9 | convolution fusion | flops 537001984 | bytes 4457472 | tf_op jit(solution)/shard_map/dot_general | solution.py:39
  57.2 0.0 copy-done.1
  57.2 0.9 fusion.5
  58.2 0.0 copy-done.3
  58.2 1.0 fusion.9
  59.2 0.0 copy-start.2
  59.2 38.4 %all-gather.5.cloned.1.call-done = bf16[4096,256]{0,1:T(8,128)(2,1)} async-done(((bf16[256,256]{0,1:T(8,128)(2,1)}), bf16[4096,256]{0,1:T(8,128)(2,1)}) %all-gather.5.cloned.1.call-update) | async-done | bytes 2097168 | tf_op jit(solution)/shard_map/all_gather | solution.py:46
  97.6 2.3 %convolution_bitcast_fusion.1 = f32[256,256]{0,1:T(8,128)S(1)} fusion(bf16[4096,256]{0,1:T(8,128)(2,1)} %all-gather.5.cloned.1.call-done, bf16[256,4096]{1,0:T(8,128)(2,1)S(1)} %copy-done), kind=kOutput, calls=%fused_computation.7 | convolution fusion | flops 536870912 | bytes 4456448 | tf_op jit(solution)/shard_map/dot_general | solution.py:39
  99.9 0.0 copy-done.2
  100.0 0.0 copy-start.6
  100.0 0.2 fusion.8
  100.2 0.0 copy-start.7
  100.2 1.0 fusion.10
  101.3 0.0 all-reduce.3.cloned.1.call-update
  101.3 0.8 copy.22
  102.1 0.8 copy.21
  102.8 90.7 %all-reduce.3.cloned.1.call-done = (f32[256,256]{1,0:T(8,128)}, f32[256,256]{1,0:T(8,128)}, f32[256,256]{1,0:T(8,128)}) async-done(((f32[256,256]{1,0:T(8,128)}, f32[256,256]{1,0:T(8,128)}, f32[256,256]{1,0:T(8,128)}), (f32[256,256]{1,0:T(8,128)}, f32[256,256]{1,0:T(8,128)}, f32[256,256]{1,0:T(8,128)})) %all-reduce.3.cloned.1.call-update) | async-done | bytes 786448 | tf_op jit(solution)/shard_map/psum | solution.py:45
  193.5 0.0 copy-done.6
  193.5 1.0 sub.9
  194.5 0.0 copy-start.4
  194.5 1.3 fusion.1
  195.8 0.0 copy-start.5
  195.8 0.0 copy-done.7
  195.8 2.1 %fusion = f32[256,256]{1,0:T(8,128)} fusion(f32[256,256]{1,0:T(8,128)S(1)} %fusion.1, bf16[256,256]{1,0:T(8,128)(2,1)S(1)} %copy-done.2, f32[256,256]{1,0:T(8,128)S(1)} %copy-done.7, f32[256,256]{1,0:T(8,128)} %get-tuple-element.19), kind=kOutput, calls=%fused_computation.1 | convolution fusion | flops 201457664 | bytes 1179648 | tf_op jit(solution)/shard_map/dot_general | solution.py:54
  197.9 0.0 copy-done.4
  197.9 0.0 copy-done.5
  (3 shorter events, 0.0 us)
Async XLA Ops:
  7.2 47.7 %copy-start = (bf16[256,4096]{1,0:T(8,128)(2,1)S(1)}, bf16[256,4096]{1,0:T(8,128)(2,1)}, u32[]{:S(2)}) copy-start(bf16[256,4096]{1,0:T(8,128)(2,1)} %param.8) | copy-start | bytes 6291460
  7.2 47.7 %all-gather.3.cloned.1.call-start = ((), (), s32[]{:S(2)}) async-start(), calls=%async_computation | async-start | bytes 2228224 | tf_op jit(solution)/shard_map/all_gather | solution.py:41
  10.5 87.1 %all-gather.5.cloned.1.call-start = ((), (), s32[]{:S(2)}) async-start(), calls=%async_computation.1 | async-start | bytes 2228224 | tf_op jit(solution)/shard_map/all_gather | solution.py:46
  12.3 44.9 %copy-start.1 = (bf16[256,256]{0,1:T(8,128)(2,1)S(1)}, bf16[256,256]{0,1:T(8,128)(2,1)}, u32[]{:S(2)}) copy-start(bf16[256,256]{0,1:T(8,128)(2,1)} %multiply_convert_fusion) | copy-start | bytes 393220
  12.3 45.9 %copy-start.3 = (bf16[256,256]{1,0:T(8,128)(2,1)S(1)}, bf16[256,256]{1,0:T(8,128)(2,1)}, u32[]{:S(2)}) copy-start(bf16[256,256]{1,0:T(8,128)(2,1)} %multiply_convert_fusion.1) | copy-start | bytes 393220
  12.3 181.2 %all-reduce.3.cloned.1.call-start = ((), (), s32[]{:S(2)}) async-start(), calls=%async_computation.2 | async-start | bytes 1572864 | tf_op jit(solution)/shard_map/psum | solution.py:45
  59.2 40.7 %copy-start.2 = (bf16[256,256]{1,0:T(8,128)(2,1)S(1)}, bf16[256,256]{1,0:T(8,128)(2,1)}, u32[]{:S(2)}) copy-start(bf16[256,256]{1,0:T(8,128)(2,1)} %param.11) | copy-start | bytes 393220
  100.0 93.5 %copy-start.6 = (f32[256,256]{1,0:T(8,128)S(1)}, f32[256,256]{1,0:T(8,128)}, u32[]{:S(2)}) copy-start(f32[256,256]{1,0:T(8,128)} %param.12) | copy-start | bytes 786436
  100.2 95.6 %copy-start.7 = (f32[256,256]{1,0:T(8,128)S(1)}, f32[256,256]{1,0:T(8,128)}, u32[]{:S(2)}) copy-start(f32[256,256]{1,0:T(8,128)} %param.13) | copy-start | bytes 786436
  194.5 3.4 %copy-start.4 = (f32[256,256]{1,0:T(8,128)}, f32[256,256]{1,0:T(8,128)S(1)}, u32[]{:S(2)}) copy-start(f32[256,256]{1,0:T(8,128)S(1)} %sub.9) | copy-start | bytes 786436
  195.8 2.1 %copy-start.5 = (f32[256,256]{1,0:T(8,128)}, f32[256,256]{1,0:T(8,128)S(1)}, u32[]{:S(2)}) copy-start(f32[256,256]{1,0:T(8,128)S(1)} %fusion.1) | copy-start | bytes 786436
Sparse Core Ops, SparseCore 0:
  10.7 44.0 all-gather.2
  57.6 39.9 all-gather.4
  101.9 91.5 all-reduce.2
where the time goes:
time: 205 us; the launch traced here: 204 us
  waiting for transfers between devices  172 us (84%)
  between operations  13.9 us (7%)
  matrix products  11.3 us (6%)
  other arithmetic  4.12 us (2%)
  local copies, waits for them, and re-layouts  3.42 us (2%)
    psum x1, waiting for transfers between devices, local(): block_one = diag_one - lax.psum(schur_term, 'prow')  90.7 us
    all_gather x1, waiting for transfers between devices, local(): lax.all_gather(masked_one, 'prow', axis=0, tiled=True)  42.5 us
    all_gather x1, waiting for transfers between devices, local(): lax.all_gather(masked_two, 'prow', axis=0, tiled=True)  38.4 us
    dot_general x2, matrix products, add_piece(): return jnp.dot(inverse_window, piece, preferred_element_type=jnp.float32)  4.68 us
  transfers between devices with their start and end apart: 3, of which 3 were waited for; matrix products, arithmetic and copies ran while one was open for 4% of the time, Pallas kernels for 0%

commit v1 on v0

v1 whole, which is shorter than its diff:
```python
import functools

import jax
import jax.numpy as jnp
from jax import lax
from jax.experimental import pallas as pl
from jax.experimental.pallas import tpu as pltpu
from jax.sharding import PartitionSpec as P

F32, BF16 = jnp.float32, jnp.bfloat16
AXIS = "prow"
VMEM = pl.BlockSpec(memory_space=pltpu.VMEM)
SMEM = pl.BlockSpec(memory_space=pltpu.SMEM)


def dot(left, right):
    return jnp.dot(left, right, preferred_element_type=F32)


def dot_t(left, right):
    return lax.dot_general(left, right, (((0,), (0,)), ((), ())), preferred_element_type=F32)


def halves(x):
    high = x.astype(BF16)
    return high, (x - high.astype(F32)).astype(BF16)


def call(body, name, outs, args, n_smem=0, flops=0):
    size = sum(a.size * a.dtype.itemsize for a in args)
    return pl.pallas_call(
        body,
        name=name,
        out_shape=tuple(jax.ShapeDtypeStruct(s, d) for s, d in outs),
        in_specs=[SMEM] * n_smem + [VMEM] * (len(args) - n_smem),
        out_specs=tuple(VMEM for _ in outs),
        compiler_params=pltpu.CompilerParams(vmem_limit_bytes=32 << 20),
        cost_estimate=pl.CostEstimate(flops=flops, bytes_accessed=size, transcendentals=0),
    )(*args)


def mask_body(table, rows, one, two, m_one, m_two, w_one, w_two):
    n = one.shape[0]
    index = rows[...]
    on_diagonal = lax.broadcasted_iota(jnp.int32, (n, n), 0) == lax.broadcasted_iota(jnp.int32, (n, n), 1)
    ones = jnp.ones((n, n), BF16)
    for which, panel, masked, weights in ((0, one, m_one, w_one), (1, two, m_two, w_two)):
        weight = jnp.zeros(index.shape, F32)
        for s in range(table.shape[1]):
            weight = jnp.where(index == s, table[which, s].astype(F32), weight)
        chosen = jnp.where(on_diagonal, jnp.broadcast_to(weight, (n, n)), 0.0).astype(BF16)
        masked[...] = dot(chosen, panel[...]).astype(BF16)
        weights[...] = dot(chosen, ones).astype(BF16)


def swap_body(place, window, out):
    width = out.shape[0]
    other = 1 - place[0]
    for t in range(out.shape[1] // width):
        out[:, t * width : (t + 1) * width] = window[:, pl.ds((2 * t + other) * width, width)]


def image_body(place, window, swapped, mine, sibling, *rest):
    pieces, (own, other, total) = rest[:-3], rest[-3:]
    n = mine.shape[0]
    core = place[0]
    x_own = jnp.zeros(own.shape, F32)
    x_other = jnp.zeros(own.shape, F32)
    for k, piece in enumerate(pieces):
        chip = place[1 + k]
        value = piece[...]
        x_own += dot(window[:, pl.ds(pl.multiple_of((2 * chip + core) * n, n), n)], value)
        x_other += dot(swapped[:, pl.ds(pl.multiple_of(chip * n, n), n)], value)
    own[...] = x_own
    other[...] = x_other
    (a, b), (c, d) = halves(x_own), halves(x_other)
    total[...] = (dot_t(mine[...], a) + dot_t(sibling[...], c)) + (dot_t(mine[...], b) + dot_t(sibling[...], d))


def column_one_body(place, own, received, w_one, m_two, cross, column, carried, keep, send):
    exact = -(w_one[...].astype(F32) * (own[...] + received[...]))
    rounded = exact.astype(BF16)
    column[...] = rounded
    carried[...] = dot(rounded, cross[...])
    both = dot_t(m_two[...], rounded)
    half = both.shape[0] // 2
    first = place[0] == 0
    keep[...] = jnp.where(first, both[:half], both[half:])
    send[...] = jnp.where(first, both[half:], both[:half])


def column_two_body(own, received, w_two, carried, column):
    image = own[...] + received[...]
    column[...] = (-(w_two[...].astype(F32) * (image + carried[...]))).astype(BF16)


def pack_body(place, one, two, keep, send):
    n = one.shape[0]
    half = n // 2
    row = lax.broadcasted_iota(jnp.int32, (n, n), 0)
    col = lax.broadcasted_iota(jnp.int32, (n, n), 1)
    second = two[...]
    both = jnp.where(row <= col, one[...], second)
    diagonal = jnp.sum(jnp.where(row == col, second, 0.0), axis=0, keepdims=True)
    diagonal = jnp.broadcast_to(diagonal, (keep.shape[0] - half, n))
    first = place[0] == 0
    keep[:half] = jnp.where(first, both[:half], both[half:])
    send[:half] = jnp.where(first, both[half:], both[:half])
    keep[half:] = diagonal
    send[half:] = diagonal


def last_body(place, pack_a, pack_b, cross_a, cross_b, cross, diag_one, diag_two, block_one, edge, block_two):
    n = cross.shape[0]
    half = n // 2
    first = place[0] == 0

    def whole(a, b):
        return jnp.concatenate([jnp.where(first, a, b), jnp.where(first, b, a)], axis=0)

    row = lax.broadcasted_iota(jnp.int32, (n, n), 0)
    col = lax.broadcasted_iota(jnp.int32, (n, n), 1)
    packed = whole(pack_a[:half], pack_b[:half])
    turned = packed.T
    diagonal = jnp.where(first, pack_a[half : half + 1], pack_b[half : half + 1])
    s_one = jnp.where(row <= col, packed, turned)
    s_two = jnp.where(row > col, packed, turned)
    s_two = jnp.where(row == col, jnp.broadcast_to(diagonal, (n, n)), s_two)
    cross_sum = whole(cross_a[...], cross_b[...])
    c = cross[...]
    one = diag_one[...] + s_one
    block_one[...] = one
    a, b = halves(one)
    out = -(cross_sum.T + (dot(a, c) + dot(b, c)))
    edge[...] = out
    a, b = halves(out)
    d, e = halves(cross_sum)
    block_two[...] = diag_two[...] + s_two + (dot(d, c) + dot(e, c)) - (dot_t(c, a) + dot_t(c, b))


def local(
    inverse_window, panel_one, panel_two, cross_block, diag_one, diag_two, row_super, struct_mask, *, size
):
    chips = size // 2
    rows, width = panel_one.shape
    half = width // 2
    ring = [2 * r if r < chips // 2 else 2 * (chips - 1 - r) + 1 for r in range(chips)]
    position = [ring.index(t) for t in range(chips)]
    ahead = [(2 * ring[r] + c, 2 * ring[(r + 1) % chips] + c) for r in range(chips) for c in (0, 1)]
    back = [(b, a) for a, b in ahead]
    flip = [[(i, i ^ (1 << b)) for i in range(size)] for b in range(size.bit_length() - 1)]

    def send(x, perm):
        return lax.ppermute(x, AXIS, perm)

    me = lax.axis_index(AXIS)
    core = me % 2
    spot = jnp.array(position, jnp.int32)[me // 2]

    def chip_at(offset):
        return jnp.array(ring, jnp.int32)[(spot + offset + chips) % chips]

    where = core.reshape(1).astype(jnp.int32)

    square = ((rows, width), F32)
    tile = ((rows, width), BF16)
    m_one, m_two, w_one, w_two = call(
        mask_body,
        "mask",
        (tile, tile, tile, tile),
        (struct_mask, row_super.reshape(1, -1), panel_one, panel_two),
        n_smem=1,
    )
    (window_part,) = call(
        swap_body, "swap", (((rows, inverse_window.shape[1] // 2), BF16),), (where, inverse_window), n_smem=1
    )

    steps = chips // 2
    one, two, order_one, order_two = [m_one], [m_two], [0], [0]
    one_up = one_down = m_one
    two_up = two_down = m_two
    for k in range(1, steps):
        one_up, one_down = send(one_up, ahead), send(one_down, back)
        two_up, two_down = send(two_up, ahead), send(two_down, back)
        one += [one_up, one_down]
        two += [two_up, two_down]
        order_one += [-k, k]
        order_two += [-k, k]
    one.append(send(one_up, ahead))
    two.append(send(two_down, back))
    order_one.append(-steps)
    order_two.append(steps)

    swapped = send(window_part, flip[0])
    sibling_one = send(m_one, flip[0])
    sibling_two = send(m_two, flip[0])
    flops = 2 * 2 * rows * width * (width + inverse_window.shape[1] // 2)

    def image(name, order, pieces, mine, sibling):
        place = jnp.stack([core] + [chip_at(d) for d in order]).astype(jnp.int32)
        return call(
            image_body,
            name,
            (square, square, ((width, width), F32)),
            (place, inverse_window, swapped, mine, sibling, *pieces),
            n_smem=1,
            flops=flops,
        )

    own_one, other_one, total_one = image("image_one", order_one, one, m_one, sibling_one)
    received_one = send(other_one, flip[0])
    column_one, carried, keep_x, send_x = call(
        column_one_body,
        "column_one",
        (tile, square, ((half, width), F32), ((half, width), F32)),
        (where, own_one, received_one, w_one, m_two, cross_block),
        n_smem=1,
    )
    own_two, other_two, total_two = image("image_two", order_two, two, m_two, sibling_two)
    keep_p, send_p = call(
        pack_body,
        "pack",
        (((half + 16, width), F32), ((half + 16, width), F32)),
        (where, total_one, total_two),
        n_smem=1,
    )
    received_two = send(other_two, flip[0])
    (column_two,) = call(column_two_body, "column_two", (tile,), (own_two, received_two, w_two, carried))

    def summed(keep, away):
        value = keep + send(away, flip[0])
        for perm in flip[1:]:
            value = value.astype(BF16)
            value = value.astype(F32) + send(value, perm).astype(F32)
        return value, send(value, flip[0])

    cross_a, cross_b = summed(keep_x, send_x)
    pack_a, pack_b = summed(keep_p, send_p)
    full = ((width, width), F32)
    block_one, edge_block, block_two = call(
        last_body,
        "last",
        (full, full, full),
        (where, pack_a, pack_b, cross_a, cross_b, cross_block, diag_one, diag_two),
        n_smem=1,
    )
    return column_one, block_one, column_two, edge_block, block_two


def solution(mesh):
    return jax.shard_map(
        functools.partial(local, size=mesh.shape[AXIS]),
        mesh=mesh,
        in_specs=(
            P(("pole", "prow"), None),
            P(("pole", "prow"), None),
            P(("pole", "prow"), None),
            P("pole", None),
            P("pole", None),
            P("pole", None),
            P("prow"),
            P(),
        ),
        out_specs=(
            P(("pole", "prow"), None),
            P("pole", None),
            P(("pole", "prow"), None),
            P("pole", None),
            P("pole", None),
        ),
        check_vma=False,
    )
```

time: 205 us -> 85 us (0.41)
  waiting for transfers between devices: 172 us -> 12.3 us
  starting transfers between devices: 0.12 us -> 27.2 us
  local copies, waits for them, and re-layouts: 3.42 us -> 28.3 us
  matrix products: 11.3 us -> 0 us
  Pallas kernels: 0 us -> 9.75 us
  between operations: 13.9 us -> 6.7 us
  other arithmetic: 4.12 us -> 0.14 us
    psum x1 -> x0, waiting for transfers between devices: 90.7 us -> none  [local(): block_one = diag_one - lax.psum(schur_term, 'prow')]
    all_gather x2 -> x0, waiting for transfers between devices: 80.9 us -> none  [the longest x1 42.5 us: local(): lax.all_gather(masked_one, 'prow', axis=0, tiled=True)]
    ppermute x0 -> x29, starting transfers between devices: none -> 27.2 us  [send(): return lax.ppermute(x, AXIS, perm)]
    unnamed x19 -> x70, local copies, waits for them, and re-layouts: 2.58 us -> 16.9 us
    ppermute x0 -> x29, waiting for transfers between devices: none -> 12.3 us  [send(): return lax.ppermute(x, AXIS, perm)]
    dot_general x8 -> x0, matrix products: 11.3 us -> none  [the longest x2 4.68 us: add_piece(): return jnp.dot(inverse_window, piece, preferred_element_type=jnp.float32)]
    another operation x0 -> x2, local copies, waits for them, and re-layouts: none -> 10.1 us  [image(): place = jnp.stack([core] + [chip_at(d) for d in order]).astype(jnp.int32)]
    pallas_call x0 -> x8, Pallas kernels: none -> 9.75 us  [call(): pl.pallas_call(body, name=name, out_shape=tuple((jax.ShapeDtypeStruct(s,...]
  transfers between devices with their start and end apart: 3 -> 29, of which waited for: 3 -> 9; matrix products, arithmetic and copies ran while one was open for 4% -> 14% of each run, Pallas kernels for 0% -> 9%
where the time goes in v1:
time: 85 us; the launch traced here: 84.4 us
  local copies, waits for them, and re-layouts  28.3 us (33%)
  starting transfers between devices  27.2 us (32%)
  waiting for transfers between devices  12.3 us (14%)
  Pallas kernels  9.75 us (11%)
  between operations  6.7 us (8%)
    ppermute x29, starting transfers between devices, send(): return lax.ppermute(x, AXIS, perm)  27.2 us
    unnamed x70, local copies, waits for them, and re-layouts  16.9 us
    ppermute x29, waiting for transfers between devices, send(): return lax.ppermute(x, AXIS, perm)  12.3 us
    another operation x2, local copies, waits for them, and re-layouts, image(): place = jnp.stack([core] + [chip_at(d) for d in order]).astype(jnp.int32)  10.1 us
    pallas_call x8, Pallas kernels, call(): pl.pallas_call(body, name=name, out_shape=tuple((jax.ShapeDtypeStruct(s,...  9.75 us
  transfers between devices with their start and end apart: 29, of which 9 were waited for; matrix products, arithmetic and copies ran while one was open for 14% of the time, Pallas kernels for 9%

profile of v1, /device:TPU:0, one launch (start us, length us, event | category | flops | bytes accessed | tf_op | source)
XLA Modules:
  0.0 84.4 jit_solution(8072303467608617817)
XLA Ops:
  0.7 1.6 %copy-done = bf16[256,4096]{1,0:T(8,128)(2,1)S(1)} copy-done((bf16[256,4096]{1,0:T(8,128)(2,1)S(1)}, bf16[256,4096]{1,0:T(8,128)(2,1)}, u32[]{:S(2)}) %copy-start) | copy-done | bytes 2097176
  2.3 1.2 %swap.1 = bf16[256,2048]{1,0:T(8,128)(2,1)} custom-call(s32[1]{0:T(128)} %bitcast.place, bf16[256,4096]{1,0:T(8,128)(2,1)S(1)} %copy-done), custom_call_target="tpu_custom_call" | custom-call | bytes 2097156 | tf_op jit(solution)/shard_map/swap/pallas_call | solution.py:31
  3.5 0.5 collective-permute-start
  3.9 0.8 %mask.1 = (bf16[256,256]{1,0:T(8,128)(2,1)S(1)}, bf16[256,256]{1,0:T(8,128)(2,1)S(1)}, bf16[256,256]{1,0:T(8,128)(2,1)S(1)}, bf16[256,256]{1,0:T(8,128)(2,1)S(1)}) custom-call(s32[2,16]{1,0:T(2,128)S(1)} %copy-done.31, s32[1,256]{1,0:T(1,128)S(1)} %bitcast.11, bf16[256,256]{1,0:T(8,128)(2,1)S(1)} %copy-done.27, bf16[256,256]{1,0:T(8,128)(2,1)S(1)} %copy-done.28), custom_call_target="tpu_custom_call" | custom-call | bytes 263296 | tf_op jit(solution)/shard_map/mask/pallas_call | solution.py:31
  4.8 0.6 copy-done.9
  5.5 0.6 copy-done.29
  6.1 2.6 %collective-permute-start.2 = (bf16[256,256]{1,0:T(8,128)(2,1)S(1)}, bf16[256,256]{1,0:T(8,128)(2,1)S(1)}, u32[]{:S(2)}, u32[]{:S(2)}) collective-permute-start(bf16[256,256]{1,0:T(8,128)(2,1)S(1)} %get-tuple-element.24.mine.rest_0_), channel_id=1, source_target_pairs={{0,4},{1,5},{4,8},{5,9},{8,12},{9,13},{12,14},{13,15},{14,10},{15,... | collective-permute-start | bytes 393224 | tf_op jit(solution)/shard_map/ppermute | solution.py:154
  8.7 0.2 collective-permute-start.1
  8.9 0.2 collective-permute-start.3
  9.1 1.7 %collective-permute-start.12 = (bf16[256,256]{1,0:T(8,128)(2,1)S(1)}, bf16[256,256]{1,0:T(8,128)(2,1)S(1)}, u32[]{:S(2)}, u32[]{:S(2)}) collective-permute-start(bf16[256,256]{1,0:T(8,128)(2,1)S(1)} %get-tuple-element.28.m_two.mine.rest_0_), channel_id=1, source_target_pairs={{4,0},{5,1},{8,4},{9,5},{12,8},{13,9},{14,12},{15,13},{10,14},{11,... | collective-permute-start | bytes 393224 | tf_op jit(solution)/shard_map/ppermute | solution.py:154
  10.9 1.9 %collective-permute-done.2.rest_1_ = bf16[256,256]{1,0:T(8,128)(2,1)S(1)} collective-permute-done((bf16[256,256]{1,0:T(8,128)(2,1)S(1)}, bf16[256,256]{1,0:T(8,128)(2,1)S(1)}, u32[]{:S(2)}, u32[]{:S(2)}) %collective-permute-start.2) | collective-permute-done | bytes 131104 | tf_op jit(solution)/shard_map/ppermute | solution.py:154
  12.8 1.8 %collective-permute-start.4 = (bf16[256,256]{1,0:T(8,128)(2,1)S(1)}, bf16[256,256]{1,0:T(8,128)(2,1)S(1)}, u32[]{:S(2)}, u32[]{:S(2)}) collective-permute-start(bf16[256,256]{1,0:T(8,128)(2,1)S(1)} %collective-permute-done.2.rest_1_), channel_id=1, source_target_pairs={{0,4},{1,5},{4,8},{5,9},{8,12},{9,13},{12,14},{13,15},{14,10},{15,... | collective-permute-start | bytes 393224 | tf_op jit(solution)/shard_map/ppermute | solution.py:154
  14.6 0.7 copy-done.17
  15.2 1.6 %collective-permute-start.11 = (bf16[256,256]{1,0:T(8,128)(2,1)S(1)}, bf16[256,256]{1,0:T(8,128)(2,1)S(1)}, u32[]{:S(2)}, u32[]{:S(2)}) collective-permute-start(bf16[256,256]{1,0:T(8,128)(2,1)S(1)} %get-tuple-element.28.m_two.mine.rest_0_), channel_id=1, source_target_pairs={{0,4},{1,5},{4,8},{5,9},{8,12},{9,13},{12,14},{13,15},{14,10},{15,... | collective-permute-start | bytes 393224 | tf_op jit(solution)/shard_map/ppermute | solution.py:154
  16.8 0.5 collective-permute-start.5
  17.3 0.7 copy-done.19
  17.9 0.2 collective-permute-start.14
  18.2 0.6 copy-done.11
  18.9 1.7 %collective-permute-start.6 = (bf16[256,256]{1,0:T(8,128)(2,1)S(1)}, bf16[256,256]{1,0:T(8,128)(2,1)}, u32[]{:S(2)}, u32[]{:S(2)}) collective-permute-start(bf16[256,256]{1,0:T(8,128)(2,1)S(1)} %collective-permute-done.4.rest_3_), channel_id=1, source_target_pairs={{0,4},{1,5},{4,8},{5,9},{8,12},{9,13},{12,14},{13,15},{14,10},{15,... | collective-permute-start | bytes 393224 | tf_op jit(solution)/shard_map/ppermute | solution.py:154
  20.6 0.7 copy-done.21
  21.3 0.3 collective-permute-done.11.rest_1_
  21.5 1.5 %collective-permute-start.13 = (bf16[256,256]{1,0:T(8,128)(2,1)S(1)}, bf16[256,256]{1,0:T(8,128)(2,1)}, u32[]{:S(2)}, u32[]{:S(2)}) collective-permute-start(bf16[256,256]{1,0:T(8,128)(2,1)S(1)} %collective-permute-done.11.rest_1_), channel_id=1, source_target_pairs={{0,4},{1,5},{4,8},{5,9},{8,12},{9,13},{12,14},{13,15},{14,10},{15,... | collective-permute-start | bytes 393224 | tf_op jit(solution)/shard_map/ppermute | solution.py:154
  23.1 0.7 copy-done.13
  23.7 0.5 collective-permute-start.7
  24.2 0.7 copy-done.23
  24.9 1.5 %collective-permute-start.16 = (bf16[256,256]{1,0:T(8,128)(2,1)S(1)}, bf16[256,256]{1,0:T(8,128)(2,1)}, u32[]{:S(2)}, u32[]{:S(2)}) collective-permute-start(bf16[256,256]{1,0:T(8,128)(2,1)S(1)} %collective-permute-done.14.rest_4_), channel_id=1, source_target_pairs={{4,0},{5,1},{8,4},{9,5},{12,8},{13,9},{14,12},{15,13},{10,14},{11,... | collective-permute-start | bytes 393224 | tf_op jit(solution)/shard_map/ppermute | solution.py:154
  26.4 0.7 copy-done.15
  27.0 0.6 collective-permute-start.8
  27.6 1.3 %collective-permute-done.7.rest_6_ = bf16[256,256]{1,0:T(8,128)(2,1)S(1)} collective-permute-done((bf16[256,256]{1,0:T(8,128)(2,1)S(1)}, bf16[256,256]{1,0:T(8,128)(2,1)S(1)}, u32[]{:S(2)}, u32[]{:S(2)}) %collective-permute-start.7) | collective-permute-done | bytes 131104 | tf_op jit(solution)/shard_map/ppermute | solution.py:154
  28.9 0.7 copy-done.25
  29.6 1.6 %collective-permute-start.15 = (bf16[256,256]{1,0:T(8,128)(2,1)}, bf16[256,256]{1,0:T(8,128)(2,1)}, u32[]{:S(2)}, u32[]{:S(2)}) collective-permute-start(bf16[256,256]{1,0:T(8,128)(2,1)} %collective-permute-done.13.rest_3_), channel_id=1, source_target_pairs={{0,4},{1,5},{4,8},{5,9},{8,12},{9,13},{12,14},{13,15},{14,10},{15,... | collective-permute-start | bytes 393224 | tf_op jit(solution)/shard_map/ppermute | solution.py:154
  31.1 0.5 collective-permute-start.17
  31.6 0.6 dynamic_slice.51
  38.0 0.7 fusion
  38.7 5.1 %stack.8.place = s32[9]{0:T(128)S(1)} concatenate(s32[1]{0:T(128)} %bitcast.place, s32[1]{0:T(128)} %get-tuple-element.50, s32[1]{0:T(128)} %get-tuple-element.49, s32[1]{0:T(128)} %get-tuple-element.48, s32[1]{0:T(128)} %get-tuple-element.47, s32[1]{0:T(128)} %get-tuple-element.46, s32[1]{0:T(128)} %get-tuple-element.45, s32[1]{0:T(128)} %get-tuple-element.44, s32[1]{0:T(128)} %get-tuple-element.51), dimensions={0} | concatenate | bytes 72 | tf_op jit(solution)/shard_map/stack | solution.py:200
  43.8 0.9 %copy-done.18 = bf16[256,256]{1,0:T(8,128)(2,1)S(1)} copy-done((bf16[256,256]{1,0:T(8,128)(2,1)S(1)}, bf16[256,256]{1,0:T(8,128)(2,1)}, u32[]{:S(2)}) %copy-start.18) | copy-done | bytes 131096
  44.7 0.9 %copy-done.20 = bf16[256,256]{1,0:T(8,128)(2,1)S(1)} copy-done((bf16[256,256]{1,0:T(8,128)(2,1)S(1)}, bf16[256,256]{1,0:T(8,128)(2,1)}, u32[]{:S(2)}) %copy-start.20) | copy-done | bytes 131096
  45.6 0.9 %copy-done.22 = bf16[256,256]{1,0:T(8,128)(2,1)S(1)} copy-done((bf16[256,256]{1,0:T(8,128)(2,1)S(1)}, bf16[256,256]{1,0:T(8,128)(2,1)}, u32[]{:S(2)}) %copy-start.22) | copy-done | bytes 131096
  46.5 0.9 %copy-done.24 = bf16[256,256]{1,0:T(8,128)(2,1)S(1)} copy-done((bf16[256,256]{1,0:T(8,128)(2,1)S(1)}, bf16[256,256]{1,0:T(8,128)(2,1)}, u32[]{:S(2)}) %copy-start.24) | copy-done | bytes 131096
  47.4 0.9 %copy-done.26 = bf16[256,256]{1,0:T(8,128)(2,1)S(1)} copy-done((bf16[256,256]{1,0:T(8,128)(2,1)S(1)}, bf16[256,256]{1,0:T(8,128)(2,1)}, u32[]{:S(2)}) %copy-start.26) | copy-done | bytes 131096
  48.3 2.5 %image_one.1 = (f32[256,256]{1,0:T(8,128)S(1)}, f32[256,256]{1,0:T(8,128)}, f32[256,256]{1,0:T(8,128)S(1)}) custom-call(s32[9]{0:T(128)S(1)} %stack.8.place, bf16[256,4096]{1,0:T(8,128)(2,1)S(1)} %copy-done.1, bf16[256,2048]{1,0:T(8,128)(2,1)S(1)} %collective-permute-done.swapped, bf16[256,256]{1,0:T(8,128)(2,1)S(1)} %get-tuple-element.24.mine.rest_0_, ...), custom_call_target="tpu_custom_call" | custom-call | flops 603979776 | bytes 4456484 | tf_op jit(solution)/shard_map/image_one/pallas_call | solution.py:31
  50.8 0.7 copy-done.3
  51.5 0.7 copy-done.5
  52.2 5.0 %stack.9.place = s32[9]{0:T(128)S(1)} concatenate(s32[1]{0:T(128)} %bitcast.place, s32[1]{0:T(128)} %get-tuple-element.50, s32[1]{0:T(128)} %get-tuple-element.49, s32[1]{0:T(128)} %get-tuple-element.48, s32[1]{0:T(128)} %get-tuple-element.47, s32[1]{0:T(128)} %get-tuple-element.46, s32[1]{0:T(128)} %get-tuple-element.45, s32[1]{0:T(128)} %get-tuple-element.44, s32[1]{0:T(128)} %get-tuple-element.43), dimensions={0} | concatenate | bytes 72 | tf_op jit(solution)/shard_map/stack | solution.py:200
  57.4 1.0 %copy-done.12 = bf16[256,256]{1,0:T(8,128)(2,1)S(1)} copy-done((bf16[256,256]{1,0:T(8,128)(2,1)S(1)}, bf16[256,256]{1,0:T(8,128)(2,1)}, u32[]{:S(2)}) %copy-start.12) | copy-done | bytes 131096
  58.3 0.9 %copy-done.14 = bf16[256,256]{1,0:T(8,128)(2,1)S(1)} copy-done((bf16[256,256]{1,0:T(8,128)(2,1)S(1)}, bf16[256,256]{1,0:T(8,128)(2,1)}, u32[]{:S(2)}) %copy-start.14) | copy-done | bytes 131096
  59.2 0.9 %copy-done.16 = bf16[256,256]{1,0:T(8,128)(2,1)S(1)} copy-done((bf16[256,256]{1,0:T(8,128)(2,1)S(1)}, bf16[256,256]{1,0:T(8,128)(2,1)}, u32[]{:S(2)}) %copy-start.16) | copy-done | bytes 131096
  60.1 2.4 %image_two.1 = (f32[256,256]{1,0:T(8,128)S(1)}, f32[256,256]{1,0:T(8,128)S(1)}, f32[256,256]{1,0:T(8,128)S(1)}) custom-call(s32[9]{0:T(128)S(1)} %stack.9.place, bf16[256,4096]{1,0:T(8,128)(2,1)S(1)} %copy-done.1, bf16[256,2048]{1,0:T(8,128)(2,1)S(1)} %collective-permute-done.swapped, bf16[256,256]{1,0:T(8,128)(2,1)S(1)} %get-tuple-element.28.m_two.mine.rest_0_, ...), custom_call_target="tpu_custom_call" | custom-call | flops 603979776 | bytes 4456484 | tf_op jit(solution)/shard_map/image_two/pallas_call | solution.py:31
  62.7 0.6 collective-permute-start.18
  63.3 0.7 column_one.1
  64.1 0.4 collective-permute-start.23
  64.5 1.5 %collective-permute-start.19 = (bf16[144,256]{1,0:T(8,128)(2,1)S(1)}, bf16[144,256]{1,0:T(8,128)(2,1)S(1)}, u32[]{:S(2)}, u32[]{:S(2)}) collective-permute-start(bf16[144,256]{1,0:T(8,128)(2,1)S(1)} %add_convert_fusion.2), channel_id=1, source_target_pairs={{0,2},{1,3},{2,0},{3,1},{4,6},{5,7},{6,4},{7,5},{8,10},{9,11},{10,... | collective-permute-start | bytes 221192 | tf_op jit(solution)/shard_map/ppermute | solution.py:154
  66.0 1.0 %collective-permute-start.24 = (bf16[128,256]{1,0:T(8,128)(2,1)S(1)}, bf16[128,256]{1,0:T(8,128)(2,1)S(1)}, u32[]{:S(2)}, u32[]{:S(2)}) collective-permute-start(bf16[128,256]{1,0:T(8,128)(2,1)S(1)} %add_convert_fusion.5), channel_id=1, source_target_pairs={{0,2},{1,3},{2,0},{3,1},{4,6},{5,7},{6,4},{7,5},{8,10},{9,11},{10,... | collective-permute-start | bytes 196616 | tf_op jit(solution)/shard_map/ppermute | solution.py:154
  67.0 2.5 %collective-permute-done.19 = bf16[144,256]{1,0:T(8,128)(2,1)S(1)} collective-permute-done((bf16[144,256]{1,0:T(8,128)(2,1)S(1)}, bf16[144,256]{1,0:T(8,128)(2,1)S(1)}, u32[]{:S(2)}, u32[]{:S(2)}) %collective-permute-start.19) | collective-permute-done | bytes 73760 | tf_op jit(solution)/shard_map/ppermute | solution.py:154
  69.5 1.6 %collective-permute-start.20 = (bf16[144,256]{1,0:T(8,128)(2,1)S(1)}, bf16[144,256]{1,0:T(8,128)(2,1)S(1)}, u32[]{:S(2)}, u32[]{:S(2)}) collective-permute-start(bf16[144,256]{1,0:T(8,128)(2,1)S(1)} %add_convert_fusion.1), channel_id=1, source_target_pairs={{0,4},{1,5},{2,6},{3,7},{4,0},{5,1},{6,2},{7,3},{8,12},{9,13},{10,... | collective-permute-start | bytes 221192 | tf_op jit(solution)/shard_map/ppermute | solution.py:154
  71.1 0.9 %collective-permute-start.25 = (bf16[128,256]{1,0:T(8,128)(2,1)S(1)}, bf16[128,256]{1,0:T(8,128)(2,1)S(1)}, u32[]{:S(2)}, u32[]{:S(2)}) collective-permute-start(bf16[128,256]{1,0:T(8,128)(2,1)S(1)} %add_convert_fusion.4), channel_id=1, source_target_pairs={{0,4},{1,5},{2,6},{3,7},{4,0},{5,1},{6,2},{7,3},{8,12},{9,13},{10,... | collective-permute-start | bytes 196616 | tf_op jit(solution)/shard_map/ppermute | solution.py:154
  72.0 1.9 %collective-permute-done.20 = bf16[144,256]{1,0:T(8,128)(2,1)S(1)} collective-permute-done((bf16[144,256]{1,0:T(8,128)(2,1)S(1)}, bf16[144,256]{1,0:T(8,128)(2,1)S(1)}, u32[]{:S(2)}, u32[]{:S(2)}) %collective-permute-start.20) | collective-permute-done | bytes 73760 | tf_op jit(solution)/shard_map/ppermute | solution.py:154
  73.9 2.6 %collective-permute-start.21 = (bf16[144,256]{1,0:T(8,128)(2,1)S(1)}, bf16[144,256]{1,0:T(8,128)(2,1)S(1)}, u32[]{:S(2)}, u32[]{:S(2)}) collective-permute-start(bf16[144,256]{1,0:T(8,128)(2,1)S(1)} %add_convert_fusion), channel_id=1, source_target_pairs={{0,8},{1,9},{2,10},{3,11},{4,12},{5,13},{6,14},{7,15},{8,0},{9,1},... | collective-permute-start | bytes 221192 | tf_op jit(solution)/shard_map/ppermute | solution.py:154
  76.5 1.4 %collective-permute-start.26 = (bf16[128,256]{1,0:T(8,128)(2,1)S(1)}, bf16[128,256]{1,0:T(8,128)(2,1)S(1)}, u32[]{:S(2)}, u32[]{:S(2)}) collective-permute-start(bf16[128,256]{1,0:T(8,128)(2,1)S(1)} %add_convert_fusion.3), channel_id=1, source_target_pairs={{0,8},{1,9},{2,10},{3,11},{4,12},{5,13},{6,14},{7,15},{8,0},{9,1},... | collective-permute-start | bytes 196616 | tf_op jit(solution)/shard_map/ppermute | solution.py:154
  77.9 1.6 %collective-permute-done.21 = bf16[144,256]{1,0:T(8,128)(2,1)S(1)} collective-permute-done((bf16[144,256]{1,0:T(8,128)(2,1)S(1)}, bf16[144,256]{1,0:T(8,128)(2,1)S(1)}, u32[]{:S(2)}, u32[]{:S(2)}) %collective-permute-start.21) | collective-permute-done | bytes 73760 | tf_op jit(solution)/shard_map/ppermute | solution.py:154
  79.6 2.1 %collective-permute-done.26 = bf16[128,256]{1,0:T(8,128)(2,1)S(1)} collective-permute-done((bf16[128,256]{1,0:T(8,128)(2,1)S(1)}, bf16[128,256]{1,0:T(8,128)(2,1)S(1)}, u32[]{:S(2)}, u32[]{:S(2)}) %collective-permute-start.26) | collective-permute-done | bytes 65568 | tf_op jit(solution)/shard_map/ppermute | solution.py:154
  81.9 0.7 column_two.1
  82.6 0.6 collective-permute-done.27.cross_b
  83.2 1.3 %last.1 = (f32[256,256]{1,0:T(8,128)}, f32[256,256]{1,0:T(8,128)}, f32[256,256]{1,0:T(8,128)}) custom-call(s32[1]{0:T(128)} %bitcast.place, f32[144,256]{1,0:T(8,128)S(1)} %convert_add_fusion.pack_a, f32[144,256]{1,0:T(8,128)S(1)} %collective-permute-done.22.pack_b, f32[128,256]{1,0:T(8,128)S(1)} %convert_add_fusion.1.cross_a, ...), custom_call_target="tpu_custom_call" | custom-call | bytes 1212420 | tf_op jit(solution)/shard_map/last/pallas_call | solution.py:31
  (84 shorter events, 0.7 us)
Async XLA Ops:
  0.6 31.0 %copy-start.34 = (s32[8]{0:T(128)S(1)}, s32[8]{0:T(128)}, u32[]{:S(2)}) copy-start(s32[8]{0:T(128)} %constant.122.clone) | copy-start | bytes 100
  0.6 37.3 %copy-start.33 = (s32[8]{0:T(128)S(1)}, s32[8]{0:T(128)}, u32[]{:S(2)}) copy-start(s32[8]{0:T(128)} %constant.123.clone) | copy-start | bytes 100
  0.7 3.3 %copy-start.31 = (s32[2,16]{1,0:T(2,128)S(1)}, s32[2,16]{1,0:T(2,128)}, u32[]{:S(2)}) copy-start(s32[2,16]{1,0:T(2,128)} %table.1) | copy-start | bytes 388
  0.7 3.3 %copy-start.32 = (s32[256]{0:T(256)S(1)}, s32[256]{0:T(256)}, u32[]{:S(2)}) copy-start(s32[256]{0:T(256)} %param.31) | copy-start | bytes 3076
  0.7 1.6 %copy-start = (bf16[256,4096]{1,0:T(8,128)(2,1)S(1)}, bf16[256,4096]{1,0:T(8,128)(2,1)}, u32[]{:S(2)}) copy-start(bf16[256,4096]{1,0:T(8,128)(2,1)} %window.5) | copy-start | bytes 6291460
  2.3 1.7 %copy-start.27 = (bf16[256,256]{1,0:T(8,128)(2,1)S(1)}, bf16[256,256]{1,0:T(8,128)(2,1)}, u32[]{:S(2)}) copy-start(bf16[256,256]{1,0:T(8,128)(2,1)} %one.1) | copy-start | bytes 393220
  2.3 1.7 %copy-start.28 = (bf16[256,256]{1,0:T(8,128)(2,1)S(1)}, bf16[256,256]{1,0:T(8,128)(2,1)}, u32[]{:S(2)}) copy-start(bf16[256,256]{1,0:T(8,128)(2,1)} %two.1) | copy-start | bytes 393220
  2.3 41.5 %copy-start.1 = (bf16[256,4096]{1,0:T(8,128)(2,1)S(1)}, bf16[256,4096]{1,0:T(8,128)(2,1)}, u32[]{:S(2)}) copy-start(bf16[256,4096]{1,0:T(8,128)(2,1)} %window.5) | copy-start | bytes 6291460
  3.5 40.3 %collective-permute-start = (bf16[256,2048]{1,0:T(8,128)(2,1)}, bf16[256,2048]{1,0:T(8,128)(2,1)S(1)}, u32[]{:S(2)}, u32[]{:S(2)}) collective-permute-start(bf16[256,2048]{1,0:T(8,128)(2,1)} %swap.1), channel_id=1, source_target_pairs={{0,1},{1,0},{2,3},{3,2},{4,5},{5,4},{6,7},{7,6},{8,9},{9,8},{10,11... | collective-permute-start | bytes 3145736 | tf_op jit(solution)/shard_map/ppermute | solution.py:154
  4.8 0.7 copy-start.9
  5.5 0.6 copy-start.29
  6.1 6.7 %collective-permute-start.2 = (bf16[256,256]{1,0:T(8,128)(2,1)S(1)}, bf16[256,256]{1,0:T(8,128)(2,1)S(1)}, u32[]{:S(2)}, u32[]{:S(2)}) collective-permute-start(bf16[256,256]{1,0:T(8,128)(2,1)S(1)} %get-tuple-element.24.mine.rest_0_), channel_id=1, source_target_pairs={{0,4},{1,5},{4,8},{5,9},{8,12},{9,13},{12,14},{13,15},{14,10},{15,... | collective-permute-start | bytes 393224 | tf_op jit(solution)/shard_map/ppermute | solution.py:154
  8.7 5.9 %collective-permute-start.1 = (bf16[256,256]{1,0:T(8,128)(2,1)S(1)}, bf16[256,256]{1,0:T(8,128)(2,1)S(1)}, u32[]{:S(2)}, u32[]{:S(2)}) collective-permute-start(bf16[256,256]{1,0:T(8,128)(2,1)S(1)} %get-tuple-element.24.mine.rest_0_), channel_id=1, source_target_pairs={{0,1},{1,0},{2,3},{3,2},{4,5},{5,4},{6,7},{7,6},{8,9},{9,8},{10,11... | collective-permute-start | bytes 393224 | tf_op jit(solution)/shard_map/ppermute | solution.py:154
  8.9 7.9 %collective-permute-start.3 = (bf16[256,256]{1,0:T(8,128)(2,1)S(1)}, bf16[256,256]{1,0:T(8,128)(2,1)S(1)}, u32[]{:S(2)}, u32[]{:S(2)}) collective-permute-start(bf16[256,256]{1,0:T(8,128)(2,1)S(1)} %get-tuple-element.24.mine.rest_0_), channel_id=1, source_target_pairs={{4,0},{5,1},{8,4},{9,5},{12,8},{13,9},{14,12},{15,13},{10,14},{11,... | collective-permute-start | bytes 393224 | tf_op jit(solution)/shard_map/ppermute | solution.py:154
  9.1 8.8 %collective-permute-start.12 = (bf16[256,256]{1,0:T(8,128)(2,1)S(1)}, bf16[256,256]{1,0:T(8,128)(2,1)S(1)}, u32[]{:S(2)}, u32[]{:S(2)}) collective-permute-start(bf16[256,256]{1,0:T(8,128)(2,1)S(1)} %get-tuple-element.28.m_two.mine.rest_0_), channel_id=1, source_target_pairs={{4,0},{5,1},{8,4},{9,5},{12,8},{13,9},{14,12},{15,13},{10,14},{11,... | collective-permute-start | bytes 393224 | tf_op jit(solution)/shard_map/ppermute | solution.py:154
  12.8 6.2 %collective-permute-start.4 = (bf16[256,256]{1,0:T(8,128)(2,1)S(1)}, bf16[256,256]{1,0:T(8,128)(2,1)S(1)}, u32[]{:S(2)}, u32[]{:S(2)}) collective-permute-start(bf16[256,256]{1,0:T(8,128)(2,1)S(1)} %collective-permute-done.2.rest_1_), channel_id=1, source_target_pairs={{0,4},{1,5},{4,8},{5,9},{8,12},{9,13},{12,14},{13,15},{14,10},{15,... | collective-permute-start | bytes 393224 | tf_op jit(solution)/shard_map/ppermute | solution.py:154
  14.6 0.7 copy-start.17
  15.2 6.3 %collective-permute-start.11 = (bf16[256,256]{1,0:T(8,128)(2,1)S(1)}, bf16[256,256]{1,0:T(8,128)(2,1)S(1)}, u32[]{:S(2)}, u32[]{:S(2)}) collective-permute-start(bf16[256,256]{1,0:T(8,128)(2,1)S(1)} %get-tuple-element.28.m_two.mine.rest_0_), channel_id=1, source_target_pairs={{0,4},{1,5},{4,8},{5,9},{8,12},{9,13},{12,14},{13,15},{14,10},{15,... | collective-permute-start | bytes 393224 | tf_op jit(solution)/shard_map/ppermute | solution.py:154
  16.8 6.9 %collective-permute-start.5 = (bf16[256,256]{1,0:T(8,128)(2,1)S(1)}, bf16[256,256]{1,0:T(8,128)(2,1)S(1)}, u32[]{:S(2)}, u32[]{:S(2)}) collective-permute-start(bf16[256,256]{1,0:T(8,128)(2,1)S(1)} %collective-permute-done.3.rest_2_), channel_id=1, source_target_pairs={{4,0},{5,1},{8,4},{9,5},{12,8},{13,9},{14,12},{15,13},{10,14},{11,... | collective-permute-start | bytes 393224 | tf_op jit(solution)/shard_map/ppermute | solution.py:154
  17.3 0.7 copy-start.19
  17.9 7.0 %collective-permute-start.14 = (bf16[256,256]{1,0:T(8,128)(2,1)S(1)}, bf16[256,256]{1,0:T(8,128)(2,1)S(1)}, u32[]{:S(2)}, u32[]{:S(2)}) collective-permute-start(bf16[256,256]{1,0:T(8,128)(2,1)S(1)} %collective-permute-done.12.rest_2_), channel_id=1, source_target_pairs={{4,0},{5,1},{8,4},{9,5},{12,8},{13,9},{14,12},{15,13},{10,14},{11,... | collective-permute-start | bytes 393224 | tf_op jit(solution)/shard_map/ppermute | solution.py:154
  18.2 0.6 copy-start.11
  18.9 8.1 %collective-permute-start.6 = (bf16[256,256]{1,0:T(8,128)(2,1)S(1)}, bf16[256,256]{1,0:T(8,128)(2,1)}, u32[]{:S(2)}, u32[]{:S(2)}) collective-permute-start(bf16[256,256]{1,0:T(8,128)(2,1)S(1)} %collective-permute-done.4.rest_3_), channel_id=1, source_target_pairs={{0,4},{1,5},{4,8},{5,9},{8,12},{9,13},{12,14},{13,15},{14,10},{15,... | collective-permute-start | bytes 393224 | tf_op jit(solution)/shard_map/ppermute | solution.py:154
  20.6 0.7 copy-start.21
  21.5 6.0 %collective-permute-start.13 = (bf16[256,256]{1,0:T(8,128)(2,1)S(1)}, bf16[256,256]{1,0:T(8,128)(2,1)}, u32[]{:S(2)}, u32[]{:S(2)}) collective-permute-start(bf16[256,256]{1,0:T(8,128)(2,1)S(1)} %collective-permute-done.11.rest_1_), channel_id=1, source_target_pairs={{0,4},{1,5},{4,8},{5,9},{8,12},{9,13},{12,14},{13,15},{14,10},{15,... | collective-permute-start | bytes 393224 | tf_op jit(solution)/shard_map/ppermute | solution.py:154
  23.1 0.7 copy-start.13
  23.7 5.2 %collective-permute-start.7 = (bf16[256,256]{1,0:T(8,128)(2,1)S(1)}, bf16[256,256]{1,0:T(8,128)(2,1)S(1)}, u32[]{:S(2)}, u32[]{:S(2)}) collective-permute-start(bf16[256,256]{1,0:T(8,128)(2,1)S(1)} %collective-permute-done.5.rest_4_), channel_id=1, source_target_pairs={{4,0},{5,1},{8,4},{9,5},{12,8},{13,9},{14,12},{15,13},{10,14},{11,... | collective-permute-start | bytes 393224 | tf_op jit(solution)/shard_map/ppermute | solution.py:154
  24.2 0.7 copy-start.23
  24.9 6.2 %collective-permute-start.16 = (bf16[256,256]{1,0:T(8,128)(2,1)S(1)}, bf16[256,256]{1,0:T(8,128)(2,1)}, u32[]{:S(2)}, u32[]{:S(2)}) collective-permute-start(bf16[256,256]{1,0:T(8,128)(2,1)S(1)} %collective-permute-done.14.rest_4_), channel_id=1, source_target_pairs={{4,0},{5,1},{8,4},{9,5},{12,8},{13,9},{14,12},{15,13},{10,14},{11,... | collective-permute-start | bytes 393224 | tf_op jit(solution)/shard_map/ppermute | solution.py:154
  26.3 0.7 copy-start.15
  27.0 16.7 %collective-permute-start.8 = (bf16[256,256]{1,0:T(8,128)(2,1)}, bf16[256,256]{1,0:T(8,128)(2,1)}, u32[]{:S(2)}, u32[]{:S(2)}) collective-permute-start(bf16[256,256]{1,0:T(8,128)(2,1)} %collective-permute-done.6.rest_5_), channel_id=1, source_target_pairs={{0,4},{1,5},{4,8},{5,9},{8,12},{9,13},{12,14},{13,15},{14,10},{15,... | collective-permute-start | bytes 393224 | tf_op jit(solution)/shard_map/ppermute | solution.py:154
  27.6 29.7 %collective-permute-start.10 = (bf16[256,256]{1,0:T(8,128)(2,1)S(1)}, bf16[256,256]{1,0:T(8,128)(2,1)}, u32[]{:S(2)}, u32[]{:S(2)}) collective-permute-start(bf16[256,256]{1,0:T(8,128)(2,1)S(1)} %get-tuple-element.28.m_two.mine.rest_0_), channel_id=1, source_target_pairs={{0,1},{1,0},{2,3},{3,2},{4,5},{5,4},{6,7},{7,6},{8,9},{9,8},{10,11... | collective-permute-start | bytes 393224 | tf_op jit(solution)/shard_map/ppermute | solution.py:154
  28.9 0.7 copy-start.25
  29.6 27.8 %collective-permute-start.15 = (bf16[256,256]{1,0:T(8,128)(2,1)}, bf16[256,256]{1,0:T(8,128)(2,1)}, u32[]{:S(2)}, u32[]{:S(2)}) collective-permute-start(bf16[256,256]{1,0:T(8,128)(2,1)} %collective-permute-done.13.rest_3_), channel_id=1, source_target_pairs={{0,4},{1,5},{4,8},{5,9},{8,12},{9,13},{12,14},{13,15},{14,10},{15,... | collective-permute-start | bytes 393224 | tf_op jit(solution)/shard_map/ppermute | solution.py:154
  31.1 26.2 %collective-permute-start.17 = (bf16[256,256]{1,0:T(8,128)(2,1)}, bf16[256,256]{1,0:T(8,128)(2,1)}, u32[]{:S(2)}, u32[]{:S(2)}) collective-permute-start(bf16[256,256]{1,0:T(8,128)(2,1)} %collective-permute-done.16.rest_6_), channel_id=1, source_target_pairs={{4,0},{5,1},{8,4},{9,5},{12,8},{13,9},{14,12},{15,13},{10,14},{11,... | collective-permute-start | bytes 393224 | tf_op jit(solution)/shard_map/ppermute | solution.py:154
  43.8 0.9 %copy-start.18 = (bf16[256,256]{1,0:T(8,128)(2,1)S(1)}, bf16[256,256]{1,0:T(8,128)(2,1)}, u32[]{:S(2)}) copy-start(bf16[256,256]{1,0:T(8,128)(2,1)} %copy-done.17) | copy-start | bytes 393220
  44.7 0.9 %copy-start.20 = (bf16[256,256]{1,0:T(8,128)(2,1)S(1)}, bf16[256,256]{1,0:T(8,128)(2,1)}, u32[]{:S(2)}) copy-start(bf16[256,256]{1,0:T(8,128)(2,1)} %copy-done.19) | copy-start | bytes 393220
  45.6 0.9 %copy-start.22 = (bf16[256,256]{1,0:T(8,128)(2,1)S(1)}, bf16[256,256]{1,0:T(8,128)(2,1)}, u32[]{:S(2)}) copy-start(bf16[256,256]{1,0:T(8,128)(2,1)} %copy-done.21) | copy-start | bytes 393220
  46.5 0.9 %copy-start.24 = (bf16[256,256]{1,0:T(8,128)(2,1)S(1)}, bf16[256,256]{1,0:T(8,128)(2,1)}, u32[]{:S(2)}) copy-start(bf16[256,256]{1,0:T(8,128)(2,1)} %copy-done.23) | copy-start | bytes 393220
  47.4 0.9 %copy-start.26 = (bf16[256,256]{1,0:T(8,128)(2,1)S(1)}, bf16[256,256]{1,0:T(8,128)(2,1)}, u32[]{:S(2)}) copy-start(bf16[256,256]{1,0:T(8,128)(2,1)} %copy-done.25) | copy-start | bytes 393220
  50.8 0.7 copy-start.3
  51.5 0.7 copy-start.5
  52.2 11.1 %collective-permute-start.9 = (f32[256,256]{1,0:T(8,128)}, f32[256,256]{1,0:T(8,128)S(1)}, u32[]{:S(2)}, u32[]{:S(2)}) collective-permute-start(f32[256,256]{1,0:T(8,128)} %get-tuple-element.26), channel_id=1, source_target_pairs={{0,1},{1,0},{2,3},{3,2},{4,5},{5,4},{6,7},{7,6},{8,9},{9,8},{10,11... | collective-permute-start | bytes 786440 | tf_op jit(solution)/shard_map/ppermute | solution.py:154
  57.3 5.3 %copy-start.6 = (f32[256,256]{1,0:T(8,128)S(1)}, f32[256,256]{1,0:T(8,128)}, u32[]{:S(2)}) copy-start(f32[256,256]{1,0:T(8,128)} %copy-done.5) | copy-start | bytes 786436
  57.3 6.0 %copy-start.2 = (bf16[256,256]{1,0:T(8,128)(2,1)S(1)}, bf16[256,256]{1,0:T(8,128)(2,1)}, u32[]{:S(2)}) copy-start(bf16[256,256]{1,0:T(8,128)(2,1)} %cross.3) | copy-start | bytes 393220
  57.3 6.0 %copy-start.4 = (f32[256,256]{1,0:T(8,128)S(1)}, f32[256,256]{1,0:T(8,128)}, u32[]{:S(2)}) copy-start(f32[256,256]{1,0:T(8,128)} %copy-done.3) | copy-start | bytes 786436
  57.3 6.0 %copy-start.10 = (bf16[256,256]{1,0:T(8,128)(2,1)S(1)}, bf16[256,256]{1,0:T(8,128)(2,1)}, u32[]{:S(2)}) copy-start(bf16[256,256]{1,0:T(8,128)(2,1)} %copy-done.9) | copy-start | bytes 393220
  57.4 1.0 %copy-start.12 = (bf16[256,256]{1,0:T(8,128)(2,1)S(1)}, bf16[256,256]{1,0:T(8,128)(2,1)}, u32[]{:S(2)}) copy-start(bf16[256,256]{1,0:T(8,128)(2,1)} %copy-done.11) | copy-start | bytes 393220
  58.3 0.9 %copy-start.14 = (bf16[256,256]{1,0:T(8,128)(2,1)S(1)}, bf16[256,256]{1,0:T(8,128)(2,1)}, u32[]{:S(2)}) copy-start(bf16[256,256]{1,0:T(8,128)(2,1)} %copy-done.13) | copy-start | bytes 393220
  59.2 0.9 %copy-start.16 = (bf16[256,256]{1,0:T(8,128)(2,1)S(1)}, bf16[256,256]{1,0:T(8,128)(2,1)}, u32[]{:S(2)}) copy-start(bf16[256,256]{1,0:T(8,128)(2,1)} %copy-done.15) | copy-start | bytes 393220
  62.5 19.3 %copy-start.30 = (bf16[256,256]{1,0:T(8,128)(2,1)S(1)}, bf16[256,256]{1,0:T(8,128)(2,1)}, u32[]{:S(2)}) copy-start(bf16[256,256]{1,0:T(8,128)(2,1)} %copy-done.29) | copy-start | bytes 393220
  62.6 20.5 %copy-start.7 = (f32[256,256]{1,0:T(8,128)S(1)}, f32[256,256]{1,0:T(8,128)}, u32[]{:S(2)}) copy-start(f32[256,256]{1,0:T(8,128)} %diag_one.1) | copy-start | bytes 786436
  62.6 20.5 %copy-start.8 = (f32[256,256]{1,0:T(8,128)S(1)}, f32[256,256]{1,0:T(8,128)}, u32[]{:S(2)}) copy-start(f32[256,256]{1,0:T(8,128)} %diag_two.1) | copy-start | bytes 786436
  62.7 1.8 %collective-permute-start.18 = (f32[144,256]{1,0:T(8,128)S(1)}, f32[144,256]{1,0:T(8,128)S(1)}, u32[]{:S(2)}, u32[]{:S(2)}) collective-permute-start(f32[144,256]{1,0:T(8,128)S(1)} %get-tuple-element.33), channel_id=1, source_target_pairs={{0,1},{1,0},{2,3},{3,2},{4,5},{5,4},{6,7},{7,6},{8,9},{9,8},{10,11... | collective-permute-start | bytes 442376 | tf_op jit(solution)/shard_map/ppermute | solution.py:154
  63.2 18.6 %collective-permute-start.28 = (f32[256,256]{1,0:T(8,128)S(1)}, f32[256,256]{1,0:T(8,128)S(1)}, u32[]{:S(2)}, u32[]{:S(2)}) collective-permute-start(f32[256,256]{1,0:T(8,128)S(1)} %get-tuple-element.38), channel_id=1, source_target_pairs={{0,1},{1,0},{2,3},{3,2},{4,5},{5,4},{6,7},{7,6},{8,9},{9,8},{10,11... | collective-permute-start | bytes 786440 | tf_op jit(solution)/shard_map/ppermute | solution.py:154
  64.1 1.9 %collective-permute-start.23 = (f32[128,256]{1,0:T(8,128)S(1)}, f32[128,256]{1,0:T(8,128)S(1)}, u32[]{:S(2)}, u32[]{:S(2)}) collective-permute-start(f32[128,256]{1,0:T(8,128)S(1)} %get-tuple-element.35), channel_id=1, source_target_pairs={{0,1},{1,0},{2,3},{3,2},{4,5},{5,4},{6,7},{7,6},{8,9},{9,8},{10,11... | collective-permute-start | bytes 393224 | tf_op jit(solution)/shard_map/ppermute | solution.py:154
  64.5 4.9 %collective-permute-start.19 = (bf16[144,256]{1,0:T(8,128)(2,1)S(1)}, bf16[144,256]{1,0:T(8,128)(2,1)S(1)}, u32[]{:S(2)}, u32[]{:S(2)}) collective-permute-start(bf16[144,256]{1,0:T(8,128)(2,1)S(1)} %add_convert_fusion.2), channel_id=1, source_target_pairs={{0,2},{1,3},{2,0},{3,1},{4,6},{5,7},{6,4},{7,5},{8,10},{9,11},{10,... | collective-permute-start | bytes 221192 | tf_op jit(solution)/shard_map/ppermute | solution.py:154
  66.0 5.1 %collective-permute-start.24 = (bf16[128,256]{1,0:T(8,128)(2,1)S(1)}, bf16[128,256]{1,0:T(8,128)(2,1)S(1)}, u32[]{:S(2)}, u32[]{:S(2)}) collective-permute-start(bf16[128,256]{1,0:T(8,128)(2,1)S(1)} %add_convert_fusion.5), channel_id=1, source_target_pairs={{0,2},{1,3},{2,0},{3,1},{4,6},{5,7},{6,4},{7,5},{8,10},{9,11},{10,... | collective-permute-start | bytes 196616 | tf_op jit(solution)/shard_map/ppermute | solution.py:154
  69.5 4.4 %collective-permute-start.20 = (bf16[144,256]{1,0:T(8,128)(2,1)S(1)}, bf16[144,256]{1,0:T(8,128)(2,1)S(1)}, u32[]{:S(2)}, u32[]{:S(2)}) collective-permute-start(bf16[144,256]{1,0:T(8,128)(2,1)S(1)} %add_convert_fusion.1), channel_id=1, source_target_pairs={{0,4},{1,5},{2,6},{3,7},{4,0},{5,1},{6,2},{7,3},{8,12},{9,13},{10,... | collective-permute-start | bytes 221192 | tf_op jit(solution)/shard_map/ppermute | solution.py:154
  71.1 5.4 %collective-permute-start.25 = (bf16[128,256]{1,0:T(8,128)(2,1)S(1)}, bf16[128,256]{1,0:T(8,128)(2,1)S(1)}, u32[]{:S(2)}, u32[]{:S(2)}) collective-permute-start(bf16[128,256]{1,0:T(8,128)(2,1)S(1)} %add_convert_fusion.4), channel_id=1, source_target_pairs={{0,4},{1,5},{2,6},{3,7},{4,0},{5,1},{6,2},{7,3},{8,12},{9,13},{10,... | collective-permute-start | bytes 196616 | tf_op jit(solution)/shard_map/ppermute | solution.py:154
  73.9 5.6 %collective-permute-start.21 = (bf16[144,256]{1,0:T(8,128)(2,1)S(1)}, bf16[144,256]{1,0:T(8,128)(2,1)S(1)}, u32[]{:S(2)}, u32[]{:S(2)}) collective-permute-start(bf16[144,256]{1,0:T(8,128)(2,1)S(1)} %add_convert_fusion), channel_id=1, source_target_pairs={{0,8},{1,9},{2,10},{3,11},{4,12},{5,13},{6,14},{7,15},{8,0},{9,1},... | collective-permute-start | bytes 221192 | tf_op jit(solution)/shard_map/ppermute | solution.py:154
  76.5 5.2 %collective-permute-start.26 = (bf16[128,256]{1,0:T(8,128)(2,1)S(1)}, bf16[128,256]{1,0:T(8,128)(2,1)S(1)}, u32[]{:S(2)}, u32[]{:S(2)}) collective-permute-start(bf16[128,256]{1,0:T(8,128)(2,1)S(1)} %add_convert_fusion.3), channel_id=1, source_target_pairs={{0,8},{1,9},{2,10},{3,11},{4,12},{5,13},{6,14},{7,15},{8,0},{9,1},... | collective-permute-start | bytes 196616 | tf_op jit(solution)/shard_map/ppermute | solution.py:154
  79.6 3.0 %collective-permute-start.22 = (f32[144,256]{1,0:T(8,128)S(1)}, f32[144,256]{1,0:T(8,128)S(1)}, u32[]{:S(2)}, u32[]{:S(2)}) collective-permute-start(f32[144,256]{1,0:T(8,128)S(1)} %convert_add_fusion.pack_a), channel_id=1, source_target_pairs={{0,1},{1,0},{2,3},{3,2},{4,5},{5,4},{6,7},{7,6},{8,9},{9,8},{10,11... | collective-permute-start | bytes 442376 | tf_op jit(solution)/shard_map/ppermute | solution.py:154
  81.8 1.4 %collective-permute-start.27 = (f32[128,256]{1,0:T(8,128)S(1)}, f32[128,256]{1,0:T(8,128)S(1)}, u32[]{:S(2)}, u32[]{:S(2)}) collective-permute-start(f32[128,256]{1,0:T(8,128)S(1)} %convert_add_fusion.1.cross_a), channel_id=1, source_target_pairs={{0,1},{1,0},{2,3},{3,2},{4,5},{5,4},{6,7},{7,6},{8,9},{9,8},{10,11... | collective-permute-start | bytes 393224 | tf_op jit(solution)/shard_map/ppermute | solution.py:154

commit v2 on v1

--- a/solution.py
+++ b/solution.py
@@ -26,7 +26,7 @@
     return high, (x - high.astype(F32)).astype(BF16)
 
 
-def call(body, name, outs, args, n_smem=0, flops=0):
+def call(body, name, outs, args, n_smem=0, flops=0, aliases=None):
     size = sum(a.size * a.dtype.itemsize for a in args)
     return pl.pallas_call(
         body,
@@ -34,9 +34,19 @@
         out_shape=tuple(jax.ShapeDtypeStruct(s, d) for s, d in outs),
         in_specs=[SMEM] * n_smem + [VMEM] * (len(args) - n_smem),
         out_specs=tuple(VMEM for _ in outs),
-        compiler_params=pltpu.CompilerParams(vmem_limit_bytes=32 << 20),
+        input_output_aliases=aliases or {},
+        compiler_params=pltpu.CompilerParams(vmem_limit_bytes=16 << 20),
         cost_estimate=pl.CostEstimate(flops=flops, bytes_accessed=size, transcendentals=0),
     )(*args)
+
+
+def chip_of(position, chips):
+    return jnp.where(position < chips // 2, 2 * position, 2 * (chips - 1 - position) + 1)
+
+
+def chip_at(chip, offset, chips):
+    position = jnp.where(chip % 2 == 0, chip // 2, chips - 1 - chip // 2)
+    return chip_of((position + offset + chips) % chips, chips)
 
 
 def mask_body(table, rows, one, two, m_one, m_two, w_one, w_two):
@@ -53,38 +63,53 @@
         weights[...] = dot(chosen, ones).astype(BF16)
 
 
-def swap_body(place, window, out):
+def swap_body(window, out):
     width = out.shape[0]
-    other = 1 - place[0]
+    other = 1 - lax.axis_index(AXIS) % 2
     for t in range(out.shape[1] // width):
-        out[:, t * width : (t + 1) * width] = window[:, pl.ds((2 * t + other) * width, width)]
-
-
-def image_body(place, window, swapped, mine, sibling, *rest):
+        out[:, t * width : (t + 1) * width] = window[:, pl.ds(pl.multiple_of((2 * t + other) * width, width), width)]
+
+
+def add_products(offsets, window, swapped, pieces, x_own, x_other):
+    n = window.shape[0]
+    me = lax.axis_index(AXIS)
+    chip, core = me // 2, me % 2
+    for offset, piece in zip(offsets, pieces, strict=True):
+        t = chip_at(chip, offset, window.shape[1] // (2 * n))
+        value = piece[...]
+        x_own += dot(window[:, pl.ds(pl.multiple_of((2 * t + core) * n, n), n)], value)
+        x_other += dot(swapped[:, pl.ds(pl.multiple_of(t * n, n), n)], value)
+    return x_own, x_other
+
+
+def image_first_body(offsets, window, swapped, *rest):
+    pieces, (own, other) = rest[:-2], rest[-2:]
+    zero = jnp.zeros(own.shape, F32)
+    own[...], other[...] = add_products(offsets, window, swapped, pieces, zero, zero)
+
+
+def image_more_body(offsets, window, swapped, own_in, other_in, *rest):
+    pieces, (own, other) = rest[:-2], rest[-2:]
+    own[...], other[...] = add_products(offsets, window, swapped, pieces, own_in[...], other_in[...])
+
+
+def image_last_body(offsets, window, swapped, own_in, other_in, mine, sibling, *rest):
     pieces, (own, other, total) = rest[:-3], rest[-3:]
-    n = mine.shape[0]
-    core = place[0]
-    x_own = jnp.zeros(own.shape, F32)
-    x_other = jnp.zeros(own.shape, F32)
-    for k, piece in enumerate(pieces):
-        chip = place[1 + k]
-        value = piece[...]
-        x_own += dot(window[:, pl.ds(pl.multiple_of((2 * chip + core) * n, n), n)], value)
-        x_other += dot(swapped[:, pl.ds(pl.multiple_of(chip * n, n), n)], value)
+    x_own, x_other = add_products(offsets, window, swapped, pieces, own_in[...], other_in[...])
     own[...] = x_own
     other[...] = x_other
     (a, b), (c, d) = halves(x_own), halves(x_other)
     total[...] = (dot_t(mine[...], a) + dot_t(sibling[...], c)) + (dot_t(mine[...], b) + dot_t(sibling[...], d))
 
 
-def column_one_body(place, own, received, w_one, m_two, cross, column, carried, keep, send):
+def column_one_body(own, received, w_one, m_two, cross, column, carried, keep, send):
     exact = -(w_one[...].astype(F32) * (own[...] + received[...]))
     rounded = exact.astype(BF16)
     column[...] = rounded
     carried[...] = dot(rounded, cross[...])
     both = dot_t(m_two[...], rounded)
     half = both.shape[0] // 2
-    first = place[0] == 0
+    first = lax.axis_index(AXIS) % 2 == 0
     keep[...] = jnp.where(first, both[:half], both[half:])
     send[...] = jnp.where(first, both[half:], both[:half])
 
@@ -94,7 +119,7 @@
     column[...] = (-(w_two[...].astype(F32) * (image + carried[...]))).astype(BF16)
 
 
-def pack_body(place, one, two, keep, send):
+def pack_body(one, two, keep, send):
     n = one.shape[0]
     half = n // 2
     row = lax.broadcasted_iota(jnp.int32, (n, n), 0)
@@ -103,17 +128,17 @@
     both = jnp.where(row <= col, one[...], second)
     diagonal = jnp.sum(jnp.where(row == col, second, 0.0), axis=0, keepdims=True)
     diagonal = jnp.broadcast_to(diagonal, (keep.shape[0] - half, n))
-    first = place[0] == 0
+    first = lax.axis_index(AXIS) % 2 == 0
     keep[:half] = jnp.where(first, both[:half], both[half:])
     send[:half] = jnp.where(first, both[half:], both[:half])
     keep[half:] = diagonal
     send[half:] = diagonal
 
 
-def last_body(place, pack_a, pack_b, cross_a, cross_b, cross, diag_one, diag_two, block_one, edge, block_two):
+def last_body(pack_a, pack_b, cross_a, cross_b, cross, diag_one, diag_two, block_one, edge, block_two):
     n = cross.shape[0]
     half = n // 2
-    first = place[0] == 0
+    first = lax.axis_index(AXIS) % 2 == 0
 
     def whole(a, b):
         return jnp.concatenate([jnp.where(first, a, b), jnp.where(first, b, a)], axis=0)
@@ -153,15 +178,6 @@
     def send(x, perm):
         return lax.ppermute(x, AXIS, perm)
 
-    me = lax.axis_index(AXIS)
-    core = me % 2
-    spot = jnp.array(position, jnp.int32)[me // 2]
-
-    def chip_at(offset):
-        return jnp.array(ring, jnp.int32)[(spot + offset + chips) % chips]
-
-    where = core.reshape(1).astype(jnp.int32)
-
     square = ((rows, width), F32)
     tile = ((rows, width), BF16)
     m_one, m_two, w_one, w_two = call(
@@ -171,58 +187,59 @@
         (struct_mask, row_super.reshape(1, -1), panel_one, panel_two),
         n_smem=1,
     )
-    (window_part,) = call(
-        swap_body, "swap", (((rows, inverse_window.shape[1] // 2), BF16),), (where, inverse_window), n_smem=1
-    )
-
     steps = chips // 2
-    one, two, order_one, order_two = [m_one], [m_two], [0], [0]
+    one, two = [(0, m_one)], [(0, m_two)]
     one_up = one_down = m_one
     two_up = two_down = m_two
     for k in range(1, steps):
         one_up, one_down = send(one_up, ahead), send(one_down, back)
         two_up, two_down = send(two_up, ahead), send(two_down, back)
-        one += [one_up, one_down]
-        two += [two_up, two_down]
-        order_one += [-k, k]
-        order_two += [-k, k]
-    one.append(send(one_up, ahead))
-    two.append(send(two_down, back))
-    order_one.append(-steps)
-    order_two.append(steps)
-
+        one += [(-k, one_up), (k, one_down)]
+        two += [(-k, two_up), (k, two_down)]
+    one.append((-steps, send(one_up, ahead)))
+    two.append((steps, send(two_down, back)))
+
+    window, _ = lax.optimization_barrier((inverse_window, one[1][1]))
+    (window_part,) = call(swap_body, "swap", (((rows, inverse_window.shape[1] // 2), BF16),), (window,))
     swapped = send(window_part, flip[0])
     sibling_one = send(m_one, flip[0])
     sibling_two = send(m_two, flip[0])
-    flops = 2 * 2 * rows * width * (width + inverse_window.shape[1] // 2)
-
-    def image(name, order, pieces, mine, sibling):
-        place = jnp.stack([core] + [chip_at(d) for d in order]).astype(jnp.int32)
-        return call(
-            image_body,
-            name,
-            (square, square, ((width, width), F32)),
-            (place, inverse_window, swapped, mine, sibling, *pieces),
-            n_smem=1,
-            flops=flops,
+
+    def image(name, pieces, mine, sibling):
+        def stage(body, label, chosen, outs, *more, aliases=None):
+            offsets, values = zip(*chosen, strict=True)
+            return call(
+                functools.partial(body, offsets),
+                name + label,
+                outs,
+                (inverse_window, swapped, *more, *values),
+                flops=2 * 2 * rows * width * width * len(chosen),
+                aliases=aliases,
+            )
+
+        kept = {2: 0, 3: 1}
+        own, other = stage(image_first_body, "_first", pieces[:3], (square, square))
+        middle = pieces[3:-1]
+        for i in range(0, len(middle), 4):
+            own, other = stage(image_more_body, "_more", middle[i : i + 4], (square, square), own, other, aliases=kept)
+        return stage(
+            image_last_body, "_last", pieces[-1:], (square, square, ((width, width), F32)), own, other, mine, sibling, aliases=kept
         )
 
-    own_one, other_one, total_one = image("image_one", order_one, one, m_one, sibling_one)
+    own_one, other_one, total_one = image("image_one", one, m_one, sibling_one)
     received_one = send(other_one, flip[0])
     column_one, carried, keep_x, send_x = call(
         column_one_body,
         "column_one",
         (tile, square, ((half, width), F32), ((half, width), F32)),
-        (where, own_one, received_one, w_one, m_two, cross_block),
-        n_smem=1,
-    )
-    own_two, other_two, total_two = image("image_two", order_two, two, m_two, sibling_two)
+        (own_one, received_one, w_one, m_two, cross_block),
+    )
+    own_two, other_two, total_two = image("image_two", two, m_two, sibling_two)
     keep_p, send_p = call(
         pack_body,
         "pack",
         (((half + 16, width), F32), ((half + 16, width), F32)),
-        (where, total_one, total_two),
-        n_smem=1,
+        (total_one, total_two),
     )
     received_two = send(other_two, flip[0])
     (column_two,) = call(column_two_body, "column_two", (tile,), (own_two, received_two, w_two, carried))
@@ -241,8 +258,7 @@
         last_body,
         "last",
         (full, full, full),
-        (where, pack_a, pack_b, cross_a, cross_b, cross_block, diag_one, diag_two),
-        n_smem=1,
+        (pack_a, pack_b, cross_a, cross_b, cross_block, diag_one, diag_two),
     )
     return column_one, block_one, column_two, edge_block, block_two
 

time: 85 us -> 62.1 us (0.73)
  local copies, waits for them, and re-layouts: 28.3 us -> 4.77 us
  waiting for transfers between devices: 12.3 us -> 19 us
  between operations: 6.7 us -> 0.88 us
  starting transfers between devices: 27.2 us -> 30.6 us
  Pallas kernels: 9.75 us -> 6.53 us
    unnamed x70 -> x16, local copies, waits for them, and re-layouts: 16.9 us -> 4.77 us
    another operation x2 -> x0, local copies, waits for them, and re-layouts: 10.1 us -> none  [image(): place = jnp.stack([core] + [chip_at(d) for d in order]).astype(jnp.int32)]
    ppermute x29, waiting for transfers between devices: 12.3 us -> 19 us  [send(): return lax.ppermute(x, AXIS, perm)]
    ppermute x29, starting transfers between devices: 27.2 us -> 30.6 us  [send(): return lax.ppermute(x, AXIS, perm)]
    pallas_call x8 -> x12, Pallas kernels: 9.75 us -> 6.53 us  [call(): pl.pallas_call(body, name=name, out_shape=tuple((jax.ShapeDtypeStruct(s,...]
    dynamic_slice x2 -> x0, local copies, waits for them, and re-layouts: 1.34 us -> none  [the longest x1 0.71 us: chip_at(): return jnp.array(ring, jnp.int32)[(spot + offset + chips) % chips]]
  transfers between devices with their start and end apart: 29 -> 29, of which waited for: 9 -> 14; matrix products, arithmetic and copies ran while one was open for 14% -> 0% of each run, Pallas kernels for 9% -> 7%
where the time goes in v2:
time: 62.1 us; the launch traced here: 61.9 us
  starting transfers between devices  30.6 us (49%)
  waiting for transfers between devices  19 us (31%)
  Pallas kernels  6.53 us (11%)
  local copies, waits for them, and re-layouts  4.77 us (8%)
  between operations  0.88 us (1%)
    ppermute x29, starting transfers between devices, send(): return lax.ppermute(x, AXIS, perm)  30.6 us
    ppermute x29, waiting for transfers between devices, send(): return lax.ppermute(x, AXIS, perm)  19 us
    pallas_call x12, Pallas kernels, call(): pl.pallas_call(body, name=name, out_shape=tuple((jax.ShapeDtypeStruct(s,...  6.53 us
    unnamed x16, local copies, waits for them, and re-layouts  4.77 us
  transfers between devices with their start and end apart: 29, of which 14 were waited for; matrix products, arithmetic and copies ran while one was open for 0% of the time, Pallas kernels for 7%

profile of v2, /device:TPU:0, one launch (start us, length us, event | category | flops | bytes accessed | tf_op | source)
XLA Modules:
  0.0 61.9 jit_solution(4706625780553230418)
XLA Ops:
  0.6 0.9 %copy-done.4 = bf16[256,256]{1,0:T(8,128)(2,1)S(1)} copy-done((bf16[256,256]{1,0:T(8,128)(2,1)S(1)}, bf16[256,256]{1,0:T(8,128)(2,1)}, u32[]{:S(2)}) %copy-start.4) | copy-done | bytes 131096
  1.5 0.9 %copy-done.5 = bf16[256,256]{1,0:T(8,128)(2,1)S(1)} copy-done((bf16[256,256]{1,0:T(8,128)(2,1)S(1)}, bf16[256,256]{1,0:T(8,128)(2,1)}, u32[]{:S(2)}) %copy-start.5) | copy-done | bytes 131096
  2.4 0.7 %copy-done.6 = s32[2,16]{1,0:T(2,128)S(1)} copy-done((s32[2,16]{1,0:T(2,128)S(1)}, s32[2,16]{1,0:T(2,128)}, u32[]{:S(2)}) %copy-start.6) | copy-done | bytes 152
  3.1 0.7 %copy-done.7 = s32[256]{0:T(256)S(1)} copy-done((s32[256]{0:T(256)S(1)}, s32[256]{0:T(256)}, u32[]{:S(2)}) %copy-start.7) | copy-done | bytes 1048
  3.8 0.8 %mask.1 = (bf16[256,256]{1,0:T(8,128)(2,1)S(1)}, bf16[256,256]{1,0:T(8,128)(2,1)S(1)}, bf16[256,256]{1,0:T(8,128)(2,1)S(1)}, bf16[256,256]{1,0:T(8,128)(2,1)S(1)}) custom-call(s32[2,16]{1,0:T(2,128)S(1)} %copy-done.6, s32[1,256]{1,0:T(1,128)S(1)} %bitcast.1, bf16[256,256]{1,0:T(8,128)(2,1)S(1)} %copy-done.4, bf16[256,256]{1,0:T(8,128)(2,1)S(1)} %copy-done.5), custom_call_target="tpu_custom_call" | custom-call | bytes 263296 | tf_op jit(solution)/shard_map/mask/pallas_call | solution.py:31
  4.7 3.1 %collective-permute-start = (bf16[256,256]{1,0:T(8,128)(2,1)S(1)}, bf16[256,256]{1,0:T(8,128)(2,1)S(1)}, u32[]{:S(2)}, u32[]{:S(2)}) collective-permute-start(bf16[256,256]{1,0:T(8,128)(2,1)S(1)} %get-tuple-element.33.rest_0_.mine), channel_id=1, source_target_pairs={{0,4},{1,5},{4,8},{5,9},{8,12},{9,13},{12,14},{13,15},{14,10},{15,... | collective-permute-start | bytes 393224 | tf_op jit(solution)/shard_map/ppermute | solution.py:179
  7.7 3.4 %collective-permute-done.rest_1_ = bf16[256,256]{1,0:T(8,128)(2,1)S(1)} collective-permute-done((bf16[256,256]{1,0:T(8,128)(2,1)S(1)}, bf16[256,256]{1,0:T(8,128)(2,1)S(1)}, u32[]{:S(2)}, u32[]{:S(2)}) %collective-permute-start) | collective-permute-done | bytes 131104 | tf_op jit(solution)/shard_map/ppermute | solution.py:179
  11.2 1.6 %copy-done = bf16[256,4096]{1,0:T(8,128)(2,1)S(1)} copy-done((bf16[256,4096]{1,0:T(8,128)(2,1)S(1)}, bf16[256,4096]{1,0:T(8,128)(2,1)}, u32[]{:S(2)}) %copy-start) | copy-done | bytes 2097176
  12.8 0.1 swap.1
  12.9 0.1 collective-permute-start.1
  13.0 1.8 %collective-permute-start.2 = (bf16[256,256]{1,0:T(8,128)(2,1)S(1)}, bf16[256,256]{1,0:T(8,128)(2,1)S(1)}, u32[]{:S(2)}, u32[]{:S(2)}) collective-permute-start(bf16[256,256]{1,0:T(8,128)(2,1)S(1)} %get-tuple-element.33.rest_0_.mine), channel_id=1, source_target_pairs={{4,0},{5,1},{8,4},{9,5},{12,8},{13,9},{14,12},{15,13},{10,14},{11,... | collective-permute-start | bytes 393224 | tf_op jit(solution)/shard_map/ppermute | solution.py:179
  14.8 1.6 %collective-permute-start.11 = (bf16[256,256]{1,0:T(8,128)(2,1)S(1)}, bf16[256,256]{1,0:T(8,128)(2,1)S(1)}, u32[]{:S(2)}, u32[]{:S(2)}) collective-permute-start(bf16[256,256]{1,0:T(8,128)(2,1)S(1)} %get-tuple-element.42.m_two.rest_0_.mine), channel_id=1, source_target_pairs={{4,0},{5,1},{8,4},{9,5},{12,8},{13,9},{14,12},{15,13},{10,14},{11,... | collective-permute-start | bytes 393224 | tf_op jit(solution)/shard_map/ppermute | solution.py:179
  16.4 0.4 collective-permute-start.10
  16.8 0.3 collective-permute-start.3
  17.1 2.2 %collective-permute-done.2.rest_2_ = bf16[256,256]{1,0:T(8,128)(2,1)S(1)} collective-permute-done((bf16[256,256]{1,0:T(8,128)(2,1)S(1)}, bf16[256,256]{1,0:T(8,128)(2,1)S(1)}, u32[]{:S(2)}, u32[]{:S(2)}) %collective-permute-start.2) | collective-permute-done | bytes 131104 | tf_op jit(solution)/shard_map/ppermute | solution.py:179
  19.3 1.7 %collective-permute-start.4 = (bf16[256,256]{1,0:T(8,128)(2,1)S(1)}, bf16[256,256]{1,0:T(8,128)(2,1)S(1)}, u32[]{:S(2)}, u32[]{:S(2)}) collective-permute-start(bf16[256,256]{1,0:T(8,128)(2,1)S(1)} %collective-permute-done.2.rest_2_), channel_id=1, source_target_pairs={{4,0},{5,1},{8,4},{9,5},{12,8},{13,9},{14,12},{15,13},{10,14},{11,... | collective-permute-start | bytes 393224 | tf_op jit(solution)/shard_map/ppermute | solution.py:179
  21.1 1.1 %collective-permute-done.11.rest_2_ = bf16[256,256]{1,0:T(8,128)(2,1)S(1)} collective-permute-done((bf16[256,256]{1,0:T(8,128)(2,1)S(1)}, bf16[256,256]{1,0:T(8,128)(2,1)S(1)}, u32[]{:S(2)}, u32[]{:S(2)}) %collective-permute-start.11) | collective-permute-done | bytes 131104 | tf_op jit(solution)/shard_map/ppermute | solution.py:179
  22.1 1.7 %collective-permute-start.13 = (bf16[256,256]{1,0:T(8,128)(2,1)S(1)}, bf16[256,256]{1,0:T(8,128)(2,1)S(1)}, u32[]{:S(2)}, u32[]{:S(2)}) collective-permute-start(bf16[256,256]{1,0:T(8,128)(2,1)S(1)} %collective-permute-done.11.rest_2_), channel_id=1, source_target_pairs={{4,0},{5,1},{8,4},{9,5},{12,8},{13,9},{14,12},{15,13},{10,14},{11,... | collective-permute-start | bytes 393224 | tf_op jit(solution)/shard_map/ppermute | solution.py:179
  23.9 0.3 collective-permute-start.12
  24.2 0.3 collective-permute-done.3.rest_0_
  24.4 1.5 %collective-permute-start.5 = (bf16[256,256]{1,0:T(8,128)(2,1)S(1)}, bf16[256,256]{1,0:T(8,128)(2,1)S(1)}, u32[]{:S(2)}, u32[]{:S(2)}) collective-permute-start(bf16[256,256]{1,0:T(8,128)(2,1)S(1)} %collective-permute-done.3.rest_0_), channel_id=1, source_target_pairs={{0,4},{1,5},{4,8},{5,9},{8,12},{9,13},{12,14},{13,15},{14,10},{15,... | collective-permute-start | bytes 393224 | tf_op jit(solution)/shard_map/ppermute | solution.py:179
  26.0 0.0 collective-permute-done.4.rest_1_
  26.0 0.8 %collective-permute-start.6 = (bf16[256,256]{1,0:T(8,128)(2,1)S(1)}, bf16[256,256]{1,0:T(8,128)(2,1)S(1)}, u32[]{:S(2)}, u32[]{:S(2)}) collective-permute-start(bf16[256,256]{1,0:T(8,128)(2,1)S(1)} %collective-permute-done.4.rest_1_), channel_id=1, source_target_pairs={{4,0},{5,1},{8,4},{9,5},{12,8},{13,9},{14,12},{15,13},{10,14},{11,... | collective-permute-start | bytes 393224 | tf_op jit(solution)/shard_map/ppermute | solution.py:179
  26.8 1.0 %collective-permute-done.13.rest_1_ = bf16[256,256]{1,0:T(8,128)(2,1)S(1)} collective-permute-done((bf16[256,256]{1,0:T(8,128)(2,1)S(1)}, bf16[256,256]{1,0:T(8,128)(2,1)S(1)}, u32[]{:S(2)}, u32[]{:S(2)}) %collective-permute-start.13) | collective-permute-done | bytes 131104 | tf_op jit(solution)/shard_map/ppermute | solution.py:179
  27.8 2.5 %collective-permute-start.15 = (bf16[256,256]{1,0:T(8,128)(2,1)S(1)}, bf16[256,256]{1,0:T(8,128)(2,1)S(1)}, u32[]{:S(2)}, u32[]{:S(2)}) collective-permute-start(bf16[256,256]{1,0:T(8,128)(2,1)S(1)} %collective-permute-done.13.rest_1_), channel_id=1, source_target_pairs={{4,0},{5,1},{8,4},{9,5},{12,8},{13,9},{14,12},{15,13},{10,14},{11,... | collective-permute-start | bytes 393224 | tf_op jit(solution)/shard_map/ppermute | solution.py:179
  30.3 0.7 %collective-permute-done.5.rest_2_ = bf16[256,256]{1,0:T(8,128)(2,1)S(1)} collective-permute-done((bf16[256,256]{1,0:T(8,128)(2,1)S(1)}, bf16[256,256]{1,0:T(8,128)(2,1)S(1)}, u32[]{:S(2)}, u32[]{:S(2)}) %collective-permute-start.5) | collective-permute-done | bytes 131104 | tf_op jit(solution)/shard_map/ppermute | solution.py:179
  31.0 0.4 collective-permute-start.8
  31.4 1.7 %collective-permute-start.14 = (bf16[256,256]{1,0:T(8,128)(2,1)S(1)}, bf16[256,256]{1,0:T(8,128)(2,1)S(1)}, u32[]{:S(2)}, u32[]{:S(2)}) collective-permute-start(bf16[256,256]{1,0:T(8,128)(2,1)S(1)} %collective-permute-done.12.rest_0_), channel_id=1, source_target_pairs={{0,4},{1,5},{4,8},{5,9},{8,12},{9,13},{12,14},{13,15},{14,10},{15,... | collective-permute-start | bytes 393224 | tf_op jit(solution)/shard_map/ppermute | solution.py:179
  33.1 0.4 image_one_first.1
  33.5 0.1 collective-permute-start.16
  33.6 1.7 %collective-permute-start.17 = (bf16[256,256]{1,0:T(8,128)(2,1)S(1)}, bf16[256,256]{1,0:T(8,128)(2,1)S(1)}, u32[]{:S(2)}, u32[]{:S(2)}) collective-permute-start(bf16[256,256]{1,0:T(8,128)(2,1)S(1)} %collective-permute-done.15.rest_3_), channel_id=1, source_target_pairs={{4,0},{5,1},{8,4},{9,5},{12,8},{13,9},{14,12},{15,13},{10,14},{11,... | collective-permute-start | bytes 393224 | tf_op jit(solution)/shard_map/ppermute | solution.py:179
  35.3 0.4 image_one_more.1
  35.7 1.7 %collective-permute-done.8.rest_0_ = bf16[256,256]{1,0:T(8,128)(2,1)S(1)} collective-permute-done((bf16[256,256]{1,0:T(8,128)(2,1)S(1)}, bf16[256,256]{1,0:T(8,128)(2,1)S(1)}, u32[]{:S(2)}, u32[]{:S(2)}) %collective-permute-start.8) | collective-permute-done | bytes 131104 | tf_op jit(solution)/shard_map/ppermute | solution.py:179
  37.4 0.6 image_one_last.1
  38.0 0.1 collective-permute-start.9
  38.1 0.4 image_two_first.1
  38.5 0.5 collective-permute-done.14.rest_2_
  39.0 0.4 image_two_more.1
  39.5 0.0 collective-permute-done.17.rest_0_
  39.5 0.0 copy-start.1
  39.5 0.6 image_two_last.1
  40.1 0.1 pack.1
  40.2 0.0 copy-start.2
  40.2 0.0 copy-start.3
  40.2 0.1 collective-permute-start.18
  40.3 0.5 collective-permute-start.28
  40.8 0.7 %column_one.1 = (bf16[256,256]{1,0:T(8,128)(2,1)}, f32[256,256]{1,0:T(8,128)S(1)}, f32[128,256]{1,0:T(8,128)S(1)}, f32[128,256]{1,0:T(8,128)S(1)}) custom-call(f32[256,256]{1,0:T(8,128)S(1)} %get-tuple-element.39.own, f32[256,256]{1,0:T(8,128)S(1)} %collective-permute-done.9.received, bf16[256,256]{1,0:T(8,128)(2,1)S(1)} %get-tuple-element.41.w_one, ...), custom_call_target="tpu_custom_call" | custom-call | bytes 917504 | tf_op jit(solution)/shard_map/column_one/pallas_call | solution.py:31
  41.5 0.1 collective-permute-start.23
  41.6 0.1 collective-permute-done.18
  41.6 1.7 %collective-permute-start.19 = (bf16[144,256]{1,0:T(8,128)(2,1)S(1)}, bf16[144,256]{1,0:T(8,128)(2,1)S(1)}, u32[]{:S(2)}, u32[]{:S(2)}) collective-permute-start(bf16[144,256]{1,0:T(8,128)(2,1)S(1)} %add_convert_fusion.2), channel_id=1, source_target_pairs={{0,2},{1,3},{2,0},{3,1},{4,6},{5,7},{6,4},{7,5},{8,10},{9,11},{10,... | collective-permute-start | bytes 221192 | tf_op jit(solution)/shard_map/ppermute | solution.py:179
  43.3 1.2 %collective-permute-start.24 = (bf16[128,256]{1,0:T(8,128)(2,1)S(1)}, bf16[128,256]{1,0:T(8,128)(2,1)S(1)}, u32[]{:S(2)}, u32[]{:S(2)}) collective-permute-start(bf16[128,256]{1,0:T(8,128)(2,1)S(1)} %add_convert_fusion.5), channel_id=1, source_target_pairs={{0,2},{1,3},{2,0},{3,1},{4,6},{5,7},{6,4},{7,5},{8,10},{9,11},{10,... | collective-permute-start | bytes 196616 | tf_op jit(solution)/shard_map/ppermute | solution.py:179
  44.5 2.0 %collective-permute-done.19 = bf16[144,256]{1,0:T(8,128)(2,1)S(1)} collective-permute-done((bf16[144,256]{1,0:T(8,128)(2,1)S(1)}, bf16[144,256]{1,0:T(8,128)(2,1)S(1)}, u32[]{:S(2)}, u32[]{:S(2)}) %collective-permute-start.19) | collective-permute-done | bytes 73760 | tf_op jit(solution)/shard_map/ppermute | solution.py:179
  46.5 1.6 %collective-permute-start.20 = (bf16[144,256]{1,0:T(8,128)(2,1)S(1)}, bf16[144,256]{1,0:T(8,128)(2,1)S(1)}, u32[]{:S(2)}, u32[]{:S(2)}) collective-permute-start(bf16[144,256]{1,0:T(8,128)(2,1)S(1)} %add_convert_fusion.1), channel_id=1, source_target_pairs={{0,4},{1,5},{2,6},{3,7},{4,0},{5,1},{6,2},{7,3},{8,12},{9,13},{10,... | collective-permute-start | bytes 221192 | tf_op jit(solution)/shard_map/ppermute | solution.py:179
  48.1 1.2 %collective-permute-start.25 = (bf16[128,256]{1,0:T(8,128)(2,1)S(1)}, bf16[128,256]{1,0:T(8,128)(2,1)S(1)}, u32[]{:S(2)}, u32[]{:S(2)}) collective-permute-start(bf16[128,256]{1,0:T(8,128)(2,1)S(1)} %add_convert_fusion.4), channel_id=1, source_target_pairs={{0,4},{1,5},{2,6},{3,7},{4,0},{5,1},{6,2},{7,3},{8,12},{9,13},{10,... | collective-permute-start | bytes 196616 | tf_op jit(solution)/shard_map/ppermute | solution.py:179
  49.3 2.0 %collective-permute-done.20 = bf16[144,256]{1,0:T(8,128)(2,1)S(1)} collective-permute-done((bf16[144,256]{1,0:T(8,128)(2,1)S(1)}, bf16[144,256]{1,0:T(8,128)(2,1)S(1)}, u32[]{:S(2)}, u32[]{:S(2)}) %collective-permute-start.20) | collective-permute-done | bytes 73760 | tf_op jit(solution)/shard_map/ppermute | solution.py:179
  51.4 2.6 %collective-permute-start.21 = (bf16[144,256]{1,0:T(8,128)(2,1)S(1)}, bf16[144,256]{1,0:T(8,128)(2,1)S(1)}, u32[]{:S(2)}, u32[]{:S(2)}) collective-permute-start(bf16[144,256]{1,0:T(8,128)(2,1)S(1)} %add_convert_fusion), channel_id=1, source_target_pairs={{0,8},{1,9},{2,10},{3,11},{4,12},{5,13},{6,14},{7,15},{8,0},{9,1},... | collective-permute-start | bytes 221192 | tf_op jit(solution)/shard_map/ppermute | solution.py:179
  54.0 1.8 %collective-permute-start.26 = (bf16[128,256]{1,0:T(8,128)(2,1)S(1)}, bf16[128,256]{1,0:T(8,128)(2,1)S(1)}, u32[]{:S(2)}, u32[]{:S(2)}) collective-permute-start(bf16[128,256]{1,0:T(8,128)(2,1)S(1)} %add_convert_fusion.3), channel_id=1, source_target_pairs={{0,8},{1,9},{2,10},{3,11},{4,12},{5,13},{6,14},{7,15},{8,0},{9,1},... | collective-permute-start | bytes 196616 | tf_op jit(solution)/shard_map/ppermute | solution.py:179
  55.8 2.4 %collective-permute-done.21 = bf16[144,256]{1,0:T(8,128)(2,1)S(1)} collective-permute-done((bf16[144,256]{1,0:T(8,128)(2,1)S(1)}, bf16[144,256]{1,0:T(8,128)(2,1)S(1)}, u32[]{:S(2)}, u32[]{:S(2)}) %collective-permute-start.21) | collective-permute-done | bytes 73760 | tf_op jit(solution)/shard_map/ppermute | solution.py:179
  58.2 0.1 collective-permute-start.22
  58.3 0.9 %collective-permute-done.26 = bf16[128,256]{1,0:T(8,128)(2,1)S(1)} collective-permute-done((bf16[128,256]{1,0:T(8,128)(2,1)S(1)}, bf16[128,256]{1,0:T(8,128)(2,1)S(1)}, u32[]{:S(2)}, u32[]{:S(2)}) %collective-permute-start.26) | collective-permute-done | bytes 65568 | tf_op jit(solution)/shard_map/ppermute | solution.py:179
  59.2 0.1 collective-permute-start.27
  59.3 0.7 %column_two.1 = bf16[256,256]{1,0:T(8,128)(2,1)} custom-call(f32[256,256]{1,0:T(8,128)S(1)} %get-tuple-element.55.own, f32[256,256]{1,0:T(8,128)S(1)} %collective-permute-done.28.received, bf16[256,256]{1,0:T(8,128)(2,1)S(1)} %get-tuple-element.57.w_two, f32[256,256]{1,0:T(8,128)S(1)} %get-tuple-element.58.carried), custom_call_target="tpu_custom_call" | custom-call | bytes 917504 | tf_op jit(solution)/shard_map/column_two/pallas_call | solution.py:31
  60.0 0.6 collective-permute-done.27.cross_b
  60.7 1.3 %last.1 = (f32[256,256]{1,0:T(8,128)}, f32[256,256]{1,0:T(8,128)}, f32[256,256]{1,0:T(8,128)}) custom-call(f32[144,256]{1,0:T(8,128)S(1)} %convert_add_fusion.pack_a, f32[144,256]{1,0:T(8,128)S(1)} %collective-permute-done.22.pack_b, f32[128,256]{1,0:T(8,128)S(1)} %convert_add_fusion.1.cross_a, f32[128,256]{1,0:T(8,128)S(1)} %collective-permute-done.27.cross_b, ...), custom_call_target="tpu_custom_call" | custom-call | bytes 1212416 | tf_op jit(solution)/shard_map/last/pallas_call | solution.py:31
  (30 shorter events, 0.2 us)
Async XLA Ops:
  0.6 0.9 %copy-start.4 = (bf16[256,256]{1,0:T(8,128)(2,1)S(1)}, bf16[256,256]{1,0:T(8,128)(2,1)}, u32[]{:S(2)}) copy-start(bf16[256,256]{1,0:T(8,128)(2,1)} %one.1) | copy-start | bytes 393220
  1.5 0.9 %copy-start.5 = (bf16[256,256]{1,0:T(8,128)(2,1)S(1)}, bf16[256,256]{1,0:T(8,128)(2,1)}, u32[]{:S(2)}) copy-start(bf16[256,256]{1,0:T(8,128)(2,1)} %two.1) | copy-start | bytes 393220
  2.4 0.7 %copy-start.6 = (s32[2,16]{1,0:T(2,128)S(1)}, s32[2,16]{1,0:T(2,128)}, u32[]{:S(2)}) copy-start(s32[2,16]{1,0:T(2,128)} %table.1) | copy-start | bytes 388
  3.1 0.7 %copy-start.7 = (s32[256]{0:T(256)S(1)}, s32[256]{0:T(256)}, u32[]{:S(2)}) copy-start(s32[256]{0:T(256)} %param.14) | copy-start | bytes 3076
  4.7 6.5 %collective-permute-start = (bf16[256,256]{1,0:T(8,128)(2,1)S(1)}, bf16[256,256]{1,0:T(8,128)(2,1)S(1)}, u32[]{:S(2)}, u32[]{:S(2)}) collective-permute-start(bf16[256,256]{1,0:T(8,128)(2,1)S(1)} %get-tuple-element.33.rest_0_.mine), channel_id=1, source_target_pairs={{0,4},{1,5},{4,8},{5,9},{8,12},{9,13},{12,14},{13,15},{14,10},{15,... | collective-permute-start | bytes 393224 | tf_op jit(solution)/shard_map/ppermute | solution.py:179
  11.2 1.6 %copy-start = (bf16[256,4096]{1,0:T(8,128)(2,1)S(1)}, bf16[256,4096]{1,0:T(8,128)(2,1)}, u32[]{:S(2)}) copy-start(bf16[256,4096]{1,0:T(8,128)(2,1)} %window.12) | copy-start | bytes 6291460
  12.9 18.5 %collective-permute-start.1 = (bf16[256,2048]{1,0:T(8,128)(2,1)S(1)}, bf16[256,2048]{1,0:T(8,128)(2,1)S(1)}, u32[]{:S(2)}, u32[]{:S(2)}) collective-permute-start(bf16[256,2048]{1,0:T(8,128)(2,1)S(1)} %swap.1), channel_id=1, source_target_pairs={{0,1},{1,0},{2,3},{3,2},{4,5},{5,4},{6,7},{7,6},{8,9},{9,8},{10,11... | collective-permute-start | bytes 3145736 | tf_op jit(solution)/shard_map/ppermute | solution.py:179
  13.0 6.3 %collective-permute-start.2 = (bf16[256,256]{1,0:T(8,128)(2,1)S(1)}, bf16[256,256]{1,0:T(8,128)(2,1)S(1)}, u32[]{:S(2)}, u32[]{:S(2)}) collective-permute-start(bf16[256,256]{1,0:T(8,128)(2,1)S(1)} %get-tuple-element.33.rest_0_.mine), channel_id=1, source_target_pairs={{4,0},{5,1},{8,4},{9,5},{12,8},{13,9},{14,12},{15,13},{10,14},{11,... | collective-permute-start | bytes 393224 | tf_op jit(solution)/shard_map/ppermute | solution.py:179
  14.8 7.4 %collective-permute-start.11 = (bf16[256,256]{1,0:T(8,128)(2,1)S(1)}, bf16[256,256]{1,0:T(8,128)(2,1)S(1)}, u32[]{:S(2)}, u32[]{:S(2)}) collective-permute-start(bf16[256,256]{1,0:T(8,128)(2,1)S(1)} %get-tuple-element.42.m_two.rest_0_.mine), channel_id=1, source_target_pairs={{4,0},{5,1},{8,4},{9,5},{12,8},{13,9},{14,12},{15,13},{10,14},{11,... | collective-permute-start | bytes 393224 | tf_op jit(solution)/shard_map/ppermute | solution.py:179
  16.4 7.5 %collective-permute-start.10 = (bf16[256,256]{1,0:T(8,128)(2,1)S(1)}, bf16[256,256]{1,0:T(8,128)(2,1)S(1)}, u32[]{:S(2)}, u32[]{:S(2)}) collective-permute-start(bf16[256,256]{1,0:T(8,128)(2,1)S(1)} %get-tuple-element.42.m_two.rest_0_.mine), channel_id=1, source_target_pairs={{0,4},{1,5},{4,8},{5,9},{8,12},{9,13},{12,14},{13,15},{14,10},{15,... | collective-permute-start | bytes 393224 | tf_op jit(solution)/shard_map/ppermute | solution.py:179
  16.8 7.6 %collective-permute-start.3 = (bf16[256,256]{1,0:T(8,128)(2,1)S(1)}, bf16[256,256]{1,0:T(8,128)(2,1)S(1)}, u32[]{:S(2)}, u32[]{:S(2)}) collective-permute-start(bf16[256,256]{1,0:T(8,128)(2,1)S(1)} %collective-permute-done.rest_1_), channel_id=1, source_target_pairs={{0,4},{1,5},{4,8},{5,9},{8,12},{9,13},{12,14},{13,15},{14,10},{15,... | collective-permute-start | bytes 393224 | tf_op jit(solution)/shard_map/ppermute | solution.py:179
  19.3 6.7 %collective-permute-start.4 = (bf16[256,256]{1,0:T(8,128)(2,1)S(1)}, bf16[256,256]{1,0:T(8,128)(2,1)S(1)}, u32[]{:S(2)}, u32[]{:S(2)}) collective-permute-start(bf16[256,256]{1,0:T(8,128)(2,1)S(1)} %collective-permute-done.2.rest_2_), channel_id=1, source_target_pairs={{4,0},{5,1},{8,4},{9,5},{12,8},{13,9},{14,12},{15,13},{10,14},{11,... | collective-permute-start | bytes 393224 | tf_op jit(solution)/shard_map/ppermute | solution.py:179
  22.1 5.7 %collective-permute-start.13 = (bf16[256,256]{1,0:T(8,128)(2,1)S(1)}, bf16[256,256]{1,0:T(8,128)(2,1)S(1)}, u32[]{:S(2)}, u32[]{:S(2)}) collective-permute-start(bf16[256,256]{1,0:T(8,128)(2,1)S(1)} %collective-permute-done.11.rest_2_), channel_id=1, source_target_pairs={{4,0},{5,1},{8,4},{9,5},{12,8},{13,9},{14,12},{15,13},{10,14},{11,... | collective-permute-start | bytes 393224 | tf_op jit(solution)/shard_map/ppermute | solution.py:179
  23.9 6.4 %collective-permute-start.12 = (bf16[256,256]{1,0:T(8,128)(2,1)S(1)}, bf16[256,256]{1,0:T(8,128)(2,1)S(1)}, u32[]{:S(2)}, u32[]{:S(2)}) collective-permute-start(bf16[256,256]{1,0:T(8,128)(2,1)S(1)} %collective-permute-done.10.rest_1_), channel_id=1, source_target_pairs={{0,4},{1,5},{4,8},{5,9},{8,12},{9,13},{12,14},{13,15},{14,10},{15,... | collective-permute-start | bytes 393224 | tf_op jit(solution)/shard_map/ppermute | solution.py:179
  24.4 6.6 %collective-permute-start.5 = (bf16[256,256]{1,0:T(8,128)(2,1)S(1)}, bf16[256,256]{1,0:T(8,128)(2,1)S(1)}, u32[]{:S(2)}, u32[]{:S(2)}) collective-permute-start(bf16[256,256]{1,0:T(8,128)(2,1)S(1)} %collective-permute-done.3.rest_0_), channel_id=1, source_target_pairs={{0,4},{1,5},{4,8},{5,9},{8,12},{9,13},{12,14},{13,15},{14,10},{15,... | collective-permute-start | bytes 393224 | tf_op jit(solution)/shard_map/ppermute | solution.py:179
  26.0 7.5 %collective-permute-start.6 = (bf16[256,256]{1,0:T(8,128)(2,1)S(1)}, bf16[256,256]{1,0:T(8,128)(2,1)S(1)}, u32[]{:S(2)}, u32[]{:S(2)}) collective-permute-start(bf16[256,256]{1,0:T(8,128)(2,1)S(1)} %collective-permute-done.4.rest_1_), channel_id=1, source_target_pairs={{4,0},{5,1},{8,4},{9,5},{12,8},{13,9},{14,12},{15,13},{10,14},{11,... | collective-permute-start | bytes 393224 | tf_op jit(solution)/shard_map/ppermute | solution.py:179
  27.8 5.8 %collective-permute-start.15 = (bf16[256,256]{1,0:T(8,128)(2,1)S(1)}, bf16[256,256]{1,0:T(8,128)(2,1)S(1)}, u32[]{:S(2)}, u32[]{:S(2)}) collective-permute-start(bf16[256,256]{1,0:T(8,128)(2,1)S(1)} %collective-permute-done.13.rest_1_), channel_id=1, source_target_pairs={{4,0},{5,1},{8,4},{9,5},{12,8},{13,9},{14,12},{15,13},{10,14},{11,... | collective-permute-start | bytes 393224 | tf_op jit(solution)/shard_map/ppermute | solution.py:179
  30.3 5.4 %collective-permute-start.7 = (bf16[256,256]{1,0:T(8,128)(2,1)S(1)}, bf16[256,256]{1,0:T(8,128)(2,1)S(1)}, u32[]{:S(2)}, u32[]{:S(2)}) collective-permute-start(bf16[256,256]{1,0:T(8,128)(2,1)S(1)} %get-tuple-element.33.rest_0_.mine), channel_id=1, source_target_pairs={{0,1},{1,0},{2,3},{3,2},{4,5},{5,4},{6,7},{7,6},{8,9},{9,8},{10,11... | collective-permute-start | bytes 393224 | tf_op jit(solution)/shard_map/ppermute | solution.py:179
  31.0 6.4 %collective-permute-start.8 = (bf16[256,256]{1,0:T(8,128)(2,1)S(1)}, bf16[256,256]{1,0:T(8,128)(2,1)S(1)}, u32[]{:S(2)}, u32[]{:S(2)}) collective-permute-start(bf16[256,256]{1,0:T(8,128)(2,1)S(1)} %collective-permute-done.5.rest_2_), channel_id=1, source_target_pairs={{0,4},{1,5},{4,8},{5,9},{8,12},{9,13},{12,14},{13,15},{14,10},{15,... | collective-permute-start | bytes 393224 | tf_op jit(solution)/shard_map/ppermute | solution.py:179
  31.4 7.6 %collective-permute-start.14 = (bf16[256,256]{1,0:T(8,128)(2,1)S(1)}, bf16[256,256]{1,0:T(8,128)(2,1)S(1)}, u32[]{:S(2)}, u32[]{:S(2)}) collective-permute-start(bf16[256,256]{1,0:T(8,128)(2,1)S(1)} %collective-permute-done.12.rest_0_), channel_id=1, source_target_pairs={{0,4},{1,5},{4,8},{5,9},{8,12},{9,13},{12,14},{13,15},{14,10},{15,... | collective-permute-start | bytes 393224 | tf_op jit(solution)/shard_map/ppermute | solution.py:179
  33.5 6.0 %collective-permute-start.16 = (bf16[256,256]{1,0:T(8,128)(2,1)S(1)}, bf16[256,256]{1,0:T(8,128)(2,1)S(1)}, u32[]{:S(2)}, u32[]{:S(2)}) collective-permute-start(bf16[256,256]{1,0:T(8,128)(2,1)S(1)} %get-tuple-element.42.m_two.rest_0_.mine), channel_id=1, source_target_pairs={{0,1},{1,0},{2,3},{3,2},{4,5},{5,4},{6,7},{7,6},{8,9},{9,8},{10,11... | collective-permute-start | bytes 393224 | tf_op jit(solution)/shard_map/ppermute | solution.py:179
  33.6 5.9 %collective-permute-start.17 = (bf16[256,256]{1,0:T(8,128)(2,1)S(1)}, bf16[256,256]{1,0:T(8,128)(2,1)S(1)}, u32[]{:S(2)}, u32[]{:S(2)}) collective-permute-start(bf16[256,256]{1,0:T(8,128)(2,1)S(1)} %collective-permute-done.15.rest_3_), channel_id=1, source_target_pairs={{4,0},{5,1},{8,4},{9,5},{12,8},{13,9},{14,12},{15,13},{10,14},{11,... | collective-permute-start | bytes 393224 | tf_op jit(solution)/shard_map/ppermute | solution.py:179
  38.0 2.7 %collective-permute-start.9 = (f32[256,256]{1,0:T(8,128)S(1)}, f32[256,256]{1,0:T(8,128)S(1)}, u32[]{:S(2)}, u32[]{:S(2)}) collective-permute-start(f32[256,256]{1,0:T(8,128)S(1)} %get-tuple-element.40), channel_id=1, source_target_pairs={{0,1},{1,0},{2,3},{3,2},{4,5},{5,4},{6,7},{7,6},{8,9},{9,8},{10,11... | collective-permute-start | bytes 786440 | tf_op jit(solution)/shard_map/ppermute | solution.py:179
  39.5 1.3 %copy-start.1 = (bf16[256,256]{1,0:T(8,128)(2,1)S(1)}, bf16[256,256]{1,0:T(8,128)(2,1)}, u32[]{:S(2)}) copy-start(bf16[256,256]{1,0:T(8,128)(2,1)} %cross.3) | copy-start | bytes 393220
  40.2 20.5 %copy-start.2 = (f32[256,256]{1,0:T(8,128)S(1)}, f32[256,256]{1,0:T(8,128)}, u32[]{:S(2)}) copy-start(f32[256,256]{1,0:T(8,128)} %diag_one.1) | copy-start | bytes 786436
  40.2 20.5 %copy-start.3 = (f32[256,256]{1,0:T(8,128)S(1)}, f32[256,256]{1,0:T(8,128)}, u32[]{:S(2)}) copy-start(f32[256,256]{1,0:T(8,128)} %diag_two.1) | copy-start | bytes 786436
  40.2 1.4 %collective-permute-start.18 = (f32[144,256]{1,0:T(8,128)S(1)}, f32[144,256]{1,0:T(8,128)S(1)}, u32[]{:S(2)}, u32[]{:S(2)}) collective-permute-start(f32[144,256]{1,0:T(8,128)S(1)} %get-tuple-element.51), channel_id=1, source_target_pairs={{0,1},{1,0},{2,3},{3,2},{4,5},{5,4},{6,7},{7,6},{8,9},{9,8},{10,11... | collective-permute-start | bytes 442376 | tf_op jit(solution)/shard_map/ppermute | solution.py:179
  40.3 19.1 %collective-permute-start.28 = (f32[256,256]{1,0:T(8,128)S(1)}, f32[256,256]{1,0:T(8,128)S(1)}, u32[]{:S(2)}, u32[]{:S(2)}) collective-permute-start(f32[256,256]{1,0:T(8,128)S(1)} %get-tuple-element.56), channel_id=1, source_target_pairs={{0,1},{1,0},{2,3},{3,2},{4,5},{5,4},{6,7},{7,6},{8,9},{9,8},{10,11... | collective-permute-start | bytes 786440 | tf_op jit(solution)/shard_map/ppermute | solution.py:179
  41.5 1.8 %collective-permute-start.23 = (f32[128,256]{1,0:T(8,128)S(1)}, f32[128,256]{1,0:T(8,128)S(1)}, u32[]{:S(2)}, u32[]{:S(2)}) collective-permute-start(f32[128,256]{1,0:T(8,128)S(1)} %get-tuple-element.53), channel_id=1, source_target_pairs={{0,1},{1,0},{2,3},{3,2},{4,5},{5,4},{6,7},{7,6},{8,9},{9,8},{10,11... | collective-permute-start | bytes 393224 | tf_op jit(solution)/shard_map/ppermute | solution.py:179
  41.6 4.8 %collective-permute-start.19 = (bf16[144,256]{1,0:T(8,128)(2,1)S(1)}, bf16[144,256]{1,0:T(8,128)(2,1)S(1)}, u32[]{:S(2)}, u32[]{:S(2)}) collective-permute-start(bf16[144,256]{1,0:T(8,128)(2,1)S(1)} %add_convert_fusion.2), channel_id=1, source_target_pairs={{0,2},{1,3},{2,0},{3,1},{4,6},{5,7},{6,4},{7,5},{8,10},{9,11},{10,... | collective-permute-start | bytes 221192 | tf_op jit(solution)/shard_map/ppermute | solution.py:179
  43.3 4.8 %collective-permute-start.24 = (bf16[128,256]{1,0:T(8,128)(2,1)S(1)}, bf16[128,256]{1,0:T(8,128)(2,1)S(1)}, u32[]{:S(2)}, u32[]{:S(2)}) collective-permute-start(bf16[128,256]{1,0:T(8,128)(2,1)S(1)} %add_convert_fusion.5), channel_id=1, source_target_pairs={{0,2},{1,3},{2,0},{3,1},{4,6},{5,7},{6,4},{7,5},{8,10},{9,11},{10,... | collective-permute-start | bytes 196616 | tf_op jit(solution)/shard_map/ppermute | solution.py:179
  46.5 4.8 %collective-permute-start.20 = (bf16[144,256]{1,0:T(8,128)(2,1)S(1)}, bf16[144,256]{1,0:T(8,128)(2,1)S(1)}, u32[]{:S(2)}, u32[]{:S(2)}) collective-permute-start(bf16[144,256]{1,0:T(8,128)(2,1)S(1)} %add_convert_fusion.1), channel_id=1, source_target_pairs={{0,4},{1,5},{2,6},{3,7},{4,0},{5,1},{6,2},{7,3},{8,12},{9,13},{10,... | collective-permute-start | bytes 221192 | tf_op jit(solution)/shard_map/ppermute | solution.py:179
  48.1 5.8 %collective-permute-start.25 = (bf16[128,256]{1,0:T(8,128)(2,1)S(1)}, bf16[128,256]{1,0:T(8,128)(2,1)S(1)}, u32[]{:S(2)}, u32[]{:S(2)}) collective-permute-start(bf16[128,256]{1,0:T(8,128)(2,1)S(1)} %add_convert_fusion.4), channel_id=1, source_target_pairs={{0,4},{1,5},{2,6},{3,7},{4,0},{5,1},{6,2},{7,3},{8,12},{9,13},{10,... | collective-permute-start | bytes 196616 | tf_op jit(solution)/shard_map/ppermute | solution.py:179
  51.4 6.8 %collective-permute-start.21 = (bf16[144,256]{1,0:T(8,128)(2,1)S(1)}, bf16[144,256]{1,0:T(8,128)(2,1)S(1)}, u32[]{:S(2)}, u32[]{:S(2)}) collective-permute-start(bf16[144,256]{1,0:T(8,128)(2,1)S(1)} %add_convert_fusion), channel_id=1, source_target_pairs={{0,8},{1,9},{2,10},{3,11},{4,12},{5,13},{6,14},{7,15},{8,0},{9,1},... | collective-permute-start | bytes 221192 | tf_op jit(solution)/shard_map/ppermute | solution.py:179
  54.0 5.2 %collective-permute-start.26 = (bf16[128,256]{1,0:T(8,128)(2,1)S(1)}, bf16[128,256]{1,0:T(8,128)(2,1)S(1)}, u32[]{:S(2)}, u32[]{:S(2)}) collective-permute-start(bf16[128,256]{1,0:T(8,128)(2,1)S(1)} %add_convert_fusion.3), channel_id=1, source_target_pairs={{0,8},{1,9},{2,10},{3,11},{4,12},{5,13},{6,14},{7,15},{8,0},{9,1},... | collective-permute-start | bytes 196616 | tf_op jit(solution)/shard_map/ppermute | solution.py:179
  58.2 1.8 %collective-permute-start.22 = (f32[144,256]{1,0:T(8,128)S(1)}, f32[144,256]{1,0:T(8,128)S(1)}, u32[]{:S(2)}, u32[]{:S(2)}) collective-permute-start(f32[144,256]{1,0:T(8,128)S(1)} %convert_add_fusion.pack_a), channel_id=1, source_target_pairs={{0,1},{1,0},{2,3},{3,2},{4,5},{5,4},{6,7},{7,6},{8,9},{9,8},{10,11... | collective-permute-start | bytes 442376 | tf_op jit(solution)/shard_map/ppermute | solution.py:179
  59.2 1.4 %collective-permute-start.27 = (f32[128,256]{1,0:T(8,128)S(1)}, f32[128,256]{1,0:T(8,128)S(1)}, u32[]{:S(2)}, u32[]{:S(2)}) collective-permute-start(f32[128,256]{1,0:T(8,128)S(1)} %convert_add_fusion.1.cross_a), channel_id=1, source_target_pairs={{0,1},{1,0},{2,3},{3,2},{4,5},{5,4},{6,7},{7,6},{8,9},{9,8},{10,11... | collective-permute-start | bytes 393224 | tf_op jit(solution)/shard_map/ppermute | solution.py:179

commit v3 on v2

--- a/solution.py
+++ b/solution.py
@@ -11,6 +11,7 @@
 AXIS = "prow"
 VMEM = pl.BlockSpec(memory_space=pltpu.VMEM)
 SMEM = pl.BlockSpec(memory_space=pltpu.SMEM)
+HBM = pl.BlockSpec(memory_space=pltpu.HBM)
 
 
 def dot(left, right):
@@ -26,15 +27,16 @@
     return high, (x - high.astype(F32)).astype(BF16)
 
 
-def call(body, name, outs, args, n_smem=0, flops=0, aliases=None):
+def call(body, name, outs, args, n_smem=0, flops=0, aliases=None, specs=None, scratch=()):
     size = sum(a.size * a.dtype.itemsize for a in args)
     return pl.pallas_call(
         body,
         name=name,
         out_shape=tuple(jax.ShapeDtypeStruct(s, d) for s, d in outs),
-        in_specs=[SMEM] * n_smem + [VMEM] * (len(args) - n_smem),
+        in_specs=specs or [SMEM] * n_smem + [VMEM] * (len(args) - n_smem),
         out_specs=tuple(VMEM for _ in outs),
         input_output_aliases=aliases or {},
+        scratch_shapes=scratch,
         compiler_params=pltpu.CompilerParams(vmem_limit_bytes=16 << 20),
         cost_estimate=pl.CostEstimate(flops=flops, bytes_accessed=size, transcendentals=0),
     )(*args)
@@ -49,36 +51,44 @@
     return chip_of((position + offset + chips) % chips, chips)
 
 
-def mask_body(table, rows, one, two, m_one, m_two, w_one, w_two):
-    n = one.shape[0]
-    index = rows[...]
-    on_diagonal = lax.broadcasted_iota(jnp.int32, (n, n), 0) == lax.broadcasted_iota(jnp.int32, (n, n), 1)
-    ones = jnp.ones((n, n), BF16)
-    for which, panel, masked, weights in ((0, one, m_one, w_one), (1, two, m_two, w_two)):
+def in_hbm(x):
+    return pltpu.with_memory_space_constraint(x, pltpu.HBM)
+
+
+def diagonal_of(weight):
+    n = weight.shape[1]
+    on = lax.broadcasted_iota(jnp.int32, (n, n), 0) == lax.broadcasted_iota(jnp.int32, (n, n), 1)
+    return jnp.where(on, jnp.broadcast_to(weight, (n, n)), 0.0).astype(BF16)
+
+
+def mask_body(table, rows, one, two, window, m_one, m_two, weights, window_v, table_v, rows_v, one_v, two_v, sems):
+    moves = (table, table_v), (rows, rows_v), (one, one_v), (two, two_v), (window, window_v)
+    copies = [pltpu.make_async_copy(src, dst, sems.at[i]) for i, (src, dst) in enumerate(moves)]
+    for copy in copies:
+        copy.start()
+    copies[0].wait()
+    copies[1].wait()
+    index = rows_v[...]
+    for which, panel, masked in ((0, one_v, m_one), (1, two_v, m_two)):
         weight = jnp.zeros(index.shape, F32)
         for s in range(table.shape[1]):
-            weight = jnp.where(index == s, table[which, s].astype(F32), weight)
-        chosen = jnp.where(on_diagonal, jnp.broadcast_to(weight, (n, n)), 0.0).astype(BF16)
+            weight = jnp.where(index == s, table_v[which, s].astype(F32), weight)
+        weights[which : which + 1] = weight
+        chosen = diagonal_of(weight)
+        copies[2 + which].wait()
         masked[...] = dot(chosen, panel[...]).astype(BF16)
-        weights[...] = dot(chosen, ones).astype(BF16)
-
-
-def swap_body(window, out):
-    width = out.shape[0]
-    other = 1 - lax.axis_index(AXIS) % 2
-    for t in range(out.shape[1] // width):
-        out[:, t * width : (t + 1) * width] = window[:, pl.ds(pl.multiple_of((2 * t + other) * width, width), width)]
+    copies[4].wait()
 
 
 def add_products(offsets, window, swapped, pieces, x_own, x_other):
     n = window.shape[0]
     me = lax.axis_index(AXIS)
-    chip, core = me // 2, me % 2
     for offset, piece in zip(offsets, pieces, strict=True):
-        t = chip_at(chip, offset, window.shape[1] // (2 * n))
+        block = 2 * chip_at(me // 2, offset, window.shape[1] // (2 * n)) + me % 2
+        columns = pl.ds(pl.multiple_of(block * n, n), n)
         value = piece[...]
-        x_own += dot(window[:, pl.ds(pl.multiple_of((2 * t + core) * n, n), n)], value)
-        x_other += dot(swapped[:, pl.ds(pl.multiple_of(t * n, n), n)], value)
+        x_own += dot(window[:, columns], value)
+        x_other += dot(swapped[:, columns], value)
     return x_own, x_other
 
 
@@ -102,8 +112,10 @@
     total[...] = (dot_t(mine[...], a) + dot_t(sibling[...], c)) + (dot_t(mine[...], b) + dot_t(sibling[...], d))
 
 
-def column_one_body(own, received, w_one, m_two, cross, column, carried, keep, send):
-    exact = -(w_one[...].astype(F32) * (own[...] + received[...]))
+def column_one_body(own, received, weights, m_two, cross, column, carried, keep, send):
+    n = column.shape[0]
+    weight = dot(diagonal_of(weights[0:1]), jnp.ones((n, n), BF16))
+    exact = -(weight * (own[...] + received[...]))
     rounded = exact.astype(BF16)
     column[...] = rounded
     carried[...] = dot(rounded, cross[...])
@@ -114,9 +126,11 @@
     send[...] = jnp.where(first, both[half:], both[:half])
 
 
-def column_two_body(own, received, w_two, carried, column):
+def column_two_body(own, received, weights, carried, column):
+    n = column.shape[0]
+    weight = dot(diagonal_of(weights[1:2]), jnp.ones((n, n), BF16))
     image = own[...] + received[...]
-    column[...] = (-(w_two[...].astype(F32) * (image + carried[...]))).astype(BF16)
+    column[...] = (-(weight * (image + carried[...]))).astype(BF16)
 
 
 def pack_body(one, two, keep, send):
@@ -180,13 +194,21 @@
 
     square = ((rows, width), F32)
     tile = ((rows, width), BF16)
-    m_one, m_two, w_one, w_two = call(
+    m_one, m_two, weights, window = call(
         mask_body,
         "mask",
-        (tile, tile, tile, tile),
-        (struct_mask, row_super.reshape(1, -1), panel_one, panel_two),
-        n_smem=1,
-    )
+        (tile, tile, ((2, rows), F32), (inverse_window.shape, BF16)),
+        tuple(map(in_hbm, (struct_mask, row_super.reshape(1, -1), panel_one, panel_two, inverse_window))),
+        specs=[HBM] * 5,
+        scratch=[
+            pltpu.SMEM(struct_mask.shape, jnp.int32),
+            pltpu.VMEM((1, rows), jnp.int32),
+            pltpu.VMEM((rows, width), BF16),
+            pltpu.VMEM((rows, width), BF16),
+            pltpu.SemaphoreType.DMA((5,)),
+        ],
+    )
+
     steps = chips // 2
     one, two = [(0, m_one)], [(0, m_two)]
     one_up = one_down = m_one
@@ -198,61 +220,64 @@
         two += [(-k, two_up), (k, two_down)]
     one.append((-steps, send(one_up, ahead)))
     two.append((steps, send(two_down, back)))
-
-    window, _ = lax.optimization_barrier((inverse_window, one[1][1]))
-    (window_part,) = call(swap_body, "swap", (((rows, inverse_window.shape[1] // 2), BF16),), (window,))
-    swapped = send(window_part, flip[0])
+    after = one[-3][1], one[-2][1], two[-2][1], two[-3][1]
+
+    swapped = send(window, flip[0])
     sibling_one = send(m_one, flip[0])
     sibling_two = send(m_two, flip[0])
 
-    def image(name, pieces, mine, sibling):
-        def stage(body, label, chosen, outs, *more, aliases=None):
-            offsets, values = zip(*chosen, strict=True)
-            return call(
-                functools.partial(body, offsets),
-                name + label,
-                outs,
-                (inverse_window, swapped, *more, *values),
-                flops=2 * 2 * rows * width * width * len(chosen),
-                aliases=aliases,
+    def stage(body, name, chosen, outs, *more, aliases=None):
+        offsets, values = zip(*chosen, strict=True)
+        return call(
+            functools.partial(body, offsets),
+            name,
+            outs,
+            (window, swapped, *more, *values),
+            flops=2 * 2 * rows * width * width * len(chosen),
+            aliases=aliases,
+        )
+
+    def begin(name, pieces, after):
+        pieces = [(offset, lax.optimization_barrier((piece, after))[0]) for offset, piece in pieces]
+        own, other = stage(image_first_body, name + "_first", pieces[:3], (square, square))
+        for i in range(3, len(pieces), 4):
+            own, other = stage(
+                image_more_body, name + "_more", pieces[i : i + 4], (square, square), own, other, aliases={2: 0, 3: 1}
             )
-
-        kept = {2: 0, 3: 1}
-        own, other = stage(image_first_body, "_first", pieces[:3], (square, square))
-        middle = pieces[3:-1]
-        for i in range(0, len(middle), 4):
-            own, other = stage(image_more_body, "_more", middle[i : i + 4], (square, square), own, other, aliases=kept)
-        return stage(
-            image_last_body, "_last", pieces[-1:], (square, square, ((width, width), F32)), own, other, mine, sibling, aliases=kept
-        )
-
-    own_one, other_one, total_one = image("image_one", one, m_one, sibling_one)
+        return own, other
+
+    def finish(name, last, own, other, panel, sibling):
+        outs = square, square, ((width, width), F32)
+        return stage(image_last_body, name, [last], outs, own, other, panel, sibling, aliases={2: 0, 3: 1})
+
+    def half_sum(keep, away):
+        return keep + send(away, flip[0])
+
+    own_one, other_one, total_one = finish("image_one", one[-1], *begin("image_one", one[:-1], after), m_one, sibling_one)
     received_one = send(other_one, flip[0])
     column_one, carried, keep_x, send_x = call(
         column_one_body,
         "column_one",
         (tile, square, ((half, width), F32), ((half, width), F32)),
-        (own_one, received_one, w_one, m_two, cross_block),
-    )
-    own_two, other_two, total_two = image("image_two", two, m_two, sibling_two)
+        (own_one, received_one, weights, m_two, cross_block),
+    )
+    cross_half = half_sum(keep_x, send_x)
+    own_two, other_two = begin("image_two", two[:-1], after)
+    own_two, other_two, total_two = finish("image_two", two[-1], own_two, other_two, m_two, sibling_two)
     keep_p, send_p = call(
-        pack_body,
-        "pack",
-        (((half + 16, width), F32), ((half + 16, width), F32)),
-        (total_one, total_two),
+        pack_body, "pack", (((half + 16, width), F32), ((half + 16, width), F32)), (total_one, total_two)
     )
     received_two = send(other_two, flip[0])
-    (column_two,) = call(column_two_body, "column_two", (tile,), (own_two, received_two, w_two, carried))
-
-    def summed(keep, away):
-        value = keep + send(away, flip[0])
+    (column_two,) = call(column_two_body, "column_two", (tile,), (own_two, received_two, weights, carried))
+
+    def summed(value):
         for perm in flip[1:]:
             value = value.astype(BF16)
             value = value.astype(F32) + send(value, perm).astype(F32)
         return value, send(value, flip[0])
 
-    cross_a, cross_b = summed(keep_x, send_x)
-    pack_a, pack_b = summed(keep_p, send_p)
+    cross_a, cross_b = summed(cross_half)
+    pack_a, pack_b = summed(half_sum(keep_p, send_p))
     full = ((width, width), F32)
     block_one, edge_block, block_two = call(
         last_body,

time: 62.1 us -> 54.3 us (0.87)
  local copies, waits for them, and re-layouts: 4.77 us -> 0.02 us
  starting transfers between devices: 30.6 us -> 25.9 us
  Pallas kernels: 6.53 us -> 7.65 us
    unnamed x16 -> x6, local copies, waits for them, and re-layouts: 4.77 us -> 0.02 us
    ppermute x29, starting transfers between devices: 30.6 us -> 25.9 us  [send(): return lax.ppermute(x, AXIS, perm)]
    pallas_call x12 -> x11, Pallas kernels: 6.53 us -> 7.65 us  [call(): pl.pallas_call(body, name=name, out_shape=tuple((jax.ShapeDtypeStruct(s,...]
  transfers between devices with their start and end apart: 29 -> 29, of which waited for: 14 -> 12; matrix products, arithmetic and copies ran while one was open for 0% -> 0% of each run, Pallas kernels for 7% -> 8%
where the time goes in v3:
time: 54.3 us; the launch traced here: 54 us
  starting transfers between devices  25.9 us (48%)
  waiting for transfers between devices  19.5 us (36%)
  Pallas kernels  7.65 us (14%)
  between operations  0.82 us (2%)
    ppermute x29, starting transfers between devices, send(): return lax.ppermute(x, AXIS, perm)  25.9 us
    ppermute x29, waiting for transfers between devices, send(): return lax.ppermute(x, AXIS, perm)  19.5 us
    pallas_call x11, Pallas kernels, call(): pl.pallas_call(body, name=name, out_shape=tuple((jax.ShapeDtypeStruct(s,...  7.65 us
  transfers between devices with their start and end apart: 29, of which 12 were waited for; matrix products, arithmetic and copies ran while one was open for 0% of the time, Pallas kernels for 8%

profile of v3, /device:TPU:0, one launch (start us, length us, event | category | flops | bytes accessed | tf_op | source)
XLA Modules:
  0.0 54.0 jit_solution(4279983949765663899)
XLA Ops:
  0.6 1.8 %mask.1 = (bf16[256,256]{1,0:T(8,128)(2,1)S(1)}, bf16[256,256]{1,0:T(8,128)(2,1)S(1)}, f32[2,256]{1,0:T(2,128)S(1)}, bf16[256,4096]{1,0:T(8,128)(2,1)S(1)}) custom-call(s32[2,16]{1,0:T(2,128)} %table.1, s32[1,256]{1,0:T(1,128)} %bitcast.1, bf16[256,256]{1,0:T(8,128)(2,1)} %one.1, bf16[256,256]{1,0:T(8,128)(2,1)} %two.1, bf16[256,4096]{1,0:T(8,128)(2,1)} %window.1), custom_call_target="tpu_custom_call" | custom-call | bytes 2360448 | tf_op jit(solution)/shard_map/mask/pallas_call | solution.py:32
  2.4 0.5 collective-permute-start
  3.0 2.6 %collective-permute-start.7 = (bf16[256,256]{1,0:T(8,128)(2,1)S(1)}, bf16[256,256]{1,0:T(8,128)(2,1)S(1)}, u32[]{:S(2)}, u32[]{:S(2)}) collective-permute-start(bf16[256,256]{1,0:T(8,128)(2,1)S(1)} %get-tuple-element.65.m_two.rest_0_.mine), channel_id=1, source_target_pairs={{4,0},{5,1},{8,4},{9,5},{12,8},{13,9},{14,12},{15,13},{10,14},{11,... | collective-permute-start | bytes 393224 | tf_op jit(solution)/shard_map/ppermute | solution.py:193
  5.5 0.1 collective-permute-start.1
  5.7 1.9 %collective-permute-start.10 = (bf16[256,256]{1,0:T(8,128)(2,1)S(1)}, bf16[256,256]{1,0:T(8,128)(2,1)S(1)}, u32[]{:S(2)}, u32[]{:S(2)}) collective-permute-start(bf16[256,256]{1,0:T(8,128)(2,1)S(1)} %get-tuple-element.65.m_two.rest_0_.mine), channel_id=1, source_target_pairs={{0,4},{1,5},{4,8},{5,9},{8,12},{9,13},{12,14},{13,15},{14,10},{15,... | collective-permute-start | bytes 393224 | tf_op jit(solution)/shard_map/ppermute | solution.py:193
  7.6 0.1 collective-permute-start.4
  7.7 2.0 %collective-permute-done.7.rest_2_ = bf16[256,256]{1,0:T(8,128)(2,1)S(1)} collective-permute-done((bf16[256,256]{1,0:T(8,128)(2,1)S(1)}, bf16[256,256]{1,0:T(8,128)(2,1)S(1)}, u32[]{:S(2)}, u32[]{:S(2)}) %collective-permute-start.7) | collective-permute-done | bytes 131104 | tf_op jit(solution)/shard_map/ppermute | solution.py:193
  9.7 2.1 %collective-permute-start.8 = (bf16[256,256]{1,0:T(8,128)(2,1)S(1)}, bf16[256,256]{1,0:T(8,128)(2,1)S(1)}, u32[]{:S(2)}, u32[]{:S(2)}) collective-permute-start(bf16[256,256]{1,0:T(8,128)(2,1)S(1)} %collective-permute-done.7.rest_2_), channel_id=1, source_target_pairs={{4,0},{5,1},{8,4},{9,5},{12,8},{13,9},{14,12},{15,13},{10,14},{11,... | collective-permute-start | bytes 393224 | tf_op jit(solution)/shard_map/ppermute | solution.py:193
  11.8 0.0 collective-permute-done.1.rest_1_
  11.9 0.1 collective-permute-start.2
  12.0 2.4 %collective-permute-done.10.rest_1_ = bf16[256,256]{1,0:T(8,128)(2,1)S(1)} collective-permute-done((bf16[256,256]{1,0:T(8,128)(2,1)S(1)}, bf16[256,256]{1,0:T(8,128)(2,1)S(1)}, u32[]{:S(2)}, u32[]{:S(2)}) %collective-permute-start.10) | collective-permute-done | bytes 131104 | tf_op jit(solution)/shard_map/ppermute | solution.py:193
  14.4 0.1 collective-permute-start.11
  14.5 0.0 collective-permute-done.4.rest_2_
  14.5 1.9 %collective-permute-start.5 = (bf16[256,256]{1,0:T(8,128)(2,1)S(1)}, bf16[256,256]{1,0:T(8,128)(2,1)S(1)}, u32[]{:S(2)}, u32[]{:S(2)}) collective-permute-start(bf16[256,256]{1,0:T(8,128)(2,1)S(1)} %collective-permute-done.4.rest_2_), channel_id=1, source_target_pairs={{4,0},{5,1},{8,4},{9,5},{12,8},{13,9},{14,12},{15,13},{10,14},{11,... | collective-permute-start | bytes 393224 | tf_op jit(solution)/shard_map/ppermute | solution.py:193
  16.4 0.0 collective-permute-done.8.rest_1_
  16.4 1.6 %collective-permute-start.9 = (bf16[256,256]{1,0:T(8,128)(2,1)S(1)}, bf16[256,256]{1,0:T(8,128)(2,1)S(1)}, u32[]{:S(2)}, u32[]{:S(2)}) collective-permute-start(bf16[256,256]{1,0:T(8,128)(2,1)S(1)} %collective-permute-done.8.rest_1_), channel_id=1, source_target_pairs={{4,0},{5,1},{8,4},{9,5},{12,8},{13,9},{14,12},{15,13},{10,14},{11,... | collective-permute-start | bytes 393224 | tf_op jit(solution)/shard_map/ppermute | solution.py:193
  18.0 0.5 collective-permute-start.3
  18.5 2.3 %collective-permute-done.11.rest_0_ = bf16[256,256]{1,0:T(8,128)(2,1)S(1)} collective-permute-done((bf16[256,256]{1,0:T(8,128)(2,1)S(1)}, bf16[256,256]{1,0:T(8,128)(2,1)S(1)}, u32[]{:S(2)}, u32[]{:S(2)}) %collective-permute-start.11) | collective-permute-done | bytes 131104 | tf_op jit(solution)/shard_map/ppermute | solution.py:193
  20.8 2.0 %collective-permute-start.6 = (bf16[256,256]{1,0:T(8,128)(2,1)S(1)}, bf16[256,256]{1,0:T(8,128)(2,1)S(1)}, u32[]{:S(2)}, u32[]{:S(2)}) collective-permute-start(bf16[256,256]{1,0:T(8,128)(2,1)S(1)} %collective-permute-done.5.rest_1_), channel_id=1, source_target_pairs={{4,0},{5,1},{8,4},{9,5},{12,8},{13,9},{14,12},{15,13},{10,14},{11,... | collective-permute-start | bytes 393224 | tf_op jit(solution)/shard_map/ppermute | solution.py:193
  22.8 0.0 collective-permute-done.9.rest_3_
  22.8 1.2 %collective-permute-done.3.rest_2_ = bf16[256,256]{1,0:T(8,128)(2,1)S(1)} collective-permute-done((bf16[256,256]{1,0:T(8,128)(2,1)S(1)}, bf16[256,256]{1,0:T(8,128)(2,1)S(1)}, u32[]{:S(2)}, u32[]{:S(2)}) %collective-permute-start.3) | collective-permute-done | bytes 131104 | tf_op jit(solution)/shard_map/ppermute | solution.py:193
  24.0 0.3 collective-permute-start.14
  24.3 1.4 %collective-permute-done.12.rest_2_ = bf16[256,256]{1,0:T(8,128)(2,1)S(1)} collective-permute-done((bf16[256,256]{1,0:T(8,128)(2,1)S(1)}, bf16[256,256]{1,0:T(8,128)(2,1)S(1)}, u32[]{:S(2)}, u32[]{:S(2)}) %collective-permute-start.12) | collective-permute-done | bytes 131104 | tf_op jit(solution)/shard_map/ppermute | solution.py:193
  25.7 0.0 collective-permute-done.6.rest_3_
  25.8 2.0 %collective-permute-start.17 = (bf16[256,256]{1,0:T(8,128)(2,1)S(1)}, bf16[256,256]{1,0:T(8,128)(2,1)S(1)}, u32[]{:S(2)}, u32[]{:S(2)}) collective-permute-start(bf16[256,256]{1,0:T(8,128)(2,1)S(1)} %collective-permute-done.9.rest_3_), channel_id=1, source_target_pairs={{4,0},{5,1},{8,4},{9,5},{12,8},{13,9},{14,12},{15,13},{10,14},{11,... | collective-permute-start | bytes 393224 | tf_op jit(solution)/shard_map/ppermute | solution.py:193
  27.7 0.0 collective-permute-done.swapped
  27.8 0.4 image_one_first.1
  28.1 0.4 image_one_more.1
  28.6 0.0 collective-permute-done.13.sibling
  28.6 0.4 collective-permute-done.14.rest_0_
  29.0 0.6 %image_one.1 = (f32[256,256]{1,0:T(8,128)S(1)}, f32[256,256]{1,0:T(8,128)S(1)}, f32[256,256]{1,0:T(8,128)S(1)}) custom-call(bf16[256,4096]{1,0:T(8,128)(2,1)S(1)} %get-tuple-element.46.window, bf16[256,4096]{1,0:T(8,128)(2,1)S(1)} %collective-permute-done.swapped, ...), custom_call_target="tpu_custom_call", output_to_operand_aliasing={{0}: (2, {}), {1}: (3, {})} | custom-call | flops 67108864 | bytes 5111808 | tf_op jit(solution)/shard_map/image_one/pallas_call | solution.py:32
  29.6 0.1 collective-permute-start.15
  29.6 0.4 image_two_first.1
  30.0 0.5 image_two_more.1
  30.5 0.0 collective-permute-done.16.sibling
  30.5 1.1 %collective-permute-done.17.rest_0_ = bf16[256,256]{1,0:T(8,128)(2,1)S(1)} collective-permute-done((bf16[256,256]{1,0:T(8,128)(2,1)S(1)}, bf16[256,256]{1,0:T(8,128)(2,1)S(1)}, u32[]{:S(2)}, u32[]{:S(2)}) %collective-permute-start.17) | collective-permute-done | bytes 131104 | tf_op jit(solution)/shard_map/ppermute | solution.py:193
  31.6 0.6 %image_two.1 = (f32[256,256]{1,0:T(8,128)S(1)}, f32[256,256]{1,0:T(8,128)S(1)}, f32[256,256]{1,0:T(8,128)S(1)}) custom-call(bf16[256,4096]{1,0:T(8,128)(2,1)S(1)} %get-tuple-element.46.window, bf16[256,4096]{1,0:T(8,128)(2,1)S(1)} %collective-permute-done.swapped, ...), custom_call_target="tpu_custom_call", output_to_operand_aliasing={{0}: (2, {}), {1}: (3, {})} | custom-call | flops 67108864 | bytes 5111808 | tf_op jit(solution)/shard_map/image_two/pallas_call | solution.py:32
  32.2 0.0 copy-start.1
  32.2 0.0 copy-start.2
  32.3 0.1 pack.1
  32.3 0.1 collective-permute-start.18
  32.4 0.5 collective-permute-start.28
  32.9 0.0 collective-permute-done.15.received
  32.9 0.8 %column_one.1 = (bf16[256,256]{1,0:T(8,128)(2,1)}, f32[256,256]{1,0:T(8,128)S(1)}, f32[128,256]{1,0:T(8,128)S(1)}, f32[128,256]{1,0:T(8,128)S(1)}) custom-call(f32[256,256]{1,0:T(8,128)S(1)} %get-tuple-element.60.own, f32[256,256]{1,0:T(8,128)S(1)} %collective-permute-done.15.received, f32[2,256]{1,0:T(2,128)S(1)} %get-tuple-element.62.weights, ...), custom_call_target="tpu_custom_call" | custom-call | bytes 788480 | tf_op jit(solution)/shard_map/column_one/pallas_call | solution.py:32
  33.8 0.1 collective-permute-start.23
  33.8 0.0 collective-permute-done.18
  33.9 1.6 %collective-permute-start.19 = (bf16[144,256]{1,0:T(8,128)(2,1)S(1)}, bf16[144,256]{1,0:T(8,128)(2,1)S(1)}, u32[]{:S(2)}, u32[]{:S(2)}) collective-permute-start(bf16[144,256]{1,0:T(8,128)(2,1)S(1)} %add_convert_fusion.2), channel_id=1, source_target_pairs={{0,2},{1,3},{2,0},{3,1},{4,6},{5,7},{6,4},{7,5},{8,10},{9,11},{10,... | collective-permute-start | bytes 221192 | tf_op jit(solution)/shard_map/ppermute | solution.py:193
  35.5 1.2 %collective-permute-start.24 = (bf16[128,256]{1,0:T(8,128)(2,1)S(1)}, bf16[128,256]{1,0:T(8,128)(2,1)S(1)}, u32[]{:S(2)}, u32[]{:S(2)}) collective-permute-start(bf16[128,256]{1,0:T(8,128)(2,1)S(1)} %add_convert_fusion.5), channel_id=1, source_target_pairs={{0,2},{1,3},{2,0},{3,1},{4,6},{5,7},{6,4},{7,5},{8,10},{9,11},{10,... | collective-permute-start | bytes 196616 | tf_op jit(solution)/shard_map/ppermute | solution.py:193
  36.8 2.0 %collective-permute-done.19 = bf16[144,256]{1,0:T(8,128)(2,1)S(1)} collective-permute-done((bf16[144,256]{1,0:T(8,128)(2,1)S(1)}, bf16[144,256]{1,0:T(8,128)(2,1)S(1)}, u32[]{:S(2)}, u32[]{:S(2)}) %collective-permute-start.19) | collective-permute-done | bytes 73760 | tf_op jit(solution)/shard_map/ppermute | solution.py:193
  38.8 1.3 %collective-permute-start.20 = (bf16[144,256]{1,0:T(8,128)(2,1)S(1)}, bf16[144,256]{1,0:T(8,128)(2,1)S(1)}, u32[]{:S(2)}, u32[]{:S(2)}) collective-permute-start(bf16[144,256]{1,0:T(8,128)(2,1)S(1)} %add_convert_fusion.1), channel_id=1, source_target_pairs={{0,4},{1,5},{2,6},{3,7},{4,0},{5,1},{6,2},{7,3},{8,12},{9,13},{10,... | collective-permute-start | bytes 221192 | tf_op jit(solution)/shard_map/ppermute | solution.py:193
  40.0 0.0 collective-permute-done.24
  40.1 1.5 %collective-permute-start.25 = (bf16[128,256]{1,0:T(8,128)(2,1)S(1)}, bf16[128,256]{1,0:T(8,128)(2,1)S(1)}, u32[]{:S(2)}, u32[]{:S(2)}) collective-permute-start(bf16[128,256]{1,0:T(8,128)(2,1)S(1)} %add_convert_fusion.4), channel_id=1, source_target_pairs={{0,4},{1,5},{2,6},{3,7},{4,0},{5,1},{6,2},{7,3},{8,12},{9,13},{10,... | collective-permute-start | bytes 196616 | tf_op jit(solution)/shard_map/ppermute | solution.py:193
  41.5 2.3 %collective-permute-done.20 = bf16[144,256]{1,0:T(8,128)(2,1)S(1)} collective-permute-done((bf16[144,256]{1,0:T(8,128)(2,1)S(1)}, bf16[144,256]{1,0:T(8,128)(2,1)S(1)}, u32[]{:S(2)}, u32[]{:S(2)}) %collective-permute-start.20) | collective-permute-done | bytes 73760 | tf_op jit(solution)/shard_map/ppermute | solution.py:193
  43.8 2.2 %collective-permute-start.21 = (bf16[144,256]{1,0:T(8,128)(2,1)S(1)}, bf16[144,256]{1,0:T(8,128)(2,1)S(1)}, u32[]{:S(2)}, u32[]{:S(2)}) collective-permute-start(bf16[144,256]{1,0:T(8,128)(2,1)S(1)} %add_convert_fusion), channel_id=1, source_target_pairs={{0,8},{1,9},{2,10},{3,11},{4,12},{5,13},{6,14},{7,15},{8,0},{9,1},... | collective-permute-start | bytes 221192 | tf_op jit(solution)/shard_map/ppermute | solution.py:193
  46.0 0.0 collective-permute-done.25
  46.1 1.3 %collective-permute-start.26 = (bf16[128,256]{1,0:T(8,128)(2,1)S(1)}, bf16[128,256]{1,0:T(8,128)(2,1)S(1)}, u32[]{:S(2)}, u32[]{:S(2)}) collective-permute-start(bf16[128,256]{1,0:T(8,128)(2,1)S(1)} %add_convert_fusion.3), channel_id=1, source_target_pairs={{0,8},{1,9},{2,10},{3,11},{4,12},{5,13},{6,14},{7,15},{8,0},{9,1},... | collective-permute-start | bytes 196616 | tf_op jit(solution)/shard_map/ppermute | solution.py:193
  47.4 3.2 %collective-permute-done.21 = bf16[144,256]{1,0:T(8,128)(2,1)S(1)} collective-permute-done((bf16[144,256]{1,0:T(8,128)(2,1)S(1)}, bf16[144,256]{1,0:T(8,128)(2,1)S(1)}, u32[]{:S(2)}, u32[]{:S(2)}) %collective-permute-start.21) | collective-permute-done | bytes 73760 | tf_op jit(solution)/shard_map/ppermute | solution.py:193
  50.6 0.1 collective-permute-start.22
  50.7 0.6 %collective-permute-done.26 = bf16[128,256]{1,0:T(8,128)(2,1)S(1)} collective-permute-done((bf16[128,256]{1,0:T(8,128)(2,1)S(1)}, bf16[128,256]{1,0:T(8,128)(2,1)S(1)}, u32[]{:S(2)}, u32[]{:S(2)}) %collective-permute-start.26) | collective-permute-done | bytes 65568 | tf_op jit(solution)/shard_map/ppermute | solution.py:193
  51.3 0.1 collective-permute-start.27
  51.4 0.8 %column_two.1 = bf16[256,256]{1,0:T(8,128)(2,1)} custom-call(f32[256,256]{1,0:T(8,128)S(1)} %get-tuple-element.82.own, f32[256,256]{1,0:T(8,128)S(1)} %collective-permute-done.28.received, f32[2,256]{1,0:T(2,128)S(1)} %get-tuple-element.62.weights, f32[256,256]{1,0:T(8,128)S(1)} %get-tuple-element.84.carried), custom_call_target="tpu_custom_call" | custom-call | bytes 788480 | tf_op jit(solution)/shard_map/column_two/pallas_call | solution.py:32
  52.2 0.0 collective-permute-done.22.pack_b
  52.2 0.5 collective-permute-done.27.cross_b
  52.7 1.3 %last.1 = (f32[256,256]{1,0:T(8,128)}, f32[256,256]{1,0:T(8,128)}, f32[256,256]{1,0:T(8,128)}) custom-call(f32[144,256]{1,0:T(8,128)S(1)} %convert_add_fusion.pack_a, f32[144,256]{1,0:T(8,128)S(1)} %collective-permute-done.22.pack_b, f32[128,256]{1,0:T(8,128)S(1)} %convert_add_fusion.1.cross_a, f32[128,256]{1,0:T(8,128)S(1)} %collective-permute-done.27.cross_b, ...), custom_call_target="tpu_custom_call" | custom-call | bytes 1212416 | tf_op jit(solution)/shard_map/last/pallas_call | solution.py:32
  (19 shorter events, 0.2 us)
Async XLA Ops:
  2.4 25.3 %collective-permute-start = (bf16[256,4096]{1,0:T(8,128)(2,1)S(1)}, bf16[256,4096]{1,0:T(8,128)(2,1)S(1)}, u32[]{:S(2)}, u32[]{:S(2)}) collective-permute-start(bf16[256,4096]{1,0:T(8,128)(2,1)S(1)} %get-tuple-element.46.window), channel_id=1, source_target_pairs={{0,1},{1,0},{2,3},{3,2},{4,5},{5,4},{6,7},{7,6},{8,9},{9,8},{10,11... | collective-permute-start | bytes 6291464 | tf_op jit(solution)/shard_map/ppermute | solution.py:193
  3.0 6.7 %collective-permute-start.7 = (bf16[256,256]{1,0:T(8,128)(2,1)S(1)}, bf16[256,256]{1,0:T(8,128)(2,1)S(1)}, u32[]{:S(2)}, u32[]{:S(2)}) collective-permute-start(bf16[256,256]{1,0:T(8,128)(2,1)S(1)} %get-tuple-element.65.m_two.rest_0_.mine), channel_id=1, source_target_pairs={{4,0},{5,1},{8,4},{9,5},{12,8},{13,9},{14,12},{15,13},{10,14},{11,... | collective-permute-start | bytes 393224 | tf_op jit(solution)/shard_map/ppermute | solution.py:193
  5.5 6.3 %collective-permute-start.1 = (bf16[256,256]{1,0:T(8,128)(2,1)S(1)}, bf16[256,256]{1,0:T(8,128)(2,1)S(1)}, u32[]{:S(2)}, u32[]{:S(2)}) collective-permute-start(bf16[256,256]{1,0:T(8,128)(2,1)S(1)} %get-tuple-element.49.rest_0_.mine), channel_id=1, source_target_pairs={{0,4},{1,5},{4,8},{5,9},{8,12},{9,13},{12,14},{13,15},{14,10},{15,... | collective-permute-start | bytes 393224 | tf_op jit(solution)/shard_map/ppermute | solution.py:193
  5.7 8.7 %collective-permute-start.10 = (bf16[256,256]{1,0:T(8,128)(2,1)S(1)}, bf16[256,256]{1,0:T(8,128)(2,1)S(1)}, u32[]{:S(2)}, u32[]{:S(2)}) collective-permute-start(bf16[256,256]{1,0:T(8,128)(2,1)S(1)} %get-tuple-element.65.m_two.rest_0_.mine), channel_id=1, source_target_pairs={{0,4},{1,5},{4,8},{5,9},{8,12},{9,13},{12,14},{13,15},{14,10},{15,... | collective-permute-start | bytes 393224 | tf_op jit(solution)/shard_map/ppermute | solution.py:193
  7.6 6.9 %collective-permute-start.4 = (bf16[256,256]{1,0:T(8,128)(2,1)S(1)}, bf16[256,256]{1,0:T(8,128)(2,1)S(1)}, u32[]{:S(2)}, u32[]{:S(2)}) collective-permute-start(bf16[256,256]{1,0:T(8,128)(2,1)S(1)} %get-tuple-element.49.rest_0_.mine), channel_id=1, source_target_pairs={{4,0},{5,1},{8,4},{9,5},{12,8},{13,9},{14,12},{15,13},{10,14},{11,... | collective-permute-start | bytes 393224 | tf_op jit(solution)/shard_map/ppermute | solution.py:193
  9.7 6.7 %collective-permute-start.8 = (bf16[256,256]{1,0:T(8,128)(2,1)S(1)}, bf16[256,256]{1,0:T(8,128)(2,1)S(1)}, u32[]{:S(2)}, u32[]{:S(2)}) collective-permute-start(bf16[256,256]{1,0:T(8,128)(2,1)S(1)} %collective-permute-done.7.rest_2_), channel_id=1, source_target_pairs={{4,0},{5,1},{8,4},{9,5},{12,8},{13,9},{14,12},{15,13},{10,14},{11,... | collective-permute-start | bytes 393224 | tf_op jit(solution)/shard_map/ppermute | solution.py:193
  11.9 6.1 %collective-permute-start.2 = (bf16[256,256]{1,0:T(8,128)(2,1)S(1)}, bf16[256,256]{1,0:T(8,128)(2,1)S(1)}, u32[]{:S(2)}, u32[]{:S(2)}) collective-permute-start(bf16[256,256]{1,0:T(8,128)(2,1)S(1)} %collective-permute-done.1.rest_1_), channel_id=1, source_target_pairs={{0,4},{1,5},{4,8},{5,9},{8,12},{9,13},{12,14},{13,15},{14,10},{15,... | collective-permute-start | bytes 393224 | tf_op jit(solution)/shard_map/ppermute | solution.py:193
  14.4 6.3 %collective-permute-start.11 = (bf16[256,256]{1,0:T(8,128)(2,1)S(1)}, bf16[256,256]{1,0:T(8,128)(2,1)S(1)}, u32[]{:S(2)}, u32[]{:S(2)}) collective-permute-start(bf16[256,256]{1,0:T(8,128)(2,1)S(1)} %collective-permute-done.10.rest_1_), channel_id=1, source_target_pairs={{0,4},{1,5},{4,8},{5,9},{8,12},{9,13},{12,14},{13,15},{14,10},{15,... | collective-permute-start | bytes 393224 | tf_op jit(solution)/shard_map/ppermute | solution.py:193
  14.5 6.2 %collective-permute-start.5 = (bf16[256,256]{1,0:T(8,128)(2,1)S(1)}, bf16[256,256]{1,0:T(8,128)(2,1)S(1)}, u32[]{:S(2)}, u32[]{:S(2)}) collective-permute-start(bf16[256,256]{1,0:T(8,128)(2,1)S(1)} %collective-permute-done.4.rest_2_), channel_id=1, source_target_pairs={{4,0},{5,1},{8,4},{9,5},{12,8},{13,9},{14,12},{15,13},{10,14},{11,... | collective-permute-start | bytes 393224 | tf_op jit(solution)/shard_map/ppermute | solution.py:193
  16.4 6.3 %collective-permute-start.9 = (bf16[256,256]{1,0:T(8,128)(2,1)S(1)}, bf16[256,256]{1,0:T(8,128)(2,1)S(1)}, u32[]{:S(2)}, u32[]{:S(2)}) collective-permute-start(bf16[256,256]{1,0:T(8,128)(2,1)S(1)} %collective-permute-done.8.rest_1_), channel_id=1, source_target_pairs={{4,0},{5,1},{8,4},{9,5},{12,8},{13,9},{14,12},{15,13},{10,14},{11,... | collective-permute-start | bytes 393224 | tf_op jit(solution)/shard_map/ppermute | solution.py:193
  18.0 6.0 %collective-permute-start.3 = (bf16[256,256]{1,0:T(8,128)(2,1)S(1)}, bf16[256,256]{1,0:T(8,128)(2,1)S(1)}, u32[]{:S(2)}, u32[]{:S(2)}) collective-permute-start(bf16[256,256]{1,0:T(8,128)(2,1)S(1)} %collective-permute-done.2.rest_0_), channel_id=1, source_target_pairs={{0,4},{1,5},{4,8},{5,9},{8,12},{9,13},{12,14},{13,15},{14,10},{15,... | collective-permute-start | bytes 393224 | tf_op jit(solution)/shard_map/ppermute | solution.py:193
  20.7 5.0 %collective-permute-start.12 = (bf16[256,256]{1,0:T(8,128)(2,1)S(1)}, bf16[256,256]{1,0:T(8,128)(2,1)S(1)}, u32[]{:S(2)}, u32[]{:S(2)}) collective-permute-start(bf16[256,256]{1,0:T(8,128)(2,1)S(1)} %collective-permute-done.11.rest_0_), channel_id=1, source_target_pairs={{0,4},{1,5},{4,8},{5,9},{8,12},{9,13},{12,14},{13,15},{14,10},{15,... | collective-permute-start | bytes 393224 | tf_op jit(solution)/shard_map/ppermute | solution.py:193
  20.8 5.0 %collective-permute-start.6 = (bf16[256,256]{1,0:T(8,128)(2,1)S(1)}, bf16[256,256]{1,0:T(8,128)(2,1)S(1)}, u32[]{:S(2)}, u32[]{:S(2)}) collective-permute-start(bf16[256,256]{1,0:T(8,128)(2,1)S(1)} %collective-permute-done.5.rest_1_), channel_id=1, source_target_pairs={{4,0},{5,1},{8,4},{9,5},{12,8},{13,9},{14,12},{15,13},{10,14},{11,... | collective-permute-start | bytes 393224 | tf_op jit(solution)/shard_map/ppermute | solution.py:193
  22.8 5.8 %collective-permute-start.13 = (bf16[256,256]{1,0:T(8,128)(2,1)S(1)}, bf16[256,256]{1,0:T(8,128)(2,1)S(1)}, u32[]{:S(2)}, u32[]{:S(2)}) collective-permute-start(bf16[256,256]{1,0:T(8,128)(2,1)S(1)} %get-tuple-element.49.rest_0_.mine), channel_id=1, source_target_pairs={{0,1},{1,0},{2,3},{3,2},{4,5},{5,4},{6,7},{7,6},{8,9},{9,8},{10,11... | collective-permute-start | bytes 393224 | tf_op jit(solution)/shard_map/ppermute | solution.py:193
  24.0 5.0 %collective-permute-start.14 = (bf16[256,256]{1,0:T(8,128)(2,1)S(1)}, bf16[256,256]{1,0:T(8,128)(2,1)S(1)}, u32[]{:S(2)}, u32[]{:S(2)}) collective-permute-start(bf16[256,256]{1,0:T(8,128)(2,1)S(1)} %collective-permute-done.3.rest_2_), channel_id=1, source_target_pairs={{0,4},{1,5},{4,8},{5,9},{8,12},{9,13},{12,14},{13,15},{14,10},{15,... | collective-permute-start | bytes 393224 | tf_op jit(solution)/shard_map/ppermute | solution.py:193
  25.7 4.8 %collective-permute-start.16 = (bf16[256,256]{1,0:T(8,128)(2,1)S(1)}, bf16[256,256]{1,0:T(8,128)(2,1)S(1)}, u32[]{:S(2)}, u32[]{:S(2)}) collective-permute-start(bf16[256,256]{1,0:T(8,128)(2,1)S(1)} %get-tuple-element.65.m_two.rest_0_.mine), channel_id=1, source_target_pairs={{0,1},{1,0},{2,3},{3,2},{4,5},{5,4},{6,7},{7,6},{8,9},{9,8},{10,11... | collective-permute-start | bytes 393224 | tf_op jit(solution)/shard_map/ppermute | solution.py:193
  25.8 5.9 %collective-permute-start.17 = (bf16[256,256]{1,0:T(8,128)(2,1)S(1)}, bf16[256,256]{1,0:T(8,128)(2,1)S(1)}, u32[]{:S(2)}, u32[]{:S(2)}) collective-permute-start(bf16[256,256]{1,0:T(8,128)(2,1)S(1)} %collective-permute-done.9.rest_3_), channel_id=1, source_target_pairs={{4,0},{5,1},{8,4},{9,5},{12,8},{13,9},{14,12},{15,13},{10,14},{11,... | collective-permute-start | bytes 393224 | tf_op jit(solution)/shard_map/ppermute | solution.py:193
  29.6 3.3 %collective-permute-start.15 = (f32[256,256]{1,0:T(8,128)S(1)}, f32[256,256]{1,0:T(8,128)S(1)}, u32[]{:S(2)}, u32[]{:S(2)}) collective-permute-start(f32[256,256]{1,0:T(8,128)S(1)} %get-tuple-element.61), channel_id=1, source_target_pairs={{0,1},{1,0},{2,3},{3,2},{4,5},{5,4},{6,7},{7,6},{8,9},{9,8},{10,11... | collective-permute-start | bytes 786440 | tf_op jit(solution)/shard_map/ppermute | solution.py:193
  31.6 1.3 %copy-start = (bf16[256,256]{1,0:T(8,128)(2,1)S(1)}, bf16[256,256]{1,0:T(8,128)(2,1)}, u32[]{:S(2)}) copy-start(bf16[256,256]{1,0:T(8,128)(2,1)} %cross.3) | copy-start | bytes 393220
  32.2 20.5 %copy-start.1 = (f32[256,256]{1,0:T(8,128)S(1)}, f32[256,256]{1,0:T(8,128)}, u32[]{:S(2)}) copy-start(f32[256,256]{1,0:T(8,128)} %diag_one.1) | copy-start | bytes 786436
  32.2 20.5 %copy-start.2 = (f32[256,256]{1,0:T(8,128)S(1)}, f32[256,256]{1,0:T(8,128)}, u32[]{:S(2)}) copy-start(f32[256,256]{1,0:T(8,128)} %diag_two.1) | copy-start | bytes 786436
  32.3 1.5 %collective-permute-start.18 = (f32[144,256]{1,0:T(8,128)S(1)}, f32[144,256]{1,0:T(8,128)S(1)}, u32[]{:S(2)}, u32[]{:S(2)}) collective-permute-start(f32[144,256]{1,0:T(8,128)S(1)} %get-tuple-element.78), channel_id=1, source_target_pairs={{0,1},{1,0},{2,3},{3,2},{4,5},{5,4},{6,7},{7,6},{8,9},{9,8},{10,11... | collective-permute-start | bytes 442376 | tf_op jit(solution)/shard_map/ppermute | solution.py:193
  32.4 19.0 %collective-permute-start.28 = (f32[256,256]{1,0:T(8,128)S(1)}, f32[256,256]{1,0:T(8,128)S(1)}, u32[]{:S(2)}, u32[]{:S(2)}) collective-permute-start(f32[256,256]{1,0:T(8,128)S(1)} %get-tuple-element.83), channel_id=1, source_target_pairs={{0,1},{1,0},{2,3},{3,2},{4,5},{5,4},{6,7},{7,6},{8,9},{9,8},{10,11... | collective-permute-start | bytes 786440 | tf_op jit(solution)/shard_map/ppermute | solution.py:193
  33.8 1.8 %collective-permute-start.23 = (f32[128,256]{1,0:T(8,128)S(1)}, f32[128,256]{1,0:T(8,128)S(1)}, u32[]{:S(2)}, u32[]{:S(2)}) collective-permute-start(f32[128,256]{1,0:T(8,128)S(1)} %get-tuple-element.80), channel_id=1, source_target_pairs={{0,1},{1,0},{2,3},{3,2},{4,5},{5,4},{6,7},{7,6},{8,9},{9,8},{10,11... | collective-permute-start | bytes 393224 | tf_op jit(solution)/shard_map/ppermute | solution.py:193
  33.9 4.9 %collective-permute-start.19 = (bf16[144,256]{1,0:T(8,128)(2,1)S(1)}, bf16[144,256]{1,0:T(8,128)(2,1)S(1)}, u32[]{:S(2)}, u32[]{:S(2)}) collective-permute-start(bf16[144,256]{1,0:T(8,128)(2,1)S(1)} %add_convert_fusion.2), channel_id=1, source_target_pairs={{0,2},{1,3},{2,0},{3,1},{4,6},{5,7},{6,4},{7,5},{8,10},{9,11},{10,... | collective-permute-start | bytes 221192 | tf_op jit(solution)/shard_map/ppermute | solution.py:193
  35.5 4.5 %collective-permute-start.24 = (bf16[128,256]{1,0:T(8,128)(2,1)S(1)}, bf16[128,256]{1,0:T(8,128)(2,1)S(1)}, u32[]{:S(2)}, u32[]{:S(2)}) collective-permute-start(bf16[128,256]{1,0:T(8,128)(2,1)S(1)} %add_convert_fusion.5), channel_id=1, source_target_pairs={{0,2},{1,3},{2,0},{3,1},{4,6},{5,7},{6,4},{7,5},{8,10},{9,11},{10,... | collective-permute-start | bytes 196616 | tf_op jit(solution)/shard_map/ppermute | solution.py:193
  38.8 5.0 %collective-permute-start.20 = (bf16[144,256]{1,0:T(8,128)(2,1)S(1)}, bf16[144,256]{1,0:T(8,128)(2,1)S(1)}, u32[]{:S(2)}, u32[]{:S(2)}) collective-permute-start(bf16[144,256]{1,0:T(8,128)(2,1)S(1)} %add_convert_fusion.1), channel_id=1, source_target_pairs={{0,4},{1,5},{2,6},{3,7},{4,0},{5,1},{6,2},{7,3},{8,12},{9,13},{10,... | collective-permute-start | bytes 221192 | tf_op jit(solution)/shard_map/ppermute | solution.py:193
  40.1 6.0 %collective-permute-start.25 = (bf16[128,256]{1,0:T(8,128)(2,1)S(1)}, bf16[128,256]{1,0:T(8,128)(2,1)S(1)}, u32[]{:S(2)}, u32[]{:S(2)}) collective-permute-start(bf16[128,256]{1,0:T(8,128)(2,1)S(1)} %add_convert_fusion.4), channel_id=1, source_target_pairs={{0,4},{1,5},{2,6},{3,7},{4,0},{5,1},{6,2},{7,3},{8,12},{9,13},{10,... | collective-permute-start | bytes 196616 | tf_op jit(solution)/shard_map/ppermute | solution.py:193
  43.8 6.8 %collective-permute-start.21 = (bf16[144,256]{1,0:T(8,128)(2,1)S(1)}, bf16[144,256]{1,0:T(8,128)(2,1)S(1)}, u32[]{:S(2)}, u32[]{:S(2)}) collective-permute-start(bf16[144,256]{1,0:T(8,128)(2,1)S(1)} %add_convert_fusion), channel_id=1, source_target_pairs={{0,8},{1,9},{2,10},{3,11},{4,12},{5,13},{6,14},{7,15},{8,0},{9,1},... | collective-permute-start | bytes 221192 | tf_op jit(solution)/shard_map/ppermute | solution.py:193
  46.1 5.2 %collective-permute-start.26 = (bf16[128,256]{1,0:T(8,128)(2,1)S(1)}, bf16[128,256]{1,0:T(8,128)(2,1)S(1)}, u32[]{:S(2)}, u32[]{:S(2)}) collective-permute-start(bf16[128,256]{1,0:T(8,128)(2,1)S(1)} %add_convert_fusion.3), channel_id=1, source_target_pairs={{0,8},{1,9},{2,10},{3,11},{4,12},{5,13},{6,14},{7,15},{8,0},{9,1},... | collective-permute-start | bytes 196616 | tf_op jit(solution)/shard_map/ppermute | solution.py:193
  50.6 1.7 %collective-permute-start.22 = (f32[144,256]{1,0:T(8,128)S(1)}, f32[144,256]{1,0:T(8,128)S(1)}, u32[]{:S(2)}, u32[]{:S(2)}) collective-permute-start(f32[144,256]{1,0:T(8,128)S(1)} %convert_add_fusion.pack_a), channel_id=1, source_target_pairs={{0,1},{1,0},{2,3},{3,2},{4,5},{5,4},{6,7},{7,6},{8,9},{9,8},{10,11... | collective-permute-start | bytes 442376 | tf_op jit(solution)/shard_map/ppermute | solution.py:193
  51.3 1.4 %collective-permute-start.27 = (f32[128,256]{1,0:T(8,128)S(1)}, f32[128,256]{1,0:T(8,128)S(1)}, u32[]{:S(2)}, u32[]{:S(2)}) collective-permute-start(f32[128,256]{1,0:T(8,128)S(1)} %convert_add_fusion.1.cross_a), channel_id=1, source_target_pairs={{0,1},{1,0},{2,3},{3,2},{4,5},{5,4},{6,7},{7,6},{8,9},{9,8},{10,11... | collective-permute-start | bytes 393224 | tf_op jit(solution)/shard_map/ppermute | solution.py:193

commit v4 on v3

v4 whole, which is shorter than its diff:
```python
import functools

import jax
import jax.numpy as jnp
from jax import lax
from jax.experimental import pallas as pl
from jax.experimental.pallas import tpu as pltpu
from jax.sharding import PartitionSpec as P

F32, BF16 = jnp.float32, jnp.bfloat16
AXIS = "prow"
VMEM = pl.BlockSpec(memory_space=pltpu.VMEM)
SMEM = pl.BlockSpec(memory_space=pltpu.SMEM)
HBM = pl.BlockSpec(memory_space=pltpu.HBM)


def dot(left, right):
    return jnp.dot(left, right, preferred_element_type=F32)


def dot_t(left, right):
    return lax.dot_general(left, right, (((0,), (0,)), ((), ())), preferred_element_type=F32)


def halves(x):
    high = x.astype(BF16)
    return high, (x - high.astype(F32)).astype(BF16)


def call(body, name, outs, args, n_smem=0, flops=0, aliases=None, specs=None, scratch=()):
    size = sum(a.size * a.dtype.itemsize for a in args)
    return pl.pallas_call(
        body,
        name=name,
        out_shape=tuple(jax.ShapeDtypeStruct(s, d) for s, d in outs),
        in_specs=specs or [SMEM] * n_smem + [VMEM] * (len(args) - n_smem),
        out_specs=tuple(VMEM for _ in outs),
        input_output_aliases=aliases or {},
        scratch_shapes=scratch,
        compiler_params=pltpu.CompilerParams(vmem_limit_bytes=16 << 20),
        cost_estimate=pl.CostEstimate(flops=flops, bytes_accessed=size, transcendentals=0),
    )(*args)


def chip_of(position, chips):
    return jnp.where(position < chips // 2, 2 * position, 2 * (chips - 1 - position) + 1)


def chip_at(chip, offset, chips):
    position = jnp.where(chip % 2 == 0, chip // 2, chips - 1 - chip // 2)
    return chip_of((position + offset + chips) % chips, chips)


def in_hbm(x):
    return pltpu.with_memory_space_constraint(x, pltpu.HBM)


def diagonal_of(weight):
    n = weight.shape[1]
    on = lax.broadcasted_iota(jnp.int32, (n, n), 0) == lax.broadcasted_iota(jnp.int32, (n, n), 1)
    return jnp.where(on, jnp.broadcast_to(weight, (n, n)), 0.0).astype(BF16)


def mask_body(table, rows, one, two, window, m_one, m_two, stack, weights, window_v, table_v, rows_v, one_v, two_v, sems):
    moves = (table, table_v), (rows, rows_v), (one, one_v), (two, two_v), (window, window_v)
    copies = [pltpu.make_async_copy(src, dst, sems.at[i]) for i, (src, dst) in enumerate(moves)]
    for copy in copies:
        copy.start()
    copies[0].wait()
    copies[1].wait()
    index = rows_v[...]
    n = one.shape[0]
    for which, panel, masked in ((0, one_v, m_one), (1, two_v, m_two)):
        weight = jnp.zeros(index.shape, F32)
        for s in range(table.shape[1]):
            weight = jnp.where(index == s, table_v[which, s].astype(F32), weight)
        weights[which : which + 1] = weight
        chosen = diagonal_of(weight)
        copies[2 + which].wait()
        value = dot(chosen, panel[...]).astype(BF16)
        masked[...] = value
        stack[which * n : (which + 1) * n] = value
    stack[2 * n :] = dot(diagonal_of(weights[0:1]), m_two[...]).astype(BF16)
    copies[4].wait()


def product(offset, window, swapped, piece):
    n = window.shape[0]
    me = lax.axis_index(AXIS)
    block = 2 * chip_at(me // 2, offset, window.shape[1] // (2 * n)) + me % 2
    columns = pl.ds(pl.multiple_of(block * n, n), n)
    value = piece[...]
    return dot(window[:, columns], value), dot(swapped[:, columns], value)


def plus(left, right, scale=1.0):
    return tuple(a + scale * b for a, b in zip(left, right, strict=True))


def add_products(total, chosen, window, swapped):
    for offset, piece in chosen:
        total = plus(total, product(offset, window, swapped, piece))
    return total


def early_body(window, swapped, one, up, down, two, back, *outs):
    zero = (jnp.zeros(one.shape, F32),) * 2
    own = product(0, window, swapped, one)
    side = plus(add_products(zero, up, window, swapped), own, 0.5)
    whole = plus(add_products(side, down, window, swapped), own, 0.5)
    own = product(0, window, swapped, two)
    side_two = plus(add_products(zero, back, window, swapped), own, 0.5)
    whole_two = plus(side_two, own, 0.5)
    for out, value in zip(outs, (*side, *whole, *side_two, *whole_two), strict=True):
        out[...] = value


def gram(stack, sibling, which, images):
    (a, b), (c, d) = halves(images[0]), halves(images[1])
    n = images[0].shape[0]
    mine, sibling = (x[which * n : (which + 1) * n] for x in (stack, sibling))
    return (dot_t(mine, a) + dot_t(sibling, c)) + (dot_t(mine, b) + dot_t(sibling, d))


def late_body(steps, window, swapped, *rest):
    sums, (stack, sibling, one, two), outs, (keep, send) = rest[:8], rest[8:12], rest[12:16], rest[16:]
    sums = [(sums[i][...], sums[i + 1][...]) for i in range(0, 8, 2)]
    far = product(-steps, window, swapped, one)
    image_one = plus(sums[1], far)
    first = gram(stack, sibling, 0, plus(sums[0], far, 0.5))
    far = product(steps, window, swapped, two)
    image_two = plus(sums[3], far)
    second = gram(stack, sibling, 1, plus(sums[2], far, 0.5))
    cross = -gram(stack, sibling, 2, image_one)
    for out, value in zip(outs, (*image_one, *image_two), strict=True):
        out[...] = value

    n = first.shape[0]
    half = n // 2
    row = lax.broadcasted_iota(jnp.int32, (n, n), 0)
    col = lax.broadcasted_iota(jnp.int32, (n, n), 1)
    second = second + second.T
    both = jnp.where(row <= col, first + first.T, second)
    diagonal = jnp.sum(jnp.where(row == col, second, 0.0), axis=0, keepdims=True)
    diagonal = jnp.broadcast_to(diagonal, (keep.shape[0] - n, n))
    low = lax.axis_index(AXIS) % 2 == 0
    for out, mine in ((keep, low), (send, jnp.logical_not(low))):
        out[:half] = jnp.where(mine, both[:half], both[half:])
        out[half:-half] = diagonal
        out[-half:] = jnp.where(mine, cross[:half], cross[half:])


def rest_body(window, swapped, own_in, other_in, up, own, other):
    own[...], other[...] = add_products((own_in[...], other_in[...]), up, window, swapped)


def row_weights(weights, which):
    n = weights.shape[1]
    return dot(diagonal_of(weights[which : which + 1]), jnp.ones((n, n), BF16))


def columns_body(own_one, received_one, own_two, received_two, weights, cross, column_one, column_two):
    rounded = (-(row_weights(weights, 0) * (own_one[...] + received_one[...]))).astype(BF16)
    column_one[...] = rounded
    image = own_two[...] + received_two[...]
    column_two[...] = (-(row_weights(weights, 1) * (image + dot(rounded, cross[...])))).astype(BF16)


def last_body(pack_a, pack_b, cross_a, cross_b, cross, diag_one, diag_two, block_one, edge, block_two):
    n = cross.shape[0]
    half = n // 2
    first = lax.axis_index(AXIS) % 2 == 0

    def whole(a, b):
        return jnp.concatenate([jnp.where(first, a, b), jnp.where(first, b, a)], axis=0)

    row = lax.broadcasted_iota(jnp.int32, (n, n), 0)
    col = lax.broadcasted_iota(jnp.int32, (n, n), 1)
    packed = whole(pack_a[:half], pack_b[:half])
    turned = packed.T
    diagonal = jnp.where(first, pack_a[half : half + 1], pack_b[half : half + 1])
    s_one = jnp.where(row <= col, packed, turned)
    s_two = jnp.where(row > col, packed, turned)
    s_two = jnp.where(row == col, jnp.broadcast_to(diagonal, (n, n)), s_two)
    cross_sum = whole(cross_a[...], cross_b[...])
    c = cross[...]
    one = diag_one[...] + s_one
    block_one[...] = one
    a, b = halves(one)
    out = -(cross_sum.T + (dot(a, c) + dot(b, c)))
    edge[...] = out
    a, b = halves(out)
    d, e = halves(cross_sum)
    block_two[...] = diag_two[...] + s_two + (dot(d, c) + dot(e, c)) - (dot_t(c, a) + dot_t(c, b))


def local(
    inverse_window, panel_one, panel_two, cross_block, diag_one, diag_two, row_super, struct_mask, *, size
):
    chips = size // 2
    rows, width = panel_one.shape
    half = width // 2
    ring = [2 * r if r < chips // 2 else 2 * (chips - 1 - r) + 1 for r in range(chips)]
    ahead = [(2 * ring[r] + c, 2 * ring[(r + 1) % chips] + c) for r in range(chips) for c in (0, 1)]
    back = [(b, a) for a, b in ahead]
    flip = [[(i, i ^ (1 << b)) for i in range(size)] for b in range(size.bit_length() - 1)]

    def send(x, perm):
        return lax.ppermute(x, AXIS, perm)

    square = ((rows, width), F32)
    tile = ((rows, width), BF16)
    m_one, m_two, stack, weights, window = call(
        mask_body,
        "mask",
        (tile, tile, ((3 * rows, width), BF16), ((2, rows), F32), (inverse_window.shape, BF16)),
        tuple(map(in_hbm, (struct_mask, row_super.reshape(1, -1), panel_one, panel_two, inverse_window))),
        specs=[HBM] * 5,
        scratch=[
            pltpu.SMEM(struct_mask.shape, jnp.int32),
            pltpu.VMEM((1, rows), jnp.int32),
            pltpu.VMEM((rows, width), BF16),
            pltpu.VMEM((rows, width), BF16),
            pltpu.SemaphoreType.DMA((5,)),
        ],
    )

    steps = chips // 2
    one_up, one_down, two_up, two_down = [m_one], [m_one], [m_two], [m_two]
    for k in range(1, steps):
        one_up.append(send(one_up[-1], ahead))
        two_down.append(send(two_down[-1], back))
        one_down.append(send(one_down[-1], back))
        if k < steps - 1:
            two_up.append(send(two_up[-1], ahead))
    one_far = send(one_up[-1], ahead)
    two_far = send(two_down[-1], back)
    swapped = send(window, flip[0])
    sibling = send(stack, flip[0])

    def early_refs(*refs):
        inputs, outs = refs[: len(early_in)], refs[len(early_in) :]
        fixed, pieces = inputs[:2], inputs[2:]
        n = steps - 1
        one, up, down = pieces[0], pieces[1 : 1 + n], pieces[1 + n : 1 + 2 * n]
        two, behind = pieces[1 + 2 * n], pieces[2 + 2 * n :]
        early_body(
            *fixed,
            one,
            [(-k, p) for k, p in enumerate(up, 1)],
            [(k, p) for k, p in enumerate(down, 1)],
            two,
            [(k, p) for k, p in enumerate(behind, 1)],
            *outs,
        )

    one_up[-1], *_ = lax.optimization_barrier((one_up[-1], *two_up))
    early_in = (
        *(window, swapped),
        *one_up,
        *one_down[1:],
        *two_down,
    )
    block_flops = 4 * rows * width * width
    early = call(early_refs, "early", (square,) * 8, early_in, flops=block_flops * (3 * steps + 1))
    tall = ((width + 16, width), F32)
    own_one, other_one, own_two, other_two, keep, away = call(
        functools.partial(late_body, steps),
        "late",
        (square,) * 4 + (tall, tall),
        (window, swapped, *early, stack, sibling, one_far, two_far),
        flops=block_flops * 8,
    )
    value = keep + send(away, flip[0])
    value, last_up = lax.optimization_barrier((value, two_up[-1]))
    two_up.append(send(last_up, ahead))

    stages = []

    def summed(value):
        for perm in flip[1:]:
            value = value.astype(BF16)
            value = value.astype(F32) + send(value, perm).astype(F32)
            stages.append(value)
        return value

    pack_a = summed(value[:-half])
    cross_a = summed(value[-half:])
    pack_b, cross_b = send(pack_a, flip[0]), send(cross_a, flip[0])

    received_one = send(other_one, flip[0])
    def rest_refs(*refs):
        inputs, outs = refs[: len(rest_in)], refs[len(rest_in) :]
        rest_body(*inputs[:4], [(-k, p) for k, p in enumerate(inputs[4:], 1)], *outs)

    rest_in = (window, swapped, own_two, other_two, *two_up[1:])
    own_two, other_two = call(rest_refs, "rest", (square,) * 2, rest_in, flops=block_flops * (steps - 1))
    received_two = send(other_two, flip[0])
    column_one, column_two = call(
        columns_body,
        "columns",
        (tile, tile),
        (own_one, received_one, own_two, received_two, weights, cross_block),
    )
    pack_b, column_two = lax.optimization_barrier((pack_b, column_two))
    full = ((width, width), F32)
    block_one, edge_block, block_two = call(
        last_body,
        "last",
        (full, full, full),
        (pack_a, pack_b, cross_a, cross_b, cross_block, diag_one, diag_two),
    )
    return column_one, block_one, column_two, edge_block, block_two


def solution(mesh):
    return jax.shard_map(
        functools.partial(local, size=mesh.shape[AXIS]),
        mesh=mesh,
        in_specs=(
            P(("pole", "prow"), None),
            P(("pole", "prow"), None),
            P(("pole", "prow"), None),
            P("pole", None),
            P("pole", None),
            P("pole", None),
            P("prow"),
            P(),
        ),
        out_specs=(
            P(("pole", "prow"), None),
            P("pole", None),
            P(("pole", "prow"), None),
            P("pole", None),
            P("pole", None),
        ),
        check_vma=False,
    )
```

time: 54.3 us -> 52.7 us (0.971)
  waiting for transfers between devices: 19.5 us -> 17.2 us
  starting transfers between devices: 25.9 us -> 27.9 us
  Pallas kernels: 7.65 us -> 6.4 us
    ppermute x29 -> x27, waiting for transfers between devices: 19.5 us -> 17.2 us  [send(): return lax.ppermute(x, AXIS, perm)]
    ppermute x29 -> x27, starting transfers between devices: 25.9 us -> 27.9 us  [send(): return lax.ppermute(x, AXIS, perm)]
    pallas_call x11 -> x6, Pallas kernels: 7.65 us -> 6.4 us  [call(): pl.pallas_call(body, name=name, out_shape=tuple((jax.ShapeDtypeStruct(s,...]
  transfers between devices with their start and end apart: 29 -> 27, of which waited for: 12 -> 15; matrix products, arithmetic and copies ran while one was open for 0% -> 0% of each run, Pallas kernels for 8% -> 4%
where the time goes in v4:
time: 52.7 us; the launch traced here: 52.5 us
  starting transfers between devices  27.9 us (53%)
  waiting for transfers between devices  17.2 us (33%)
  Pallas kernels  6.4 us (12%)
  between operations  0.8 us (2%)
    ppermute x27, starting transfers between devices, send(): return lax.ppermute(x, AXIS, perm)  27.9 us
    ppermute x27, waiting for transfers between devices, send(): return lax.ppermute(x, AXIS, perm)  17.2 us
    pallas_call x6, Pallas kernels, call(): pl.pallas_call(body, name=name, out_shape=tuple((jax.ShapeDtypeStruct(s,...  6.4 us
  transfers between devices with their start and end apart: 27, of which 15 were waited for; matrix products, arithmetic and copies ran while one was open for 0% of the time, Pallas kernels for 4%

profile of v4, /device:TPU:0, one launch (start us, length us, event | category | flops | bytes accessed | tf_op | source)
XLA Modules:
  0.0 52.5 jit_solution(15323802183994200397)
XLA Ops:
  0.6 1.8 %mask.1 = (bf16[256,256]{1,0:T(8,128)(2,1)S(1)}, bf16[256,256]{1,0:T(8,128)(2,1)S(1)}, bf16[768,256]{1,0:T(8,128)(2,1)S(1)}, f32[2,256]{1,0:T(2,128)S(1)}, bf16[256,4096]{1,0:T(8,128)(2,1)S(1)}) custom-call(s32[2,16]{1,0:T(2,128)} %table.1, s32[1,256]{1,0:T(1,128)} %bitcast.1, bf16[256,256]{1,0:T(8,128)(2,1)} %one.1, bf16[256,256]{1,0:T(8,128)(2,1)} %two.1, ...), custom_call_target="tpu_custom_call" | custom-call | bytes 2360448 | tf_op jit(solution)/shard_map/mask/pallas_call | solution.py:32
  2.4 0.5 collective-permute-start
  3.0 2.6 %collective-permute-start.6 = (bf16[256,256]{1,0:T(8,128)(2,1)S(1)}, bf16[256,256]{1,0:T(8,128)(2,1)S(1)}, u32[]{:S(2)}, u32[]{:S(2)}) collective-permute-start(bf16[256,256]{1,0:T(8,128)(2,1)S(1)} %get-tuple-element.37.refs_2_), channel_id=1, source_target_pairs={{4,0},{5,1},{8,4},{9,5},{12,8},{13,9},{14,12},{15,13},{10,14},{11,... | collective-permute-start | bytes 393224 | tf_op jit(solution)/shard_map/ppermute | solution.py:209
  5.5 0.1 collective-permute-start.1
  5.7 1.9 %collective-permute-start.9 = (bf16[256,256]{1,0:T(8,128)(2,1)S(1)}, bf16[256,256]{1,0:T(8,128)(2,1)S(1)}, u32[]{:S(2)}, u32[]{:S(2)}) collective-permute-start(bf16[256,256]{1,0:T(8,128)(2,1)S(1)} %get-tuple-element.38.refs_9_), channel_id=1, source_target_pairs={{4,0},{5,1},{8,4},{9,5},{12,8},{13,9},{14,12},{15,13},{10,14},{11,... | collective-permute-start | bytes 393224 | tf_op jit(solution)/shard_map/ppermute | solution.py:209
  7.6 0.1 collective-permute-start.4
  7.7 2.2 %collective-permute-done.6.refs_6_ = bf16[256,256]{1,0:T(8,128)(2,1)S(1)} collective-permute-done((bf16[256,256]{1,0:T(8,128)(2,1)S(1)}, bf16[256,256]{1,0:T(8,128)(2,1)S(1)}, u32[]{:S(2)}, u32[]{:S(2)}) %collective-permute-start.6) | collective-permute-done | bytes 131104 | tf_op jit(solution)/shard_map/ppermute | solution.py:209
  10.0 1.9 %collective-permute-start.7 = (bf16[256,256]{1,0:T(8,128)(2,1)S(1)}, bf16[256,256]{1,0:T(8,128)(2,1)S(1)}, u32[]{:S(2)}, u32[]{:S(2)}) collective-permute-start(bf16[256,256]{1,0:T(8,128)(2,1)S(1)} %collective-permute-done.6.refs_6_), channel_id=1, source_target_pairs={{4,0},{5,1},{8,4},{9,5},{12,8},{13,9},{14,12},{15,13},{10,14},{11,... | collective-permute-start | bytes 393224 | tf_op jit(solution)/shard_map/ppermute | solution.py:209
  11.8 0.0 collective-permute-done.1.refs_3_
  11.9 0.1 collective-permute-start.2
  12.0 0.8 %collective-permute-done.9.refs_10_ = bf16[256,256]{1,0:T(8,128)(2,1)S(1)} collective-permute-done((bf16[256,256]{1,0:T(8,128)(2,1)S(1)}, bf16[256,256]{1,0:T(8,128)(2,1)S(1)}, u32[]{:S(2)}, u32[]{:S(2)}) %collective-permute-start.9) | collective-permute-done | bytes 131104 | tf_op jit(solution)/shard_map/ppermute | solution.py:209
  12.8 1.9 %collective-permute-start.10 = (bf16[256,256]{1,0:T(8,128)(2,1)S(1)}, bf16[256,256]{1,0:T(8,128)(2,1)S(1)}, u32[]{:S(2)}, u32[]{:S(2)}) collective-permute-start(bf16[256,256]{1,0:T(8,128)(2,1)S(1)} %collective-permute-done.9.refs_10_), channel_id=1, source_target_pairs={{4,0},{5,1},{8,4},{9,5},{12,8},{13,9},{14,12},{15,13},{10,14},{11,... | collective-permute-start | bytes 393224 | tf_op jit(solution)/shard_map/ppermute | solution.py:209
  14.7 0.0 collective-permute-done.4.refs_4_
  14.7 0.0 collective-permute-start.12
  14.7 1.0 %collective-permute-done.7.refs_7_ = bf16[256,256]{1,0:T(8,128)(2,1)S(1)} collective-permute-done((bf16[256,256]{1,0:T(8,128)(2,1)S(1)}, bf16[256,256]{1,0:T(8,128)(2,1)S(1)}, u32[]{:S(2)}, u32[]{:S(2)}) %collective-permute-start.7) | collective-permute-done | bytes 131104 | tf_op jit(solution)/shard_map/ppermute | solution.py:209
  15.6 2.0 %collective-permute-start.5 = (bf16[256,256]{1,0:T(8,128)(2,1)S(1)}, bf16[256,256]{1,0:T(8,128)(2,1)S(1)}, u32[]{:S(2)}, u32[]{:S(2)}) collective-permute-start(bf16[256,256]{1,0:T(8,128)(2,1)S(1)} %collective-permute-done.4.refs_4_), channel_id=1, source_target_pairs={{0,4},{1,5},{4,8},{5,9},{8,12},{9,13},{12,14},{13,15},{14,10},{15,... | collective-permute-start | bytes 393224 | tf_op jit(solution)/shard_map/ppermute | solution.py:209
  17.6 0.0 collective-permute-done.2.refs_4_
  17.6 1.6 %collective-permute-start.3 = (bf16[256,256]{1,0:T(8,128)(2,1)S(1)}, bf16[256,256]{1,0:T(8,128)(2,1)S(1)}, u32[]{:S(2)}, u32[]{:S(2)}) collective-permute-start(bf16[256,256]{1,0:T(8,128)(2,1)S(1)} %collective-permute-done.2.refs_4_), channel_id=1, source_target_pairs={{0,4},{1,5},{4,8},{5,9},{8,12},{9,13},{12,14},{13,15},{14,10},{15,... | collective-permute-start | bytes 393224 | tf_op jit(solution)/shard_map/ppermute | solution.py:209
  19.2 0.0 collective-permute-done.10.refs_11_
  19.2 0.6 %collective-permute-start.11 = (bf16[256,256]{1,0:T(8,128)(2,1)S(1)}, bf16[256,256]{1,0:T(8,128)(2,1)S(1)}, u32[]{:S(2)}, u32[]{:S(2)}) collective-permute-start(bf16[256,256]{1,0:T(8,128)(2,1)S(1)} %collective-permute-done.10.refs_11_), channel_id=1, source_target_pairs={{4,0},{5,1},{8,4},{9,5},{12,8},{13,9},{14,12},{15,13},{10,14},{11,... | collective-permute-start | bytes 393224 | tf_op jit(solution)/shard_map/ppermute | solution.py:209
  19.8 2.2 %collective-permute-done.5.refs_5_ = bf16[256,256]{1,0:T(8,128)(2,1)S(1)} collective-permute-done((bf16[256,256]{1,0:T(8,128)(2,1)S(1)}, bf16[256,256]{1,0:T(8,128)(2,1)S(1)}, u32[]{:S(2)}, u32[]{:S(2)}) %collective-permute-start.5) | collective-permute-done | bytes 131104 | tf_op jit(solution)/shard_map/ppermute | solution.py:209
  22.0 1.6 %collective-permute-start.8 = (bf16[256,256]{1,0:T(8,128)(2,1)S(1)}, bf16[256,256]{1,0:T(8,128)(2,1)S(1)}, u32[]{:S(2)}, u32[]{:S(2)}) collective-permute-start(bf16[256,256]{1,0:T(8,128)(2,1)S(1)} %collective-permute-done.7.refs_7_), channel_id=1, source_target_pairs={{4,0},{5,1},{8,4},{9,5},{12,8},{13,9},{14,12},{15,13},{10,14},{11,... | collective-permute-start | bytes 393224 | tf_op jit(solution)/shard_map/ppermute | solution.py:209
  23.6 0.0 collective-permute-done.3.refs_5_
  23.6 0.6 %collective-permute-start.13 = (bf16[256,256]{1,0:T(8,128)(2,1)S(1)}, bf16[256,256]{1,0:T(8,128)(2,1)S(1)}, u32[]{:S(2)}, u32[]{:S(2)}) collective-permute-start(bf16[256,256]{1,0:T(8,128)(2,1)S(1)} %collective-permute-done.3.refs_5_), channel_id=1, source_target_pairs={{0,4},{1,5},{4,8},{5,9},{8,12},{9,13},{12,14},{13,15},{14,10},{15,... | collective-permute-start | bytes 393224 | tf_op jit(solution)/shard_map/ppermute | solution.py:209
  24.2 0.2 collective-permute-done.11.refs_12_
  24.4 1.6 %collective-permute-start.14 = (bf16[256,256]{1,0:T(8,128)(2,1)S(1)}, bf16[256,256]{1,0:T(8,128)(2,1)S(1)}, u32[]{:S(2)}, u32[]{:S(2)}) collective-permute-start(bf16[256,256]{1,0:T(8,128)(2,1)S(1)} %collective-permute-done.11.refs_12_), channel_id=1, source_target_pairs={{4,0},{5,1},{8,4},{9,5},{12,8},{13,9},{14,12},{15,13},{10,14},{11,... | collective-permute-start | bytes 393224 | tf_op jit(solution)/shard_map/ppermute | solution.py:209
  26.0 1.5 %collective-permute-done.8.refs_8_ = bf16[256,256]{1,0:T(8,128)(2,1)S(1)} collective-permute-done((bf16[256,256]{1,0:T(8,128)(2,1)S(1)}, bf16[256,256]{1,0:T(8,128)(2,1)S(1)}, u32[]{:S(2)}, u32[]{:S(2)}) %collective-permute-start.8) | collective-permute-done | bytes 131104 | tf_op jit(solution)/shard_map/ppermute | solution.py:209
  27.4 0.0 collective-permute-done.refs_1_.swapped
  27.4 0.9 %early.1 = (f32[256,256]{1,0:T(8,128)S(1)}, f32[256,256]{1,0:T(8,128)S(1)}, f32[256,256]{1,0:T(8,128)S(1)}, f32[256,256]{1,0:T(8,128)S(1)}, f32[256,256]{1,0:T(8...) custom-call(bf16[256,4096]{1,0:T(8,128)(2,1)S(1)} %get-tuple-element.36.refs_0_.window, ...), custom_call_target="tpu_custom_call" | custom-call | flops 872415232 | bytes 5636096 | tf_op jit(solution)/shard_map/early/pallas_call | solution.py:32
  28.4 0.0 collective-permute-done.12.rest_9_
  28.4 0.1 collective-permute-done.13.rest_10_
  28.5 0.8 %collective-permute-done.14.rest_11_ = bf16[256,256]{1,0:T(8,128)(2,1)S(1)} collective-permute-done((bf16[256,256]{1,0:T(8,128)(2,1)S(1)}, bf16[256,256]{1,0:T(8,128)(2,1)S(1)}, u32[]{:S(2)}, u32[]{:S(2)}) %collective-permute-start.14) | collective-permute-done | bytes 131104 | tf_op jit(solution)/shard_map/ppermute | solution.py:209
  29.4 1.0 %late.1 = (f32[256,256]{1,0:T(8,128)S(1)}, f32[256,256]{1,0:T(8,128)S(1)}, f32[256,256]{1,0:T(8,128)S(1)}, f32[256,256]{1,0:T(8,128)S(1)}, f32[272,256]{1,0:T(8,128)S(1)}, /*index=5*/f32[272,256]{1,0:T(8,128)S(1)}) custom-call(bf16[256,4096]{1,0:T(8,128)(2,1)S(1)} %get-tuple-element.36.refs_0_.window, ...), custom_call_target="tpu_custom_call" | custom-call | flops 536870912 | bytes 7340032 | tf_op jit(solution)/shard_map/late/pallas_call | solution.py:32
  30.4 0.1 collective-permute-start.16
  30.4 1.5 %collective-permute-done.16 = f32[272,256]{1,0:T(8,128)S(1)} collective-permute-done((f32[272,256]{1,0:T(8,128)S(1)}, f32[272,256]{1,0:T(8,128)S(1)}, u32[]{:S(2)}, u32[]{:S(2)}) %collective-permute-start.16) | collective-permute-done | bytes 278560 | tf_op jit(solution)/shard_map/ppermute | solution.py:209
  32.0 1.6 %collective-permute-start.19 = (bf16[144,256]{1,0:T(8,128)(2,1)S(1)}, bf16[144,256]{1,0:T(8,128)(2,1)S(1)}, u32[]{:S(2)}, u32[]{:S(2)}) collective-permute-start(bf16[144,256]{1,0:T(8,128)(2,1)S(1)} %slice.10), channel_id=1, source_target_pairs={{0,2},{1,3},{2,0},{3,1},{4,6},{5,7},{6,4},{7,5},{8,10},{9,11},{10,... | collective-permute-start | bytes 221192 | tf_op jit(solution)/shard_map/ppermute | solution.py:209
  33.7 0.0 collective-permute-start.15
  33.7 0.5 collective-permute-start.23
  34.2 1.7 %collective-permute-start.17 = (bf16[256,256]{1,0:T(8,128)(2,1)S(1)}, bf16[256,256]{1,0:T(8,128)(2,1)S(1)}, u32[]{:S(2)}, u32[]{:S(2)}) collective-permute-start(bf16[256,256]{1,0:T(8,128)(2,1)S(1)} %collective-permute-done.5.refs_5_), channel_id=1, source_target_pairs={{0,4},{1,5},{4,8},{5,9},{8,12},{9,13},{12,14},{13,15},{14,10},{15,... | collective-permute-start | bytes 393224 | tf_op jit(solution)/shard_map/ppermute | solution.py:209
  35.9 0.6 %collective-permute-done.19 = bf16[144,256]{1,0:T(8,128)(2,1)S(1)} collective-permute-done((bf16[144,256]{1,0:T(8,128)(2,1)S(1)}, bf16[144,256]{1,0:T(8,128)(2,1)S(1)}, u32[]{:S(2)}, u32[]{:S(2)}) %collective-permute-start.19) | collective-permute-done | bytes 73760 | tf_op jit(solution)/shard_map/ppermute | solution.py:209
  36.5 1.7 %collective-permute-start.20 = (bf16[144,256]{1,0:T(8,128)(2,1)S(1)}, bf16[144,256]{1,0:T(8,128)(2,1)S(1)}, u32[]{:S(2)}, u32[]{:S(2)}) collective-permute-start(bf16[144,256]{1,0:T(8,128)(2,1)S(1)} %add_convert_fusion.1), channel_id=1, source_target_pairs={{0,4},{1,5},{2,6},{3,7},{4,0},{5,1},{6,2},{7,3},{8,12},{9,13},{10,... | collective-permute-start | bytes 221192 | tf_op jit(solution)/shard_map/ppermute | solution.py:209
  38.2 0.4 collective-permute-done.23
  38.7 1.2 %collective-permute-start.24 = (bf16[128,256]{1,0:T(8,128)(2,1)S(1)}, bf16[128,256]{1,0:T(8,128)(2,1)S(1)}, u32[]{:S(2)}, u32[]{:S(2)}) collective-permute-start(bf16[128,256]{1,0:T(8,128)(2,1)S(1)} %add_convert_fusion.3), channel_id=1, source_target_pairs={{0,4},{1,5},{2,6},{3,7},{4,0},{5,1},{6,2},{7,3},{8,12},{9,13},{10,... | collective-permute-start | bytes 196616 | tf_op jit(solution)/shard_map/ppermute | solution.py:209
  39.9 1.5 %collective-permute-done.20 = bf16[144,256]{1,0:T(8,128)(2,1)S(1)} collective-permute-done((bf16[144,256]{1,0:T(8,128)(2,1)S(1)}, bf16[144,256]{1,0:T(8,128)(2,1)S(1)}, u32[]{:S(2)}, u32[]{:S(2)}) %collective-permute-start.20) | collective-permute-done | bytes 73760 | tf_op jit(solution)/shard_map/ppermute | solution.py:209
  41.4 2.6 %collective-permute-start.21 = (bf16[144,256]{1,0:T(8,128)(2,1)S(1)}, bf16[144,256]{1,0:T(8,128)(2,1)S(1)}, u32[]{:S(2)}, u32[]{:S(2)}) collective-permute-start(bf16[144,256]{1,0:T(8,128)(2,1)S(1)} %add_convert_fusion), channel_id=1, source_target_pairs={{0,8},{1,9},{2,10},{3,11},{4,12},{5,13},{6,14},{7,15},{8,0},{9,1},... | collective-permute-start | bytes 221192 | tf_op jit(solution)/shard_map/ppermute | solution.py:209
  44.0 0.0 collective-permute-done.24
  44.0 1.2 %collective-permute-start.25 = (bf16[128,256]{1,0:T(8,128)(2,1)S(1)}, bf16[128,256]{1,0:T(8,128)(2,1)S(1)}, u32[]{:S(2)}, u32[]{:S(2)}) collective-permute-start(bf16[128,256]{1,0:T(8,128)(2,1)S(1)} %add_convert_fusion.2), channel_id=1, source_target_pairs={{0,8},{1,9},{2,10},{3,11},{4,12},{5,13},{6,14},{7,15},{8,0},{9,1},... | collective-permute-start | bytes 196616 | tf_op jit(solution)/shard_map/ppermute | solution.py:209
  45.2 0.0 collective-permute-done.17.refs_6_
  45.2 0.0 copy-start
  45.2 0.4 rest.1
  45.6 0.1 collective-permute-start.18
  45.7 3.4 %collective-permute-done.21 = bf16[144,256]{1,0:T(8,128)(2,1)S(1)} collective-permute-done((bf16[144,256]{1,0:T(8,128)(2,1)S(1)}, bf16[144,256]{1,0:T(8,128)(2,1)S(1)}, u32[]{:S(2)}, u32[]{:S(2)}) %collective-permute-start.21) | collective-permute-done | bytes 73760 | tf_op jit(solution)/shard_map/ppermute | solution.py:209
  49.2 0.1 collective-permute-start.22
  49.2 0.6 %collective-permute-done.25 = bf16[128,256]{1,0:T(8,128)(2,1)S(1)} collective-permute-done((bf16[128,256]{1,0:T(8,128)(2,1)S(1)}, bf16[128,256]{1,0:T(8,128)(2,1)S(1)}, u32[]{:S(2)}, u32[]{:S(2)}) %collective-permute-start.25) | collective-permute-done | bytes 65568 | tf_op jit(solution)/shard_map/ppermute | solution.py:209
  49.9 0.1 collective-permute-start.26
  49.9 0.0 collective-permute-done.15.received_one
  50.0 0.0 collective-permute-done.18.received_two
  50.0 0.0 copy-done
  50.0 1.0 %columns.1 = (bf16[256,256]{1,0:T(8,128)(2,1)}, bf16[256,256]{1,0:T(8,128)(2,1)}) custom-call(f32[256,256]{1,0:T(8,128)S(1)} %get-tuple-element.49.own_one, f32[256,256]{1,0:T(8,128)S(1)} %collective-permute-done.15.received_one, f32[256,256]{1,0:T(8,128)S(1)} %get-tuple-element.56.own_two, f32[256,256]{1,0:T(8,128)S(1)} %collective-permute-done.18.received_two, ...), custom_call_target="tpu_custom_call" | custom-call | bytes 1181696 | tf_op jit(solution)/shard_map/columns/pallas_call | solution.py:32
  51.0 0.0 collective-permute-done.22.pack_b
  51.0 0.3 collective-permute-done.26.cross_b
  51.3 0.0 copy-done.1
  51.3 0.0 copy-done.2
  51.3 1.3 %last.1 = (f32[256,256]{1,0:T(8,128)}, f32[256,256]{1,0:T(8,128)}, f32[256,256]{1,0:T(8,128)}) custom-call(f32[144,256]{1,0:T(8,128)S(1)} %convert_add_fusion.pack_a, f32[144,256]{1,0:T(8,128)S(1)} %collective-permute-done.22.pack_b, f32[128,256]{1,0:T(8,128)S(1)} %convert_add_fusion.1.cross_a, f32[128,256]{1,0:T(8,128)S(1)} %collective-permute-done.26.cross_b, ...), custom_call_target="tpu_custom_call" | custom-call | bytes 1212416 | tf_op jit(solution)/shard_map/last/pallas_call | solution.py:32
  (11 shorter events, 0.2 us)
Async XLA Ops:
  2.4 25.0 %collective-permute-start = (bf16[256,4096]{1,0:T(8,128)(2,1)S(1)}, bf16[256,4096]{1,0:T(8,128)(2,1)S(1)}, u32[]{:S(2)}, u32[]{:S(2)}) collective-permute-start(bf16[256,4096]{1,0:T(8,128)(2,1)S(1)} %get-tuple-element.36.refs_0_.window), channel_id=1, source_target_pairs={{0,1},{1,0},{2,3},{3,2},{4,5},{5,4},{6,7},{7,6},{8,9},{9,8},{10,11... | collective-permute-start | bytes 6291464 | tf_op jit(solution)/shard_map/ppermute | solution.py:209
  3.0 7.0 %collective-permute-start.6 = (bf16[256,256]{1,0:T(8,128)(2,1)S(1)}, bf16[256,256]{1,0:T(8,128)(2,1)S(1)}, u32[]{:S(2)}, u32[]{:S(2)}) collective-permute-start(bf16[256,256]{1,0:T(8,128)(2,1)S(1)} %get-tuple-element.37.refs_2_), channel_id=1, source_target_pairs={{4,0},{5,1},{8,4},{9,5},{12,8},{13,9},{14,12},{15,13},{10,14},{11,... | collective-permute-start | bytes 393224 | tf_op jit(solution)/shard_map/ppermute | solution.py:209
  5.5 6.3 %collective-permute-start.1 = (bf16[256,256]{1,0:T(8,128)(2,1)S(1)}, bf16[256,256]{1,0:T(8,128)(2,1)S(1)}, u32[]{:S(2)}, u32[]{:S(2)}) collective-permute-start(bf16[256,256]{1,0:T(8,128)(2,1)S(1)} %get-tuple-element.37.refs_2_), channel_id=1, source_target_pairs={{0,4},{1,5},{4,8},{5,9},{8,12},{9,13},{12,14},{13,15},{14,10},{15,... | collective-permute-start | bytes 393224 | tf_op jit(solution)/shard_map/ppermute | solution.py:209
  5.7 7.1 %collective-permute-start.9 = (bf16[256,256]{1,0:T(8,128)(2,1)S(1)}, bf16[256,256]{1,0:T(8,128)(2,1)S(1)}, u32[]{:S(2)}, u32[]{:S(2)}) collective-permute-start(bf16[256,256]{1,0:T(8,128)(2,1)S(1)} %get-tuple-element.38.refs_9_), channel_id=1, source_target_pairs={{4,0},{5,1},{8,4},{9,5},{12,8},{13,9},{14,12},{15,13},{10,14},{11,... | collective-permute-start | bytes 393224 | tf_op jit(solution)/shard_map/ppermute | solution.py:209
  7.6 7.1 %collective-permute-start.4 = (bf16[256,256]{1,0:T(8,128)(2,1)S(1)}, bf16[256,256]{1,0:T(8,128)(2,1)S(1)}, u32[]{:S(2)}, u32[]{:S(2)}) collective-permute-start(bf16[256,256]{1,0:T(8,128)(2,1)S(1)} %get-tuple-element.38.refs_9_), channel_id=1, source_target_pairs={{0,4},{1,5},{4,8},{5,9},{8,12},{9,13},{12,14},{13,15},{14,10},{15,... | collective-permute-start | bytes 393224 | tf_op jit(solution)/shard_map/ppermute | solution.py:209
  10.0 5.7 %collective-permute-start.7 = (bf16[256,256]{1,0:T(8,128)(2,1)S(1)}, bf16[256,256]{1,0:T(8,128)(2,1)S(1)}, u32[]{:S(2)}, u32[]{:S(2)}) collective-permute-start(bf16[256,256]{1,0:T(8,128)(2,1)S(1)} %collective-permute-done.6.refs_6_), channel_id=1, source_target_pairs={{4,0},{5,1},{8,4},{9,5},{12,8},{13,9},{14,12},{15,13},{10,14},{11,... | collective-permute-start | bytes 393224 | tf_op jit(solution)/shard_map/ppermute | solution.py:209
  11.9 5.7 %collective-permute-start.2 = (bf16[256,256]{1,0:T(8,128)(2,1)S(1)}, bf16[256,256]{1,0:T(8,128)(2,1)S(1)}, u32[]{:S(2)}, u32[]{:S(2)}) collective-permute-start(bf16[256,256]{1,0:T(8,128)(2,1)S(1)} %collective-permute-done.1.refs_3_), channel_id=1, source_target_pairs={{0,4},{1,5},{4,8},{5,9},{8,12},{9,13},{12,14},{13,15},{14,10},{15,... | collective-permute-start | bytes 393224 | tf_op jit(solution)/shard_map/ppermute | solution.py:209
  12.8 6.4 %collective-permute-start.10 = (bf16[256,256]{1,0:T(8,128)(2,1)S(1)}, bf16[256,256]{1,0:T(8,128)(2,1)S(1)}, u32[]{:S(2)}, u32[]{:S(2)}) collective-permute-start(bf16[256,256]{1,0:T(8,128)(2,1)S(1)} %collective-permute-done.9.refs_10_), channel_id=1, source_target_pairs={{4,0},{5,1},{8,4},{9,5},{12,8},{13,9},{14,12},{15,13},{10,14},{11,... | collective-permute-start | bytes 393224 | tf_op jit(solution)/shard_map/ppermute | solution.py:209
  14.7 13.7 %collective-permute-start.12 = (bf16[768,256]{1,0:T(8,128)(2,1)S(1)}, bf16[768,256]{1,0:T(8,128)(2,1)S(1)}, u32[]{:S(2)}, u32[]{:S(2)}) collective-permute-start(bf16[768,256]{1,0:T(8,128)(2,1)S(1)} %get-tuple-element.48.rest_8_), channel_id=1, source_target_pairs={{0,1},{1,0},{2,3},{3,2},{4,5},{5,4},{6,7},{7,6},{8,9},{9,8},{10,11... | collective-permute-start | bytes 1179656 | tf_op jit(solution)/shard_map/ppermute | solution.py:209
  15.6 6.4 %collective-permute-start.5 = (bf16[256,256]{1,0:T(8,128)(2,1)S(1)}, bf16[256,256]{1,0:T(8,128)(2,1)S(1)}, u32[]{:S(2)}, u32[]{:S(2)}) collective-permute-start(bf16[256,256]{1,0:T(8,128)(2,1)S(1)} %collective-permute-done.4.refs_4_), channel_id=1, source_target_pairs={{0,4},{1,5},{4,8},{5,9},{8,12},{9,13},{12,14},{13,15},{14,10},{15,... | collective-permute-start | bytes 393224 | tf_op jit(solution)/shard_map/ppermute | solution.py:209
  17.6 5.9 %collective-permute-start.3 = (bf16[256,256]{1,0:T(8,128)(2,1)S(1)}, bf16[256,256]{1,0:T(8,128)(2,1)S(1)}, u32[]{:S(2)}, u32[]{:S(2)}) collective-permute-start(bf16[256,256]{1,0:T(8,128)(2,1)S(1)} %collective-permute-done.2.refs_4_), channel_id=1, source_target_pairs={{0,4},{1,5},{4,8},{5,9},{8,12},{9,13},{12,14},{13,15},{14,10},{15,... | collective-permute-start | bytes 393224 | tf_op jit(solution)/shard_map/ppermute | solution.py:209
  19.2 5.2 %collective-permute-start.11 = (bf16[256,256]{1,0:T(8,128)(2,1)S(1)}, bf16[256,256]{1,0:T(8,128)(2,1)S(1)}, u32[]{:S(2)}, u32[]{:S(2)}) collective-permute-start(bf16[256,256]{1,0:T(8,128)(2,1)S(1)} %collective-permute-done.10.refs_11_), channel_id=1, source_target_pairs={{4,0},{5,1},{8,4},{9,5},{12,8},{13,9},{14,12},{15,13},{10,14},{11,... | collective-permute-start | bytes 393224 | tf_op jit(solution)/shard_map/ppermute | solution.py:209
  22.0 5.5 %collective-permute-start.8 = (bf16[256,256]{1,0:T(8,128)(2,1)S(1)}, bf16[256,256]{1,0:T(8,128)(2,1)S(1)}, u32[]{:S(2)}, u32[]{:S(2)}) collective-permute-start(bf16[256,256]{1,0:T(8,128)(2,1)S(1)} %collective-permute-done.7.refs_7_), channel_id=1, source_target_pairs={{4,0},{5,1},{8,4},{9,5},{12,8},{13,9},{14,12},{15,13},{10,14},{11,... | collective-permute-start | bytes 393224 | tf_op jit(solution)/shard_map/ppermute | solution.py:209
  23.6 5.0 %collective-permute-start.13 = (bf16[256,256]{1,0:T(8,128)(2,1)S(1)}, bf16[256,256]{1,0:T(8,128)(2,1)S(1)}, u32[]{:S(2)}, u32[]{:S(2)}) collective-permute-start(bf16[256,256]{1,0:T(8,128)(2,1)S(1)} %collective-permute-done.3.refs_5_), channel_id=1, source_target_pairs={{0,4},{1,5},{4,8},{5,9},{8,12},{9,13},{12,14},{13,15},{14,10},{15,... | collective-permute-start | bytes 393224 | tf_op jit(solution)/shard_map/ppermute | solution.py:209
  24.4 5.0 %collective-permute-start.14 = (bf16[256,256]{1,0:T(8,128)(2,1)S(1)}, bf16[256,256]{1,0:T(8,128)(2,1)S(1)}, u32[]{:S(2)}, u32[]{:S(2)}) collective-permute-start(bf16[256,256]{1,0:T(8,128)(2,1)S(1)} %collective-permute-done.11.refs_12_), channel_id=1, source_target_pairs={{4,0},{5,1},{8,4},{9,5},{12,8},{13,9},{14,12},{15,13},{10,14},{11,... | collective-permute-start | bytes 393224 | tf_op jit(solution)/shard_map/ppermute | solution.py:209
  30.4 1.6 %collective-permute-start.16 = (f32[272,256]{1,0:T(8,128)S(1)}, f32[272,256]{1,0:T(8,128)S(1)}, u32[]{:S(2)}, u32[]{:S(2)}) collective-permute-start(f32[272,256]{1,0:T(8,128)S(1)} %get-tuple-element.54), channel_id=1, source_target_pairs={{0,1},{1,0},{2,3},{3,2},{4,5},{5,4},{6,7},{7,6},{8,9},{9,8},{10,11... | collective-permute-start | bytes 835592 | tf_op jit(solution)/shard_map/ppermute | solution.py:209
  32.0 4.4 %collective-permute-start.19 = (bf16[144,256]{1,0:T(8,128)(2,1)S(1)}, bf16[144,256]{1,0:T(8,128)(2,1)S(1)}, u32[]{:S(2)}, u32[]{:S(2)}) collective-permute-start(bf16[144,256]{1,0:T(8,128)(2,1)S(1)} %slice.10), channel_id=1, source_target_pairs={{0,2},{1,3},{2,0},{3,1},{4,6},{5,7},{6,4},{7,5},{8,10},{9,11},{10,... | collective-permute-start | bytes 221192 | tf_op jit(solution)/shard_map/ppermute | solution.py:209
  33.7 16.3 %collective-permute-start.15 = (f32[256,256]{1,0:T(8,128)S(1)}, f32[256,256]{1,0:T(8,128)S(1)}, u32[]{:S(2)}, u32[]{:S(2)}) collective-permute-start(f32[256,256]{1,0:T(8,128)S(1)} %get-tuple-element.50), channel_id=1, source_target_pairs={{0,1},{1,0},{2,3},{3,2},{4,5},{5,4},{6,7},{7,6},{8,9},{9,8},{10,11... | collective-permute-start | bytes 786440 | tf_op jit(solution)/shard_map/ppermute | solution.py:209
  33.7 5.0 %collective-permute-start.23 = (bf16[128,256]{1,0:T(8,128)(2,1)S(1)}, bf16[128,256]{1,0:T(8,128)(2,1)S(1)}, u32[]{:S(2)}, u32[]{:S(2)}) collective-permute-start(bf16[128,256]{1,0:T(8,128)(2,1)S(1)} %slice.11), channel_id=1, source_target_pairs={{0,2},{1,3},{2,0},{3,1},{4,6},{5,7},{6,4},{7,5},{8,10},{9,11},{10,... | collective-permute-start | bytes 196616 | tf_op jit(solution)/shard_map/ppermute | solution.py:209
  34.2 11.0 %collective-permute-start.17 = (bf16[256,256]{1,0:T(8,128)(2,1)S(1)}, bf16[256,256]{1,0:T(8,128)(2,1)S(1)}, u32[]{:S(2)}, u32[]{:S(2)}) collective-permute-start(bf16[256,256]{1,0:T(8,128)(2,1)S(1)} %collective-permute-done.5.refs_5_), channel_id=1, source_target_pairs={{0,4},{1,5},{4,8},{5,9},{8,12},{9,13},{12,14},{13,15},{14,10},{15,... | collective-permute-start | bytes 393224 | tf_op jit(solution)/shard_map/ppermute | solution.py:209
  36.5 4.9 %collective-permute-start.20 = (bf16[144,256]{1,0:T(8,128)(2,1)S(1)}, bf16[144,256]{1,0:T(8,128)(2,1)S(1)}, u32[]{:S(2)}, u32[]{:S(2)}) collective-permute-start(bf16[144,256]{1,0:T(8,128)(2,1)S(1)} %add_convert_fusion.1), channel_id=1, source_target_pairs={{0,4},{1,5},{2,6},{3,7},{4,0},{5,1},{6,2},{7,3},{8,12},{9,13},{10,... | collective-permute-start | bytes 221192 | tf_op jit(solution)/shard_map/ppermute | solution.py:209
  38.7 5.3 %collective-permute-start.24 = (bf16[128,256]{1,0:T(8,128)(2,1)S(1)}, bf16[128,256]{1,0:T(8,128)(2,1)S(1)}, u32[]{:S(2)}, u32[]{:S(2)}) collective-permute-start(bf16[128,256]{1,0:T(8,128)(2,1)S(1)} %add_convert_fusion.3), channel_id=1, source_target_pairs={{0,4},{1,5},{2,6},{3,7},{4,0},{5,1},{6,2},{7,3},{8,12},{9,13},{10,... | collective-permute-start | bytes 196616 | tf_op jit(solution)/shard_map/ppermute | solution.py:209
  41.4 7.7 %collective-permute-start.21 = (bf16[144,256]{1,0:T(8,128)(2,1)S(1)}, bf16[144,256]{1,0:T(8,128)(2,1)S(1)}, u32[]{:S(2)}, u32[]{:S(2)}) collective-permute-start(bf16[144,256]{1,0:T(8,128)(2,1)S(1)} %add_convert_fusion), channel_id=1, source_target_pairs={{0,8},{1,9},{2,10},{3,11},{4,12},{5,13},{6,14},{7,15},{8,0},{9,1},... | collective-permute-start | bytes 221192 | tf_op jit(solution)/shard_map/ppermute | solution.py:209
  44.0 5.8 %collective-permute-start.25 = (bf16[128,256]{1,0:T(8,128)(2,1)S(1)}, bf16[128,256]{1,0:T(8,128)(2,1)S(1)}, u32[]{:S(2)}, u32[]{:S(2)}) collective-permute-start(bf16[128,256]{1,0:T(8,128)(2,1)S(1)} %add_convert_fusion.2), channel_id=1, source_target_pairs={{0,8},{1,9},{2,10},{3,11},{4,12},{5,13},{6,14},{7,15},{8,0},{9,1},... | collective-permute-start | bytes 196616 | tf_op jit(solution)/shard_map/ppermute | solution.py:209
  45.2 4.7 %copy-start = (bf16[256,256]{1,0:T(8,128)(2,1)S(1)}, bf16[256,256]{1,0:T(8,128)(2,1)}, u32[]{:S(2)}) copy-start(bf16[256,256]{1,0:T(8,128)(2,1)} %cross.3) | copy-start | bytes 393220
  45.2 6.0 %copy-start.1 = (f32[256,256]{1,0:T(8,128)S(1)}, f32[256,256]{1,0:T(8,128)}, u32[]{:S(2)}) copy-start(f32[256,256]{1,0:T(8,128)} %diag_one.1) | copy-start | bytes 786436
  45.2 6.0 %copy-start.2 = (f32[256,256]{1,0:T(8,128)S(1)}, f32[256,256]{1,0:T(8,128)}, u32[]{:S(2)}) copy-start(f32[256,256]{1,0:T(8,128)} %diag_two.1) | copy-start | bytes 786436
  45.6 4.3 %collective-permute-start.18 = (f32[256,256]{1,0:T(8,128)S(1)}, f32[256,256]{1,0:T(8,128)S(1)}, u32[]{:S(2)}, u32[]{:S(2)}) collective-permute-start(f32[256,256]{1,0:T(8,128)S(1)} %get-tuple-element.57), channel_id=1, source_target_pairs={{0,1},{1,0},{2,3},{3,2},{4,5},{5,4},{6,7},{7,6},{8,9},{9,8},{10,11... | collective-permute-start | bytes 786440 | tf_op jit(solution)/shard_map/ppermute | solution.py:209
  49.2 1.8 %collective-permute-start.22 = (f32[144,256]{1,0:T(8,128)S(1)}, f32[144,256]{1,0:T(8,128)S(1)}, u32[]{:S(2)}, u32[]{:S(2)}) collective-permute-start(f32[144,256]{1,0:T(8,128)S(1)} %convert_add_fusion.pack_a), channel_id=1, source_target_pairs={{0,1},{1,0},{2,3},{3,2},{4,5},{5,4},{6,7},{7,6},{8,9},{9,8},{10,11... | collective-permute-start | bytes 442376 | tf_op jit(solution)/shard_map/ppermute | solution.py:209
  49.9 1.4 %collective-permute-start.26 = (f32[128,256]{1,0:T(8,128)S(1)}, f32[128,256]{1,0:T(8,128)S(1)}, u32[]{:S(2)}, u32[]{:S(2)}) collective-permute-start(f32[128,256]{1,0:T(8,128)S(1)} %convert_add_fusion.1.cross_a), channel_id=1, source_target_pairs={{0,1},{1,0},{2,3},{3,2},{4,5},{5,4},{6,7},{7,6},{8,9},{9,8},{10,11... | collective-permute-start | bytes 393224 | tf_op jit(solution)/shard_map/ppermute | solution.py:209

commit v5 on v4

--- a/solution.py
+++ b/solution.py
@@ -123,7 +123,7 @@
 
 
 def late_body(steps, window, swapped, *rest):
-    sums, (stack, sibling, one, two), outs, (keep, send) = rest[:8], rest[8:12], rest[12:16], rest[16:]
+    sums, (stack, sibling, one, two), outs, parts = rest[:8], rest[8:12], rest[12:16], rest[16:]
     sums = [(sums[i][...], sums[i + 1][...]) for i in range(0, 8, 2)]
     far = product(-steps, window, swapped, one)
     image_one = plus(sums[1], far)
@@ -142,12 +142,12 @@
     second = second + second.T
     both = jnp.where(row <= col, first + first.T, second)
     diagonal = jnp.sum(jnp.where(row == col, second, 0.0), axis=0, keepdims=True)
-    diagonal = jnp.broadcast_to(diagonal, (keep.shape[0] - n, n))
+    diagonal = jnp.broadcast_to(diagonal, (parts[0].shape[0] - half, n))
     low = lax.axis_index(AXIS) % 2 == 0
-    for out, mine in ((keep, low), (send, jnp.logical_not(low))):
-        out[:half] = jnp.where(mine, both[:half], both[half:])
-        out[half:-half] = diagonal
-        out[-half:] = jnp.where(mine, cross[:half], cross[half:])
+    for i, mine in enumerate((low, jnp.logical_not(low))):
+        parts[i][:half] = jnp.where(mine, both[:half], both[half:])
+        parts[i][half:] = diagonal
+        parts[2 + i][...] = jnp.where(mine, cross[:half], cross[half:])
 
 
 def rest_body(window, swapped, own_in, other_in, up, own, other):
@@ -263,29 +263,30 @@
     )
     block_flops = 4 * rows * width * width
     early = call(early_refs, "early", (square,) * 8, early_in, flops=block_flops * (3 * steps + 1))
-    tall = ((width + 16, width), F32)
-    own_one, other_one, own_two, other_two, keep, away = call(
+    packed = ((half + 8, width), F32)
+    crossed = ((half, width), F32)
+    own_one, other_one, own_two, other_two, keep_p, away_p, keep_x, away_x = call(
         functools.partial(late_body, steps),
         "late",
-        (square,) * 4 + (tall, tall),
+        (square,) * 4 + (packed, packed, crossed, crossed),
         (window, swapped, *early, stack, sibling, one_far, two_far),
         flops=block_flops * 8,
     )
-    value = keep + send(away, flip[0])
-    value, last_up = lax.optimization_barrier((value, two_up[-1]))
+    pack_half = keep_p + send(away_p, flip[0])
+    cross_half = keep_x + send(away_x, flip[0])
+    pack_half, last_up = lax.optimization_barrier((pack_half, two_up[-1]))
     two_up.append(send(last_up, ahead))
 
-    stages = []
-
-    def summed(value):
-        for perm in flip[1:]:
+    across = flip[1:]
+
+    def summed(value, order):
+        for perm in order:
             value = value.astype(BF16)
             value = value.astype(F32) + send(value, perm).astype(F32)
-            stages.append(value)
         return value
 
-    pack_a = summed(value[:-half])
-    cross_a = summed(value[-half:])
+    pack_a = summed(pack_half, across)
+    cross_a = summed(cross_half, across[1:] + across[:1])
     pack_b, cross_b = send(pack_a, flip[0]), send(cross_a, flip[0])
 
     received_one = send(other_one, flip[0])

time: 52.7 us -> 51.1 us (0.970)
  waiting for transfers between devices: 17.2 us -> 13.2 us
  starting transfers between devices: 27.9 us -> 30.4 us
    ppermute x27 -> x28, waiting for transfers between devices: 17.2 us -> 13.2 us  [send(): return lax.ppermute(x, AXIS, perm)]
    ppermute x27 -> x28, starting transfers between devices: 27.9 us -> 30.4 us  [send(): return lax.ppermute(x, AXIS, perm)]
  transfers between devices with their start and end apart: 27 -> 28, of which waited for: 15 -> 14; matrix products, arithmetic and copies ran while one was open for 0% -> 0% of each run, Pallas kernels for 4% -> 5%
where the time goes in v5:
time: 51.1 us; the launch traced here: 51 us
  starting transfers between devices  30.4 us (59%)
  waiting for transfers between devices  13.2 us (26%)
  Pallas kernels  6.41 us (13%)
  between operations  0.78 us (2%)
    ppermute x28, starting transfers between devices, send(): return lax.ppermute(x, AXIS, perm)  30.4 us
    ppermute x28, waiting for transfers between devices, send(): return lax.ppermute(x, AXIS, perm)  13.2 us
    pallas_call x6, Pallas kernels, call(): pl.pallas_call(body, name=name, out_shape=tuple((jax.ShapeDtypeStruct(s,...  6.41 us
  transfers between devices with their start and end apart: 28, of which 14 were waited for; matrix products, arithmetic and copies ran while one was open for 0% of the time, Pallas kernels for 5%

profile of v5, /device:TPU:0, one launch (start us, length us, event | category | flops | bytes accessed | tf_op | source)
XLA Modules:
  0.0 51.0 jit_solution(7620711443857604081)
XLA Ops:
  0.6 1.8 %mask.1 = (bf16[256,256]{1,0:T(8,128)(2,1)S(1)}, bf16[256,256]{1,0:T(8,128)(2,1)S(1)}, bf16[768,256]{1,0:T(8,128)(2,1)S(1)}, f32[2,256]{1,0:T(2,128)S(1)}, bf16[256,4096]{1,0:T(8,128)(2,1)S(1)}) custom-call(s32[2,16]{1,0:T(2,128)} %table.1, s32[1,256]{1,0:T(1,128)} %bitcast.1, bf16[256,256]{1,0:T(8,128)(2,1)} %one.1, bf16[256,256]{1,0:T(8,128)(2,1)} %two.1, ...), custom_call_target="tpu_custom_call" | custom-call | bytes 2360448 | tf_op jit(solution)/shard_map/mask/pallas_call | solution.py:32
  2.4 0.5 %collective-permute-start = (bf16[256,4096]{1,0:T(8,128)(2,1)S(1)}, bf16[256,4096]{1,0:T(8,128)(2,1)S(1)}, u32[]{:S(2)}, u32[]{:S(2)}) collective-permute-start(bf16[256,4096]{1,0:T(8,128)(2,1)S(1)} %get-tuple-element.38.refs_0_.window), channel_id=1, source_target_pairs={{0,1},{1,0},{2,3},{3,2},{4,5},{5,4},{6,7},{7,6},{8,9},{9,8},{10,11... | collective-permute-start | bytes 6291464 | tf_op jit(solution)/shard_map/ppermute | solution.py:209
  3.0 2.6 %collective-permute-start.6 = (bf16[256,256]{1,0:T(8,128)(2,1)S(1)}, bf16[256,256]{1,0:T(8,128)(2,1)S(1)}, u32[]{:S(2)}, u32[]{:S(2)}) collective-permute-start(bf16[256,256]{1,0:T(8,128)(2,1)S(1)} %get-tuple-element.39.refs_2_), channel_id=1, source_target_pairs={{4,0},{5,1},{8,4},{9,5},{12,8},{13,9},{14,12},{15,13},{10,14},{11,... | collective-permute-start | bytes 393224 | tf_op jit(solution)/shard_map/ppermute | solution.py:209
  5.5 0.1 collective-permute-start.1
  5.7 1.9 %collective-permute-start.9 = (bf16[256,256]{1,0:T(8,128)(2,1)S(1)}, bf16[256,256]{1,0:T(8,128)(2,1)S(1)}, u32[]{:S(2)}, u32[]{:S(2)}) collective-permute-start(bf16[256,256]{1,0:T(8,128)(2,1)S(1)} %get-tuple-element.40.refs_9_), channel_id=1, source_target_pairs={{4,0},{5,1},{8,4},{9,5},{12,8},{13,9},{14,12},{15,13},{10,14},{11,... | collective-permute-start | bytes 393224 | tf_op jit(solution)/shard_map/ppermute | solution.py:209
  7.6 0.1 collective-permute-start.4
  7.7 2.2 %collective-permute-done.6.refs_6_ = bf16[256,256]{1,0:T(8,128)(2,1)S(1)} collective-permute-done((bf16[256,256]{1,0:T(8,128)(2,1)S(1)}, bf16[256,256]{1,0:T(8,128)(2,1)S(1)}, u32[]{:S(2)}, u32[]{:S(2)}) %collective-permute-start.6) | collective-permute-done | bytes 131104 | tf_op jit(solution)/shard_map/ppermute | solution.py:209
  10.0 1.9 %collective-permute-start.7 = (bf16[256,256]{1,0:T(8,128)(2,1)S(1)}, bf16[256,256]{1,0:T(8,128)(2,1)S(1)}, u32[]{:S(2)}, u32[]{:S(2)}) collective-permute-start(bf16[256,256]{1,0:T(8,128)(2,1)S(1)} %collective-permute-done.6.refs_6_), channel_id=1, source_target_pairs={{4,0},{5,1},{8,4},{9,5},{12,8},{13,9},{14,12},{15,13},{10,14},{11,... | collective-permute-start | bytes 393224 | tf_op jit(solution)/shard_map/ppermute | solution.py:209
  11.8 0.0 collective-permute-done.1.refs_3_
  11.9 0.1 collective-permute-start.2
  12.0 0.8 %collective-permute-done.9.refs_10_ = bf16[256,256]{1,0:T(8,128)(2,1)S(1)} collective-permute-done((bf16[256,256]{1,0:T(8,128)(2,1)S(1)}, bf16[256,256]{1,0:T(8,128)(2,1)S(1)}, u32[]{:S(2)}, u32[]{:S(2)}) %collective-permute-start.9) | collective-permute-done | bytes 131104 | tf_op jit(solution)/shard_map/ppermute | solution.py:209
  12.8 1.9 %collective-permute-start.10 = (bf16[256,256]{1,0:T(8,128)(2,1)S(1)}, bf16[256,256]{1,0:T(8,128)(2,1)S(1)}, u32[]{:S(2)}, u32[]{:S(2)}) collective-permute-start(bf16[256,256]{1,0:T(8,128)(2,1)S(1)} %collective-permute-done.9.refs_10_), channel_id=1, source_target_pairs={{4,0},{5,1},{8,4},{9,5},{12,8},{13,9},{14,12},{15,13},{10,14},{11,... | collective-permute-start | bytes 393224 | tf_op jit(solution)/shard_map/ppermute | solution.py:209
  14.7 0.0 collective-permute-done.4.refs_4_
  14.7 0.0 collective-permute-start.12
  14.7 1.0 %collective-permute-done.7.refs_7_ = bf16[256,256]{1,0:T(8,128)(2,1)S(1)} collective-permute-done((bf16[256,256]{1,0:T(8,128)(2,1)S(1)}, bf16[256,256]{1,0:T(8,128)(2,1)S(1)}, u32[]{:S(2)}, u32[]{:S(2)}) %collective-permute-start.7) | collective-permute-done | bytes 131104 | tf_op jit(solution)/shard_map/ppermute | solution.py:209
  15.6 2.0 %collective-permute-start.5 = (bf16[256,256]{1,0:T(8,128)(2,1)S(1)}, bf16[256,256]{1,0:T(8,128)(2,1)S(1)}, u32[]{:S(2)}, u32[]{:S(2)}) collective-permute-start(bf16[256,256]{1,0:T(8,128)(2,1)S(1)} %collective-permute-done.4.refs_4_), channel_id=1, source_target_pairs={{0,4},{1,5},{4,8},{5,9},{8,12},{9,13},{12,14},{13,15},{14,10},{15,... | collective-permute-start | bytes 393224 | tf_op jit(solution)/shard_map/ppermute | solution.py:209
  17.6 0.0 collective-permute-done.2.refs_4_
  17.6 1.6 %collective-permute-start.3 = (bf16[256,256]{1,0:T(8,128)(2,1)S(1)}, bf16[256,256]{1,0:T(8,128)(2,1)S(1)}, u32[]{:S(2)}, u32[]{:S(2)}) collective-permute-start(bf16[256,256]{1,0:T(8,128)(2,1)S(1)} %collective-permute-done.2.refs_4_), channel_id=1, source_target_pairs={{0,4},{1,5},{4,8},{5,9},{8,12},{9,13},{12,14},{13,15},{14,10},{15,... | collective-permute-start | bytes 393224 | tf_op jit(solution)/shard_map/ppermute | solution.py:209
  19.2 0.0 collective-permute-done.10.refs_11_
  19.2 0.6 %collective-permute-start.11 = (bf16[256,256]{1,0:T(8,128)(2,1)S(1)}, bf16[256,256]{1,0:T(8,128)(2,1)S(1)}, u32[]{:S(2)}, u32[]{:S(2)}) collective-permute-start(bf16[256,256]{1,0:T(8,128)(2,1)S(1)} %collective-permute-done.10.refs_11_), channel_id=1, source_target_pairs={{4,0},{5,1},{8,4},{9,5},{12,8},{13,9},{14,12},{15,13},{10,14},{11,... | collective-permute-start | bytes 393224 | tf_op jit(solution)/shard_map/ppermute | solution.py:209
  19.8 2.2 %collective-permute-done.5.refs_5_ = bf16[256,256]{1,0:T(8,128)(2,1)S(1)} collective-permute-done((bf16[256,256]{1,0:T(8,128)(2,1)S(1)}, bf16[256,256]{1,0:T(8,128)(2,1)S(1)}, u32[]{:S(2)}, u32[]{:S(2)}) %collective-permute-start.5) | collective-permute-done | bytes 131104 | tf_op jit(solution)/shard_map/ppermute | solution.py:209
  22.0 1.6 %collective-permute-start.8 = (bf16[256,256]{1,0:T(8,128)(2,1)S(1)}, bf16[256,256]{1,0:T(8,128)(2,1)S(1)}, u32[]{:S(2)}, u32[]{:S(2)}) collective-permute-start(bf16[256,256]{1,0:T(8,128)(2,1)S(1)} %collective-permute-done.7.refs_7_), channel_id=1, source_target_pairs={{4,0},{5,1},{8,4},{9,5},{12,8},{13,9},{14,12},{15,13},{10,14},{11,... | collective-permute-start | bytes 393224 | tf_op jit(solution)/shard_map/ppermute | solution.py:209
  23.6 0.0 collective-permute-done.3.refs_5_
  23.6 0.6 %collective-permute-start.13 = (bf16[256,256]{1,0:T(8,128)(2,1)S(1)}, bf16[256,256]{1,0:T(8,128)(2,1)S(1)}, u32[]{:S(2)}, u32[]{:S(2)}) collective-permute-start(bf16[256,256]{1,0:T(8,128)(2,1)S(1)} %collective-permute-done.3.refs_5_), channel_id=1, source_target_pairs={{0,4},{1,5},{4,8},{5,9},{8,12},{9,13},{12,14},{13,15},{14,10},{15,... | collective-permute-start | bytes 393224 | tf_op jit(solution)/shard_map/ppermute | solution.py:209
  24.2 0.2 collective-permute-done.11.refs_12_
  24.4 1.6 %collective-permute-start.14 = (bf16[256,256]{1,0:T(8,128)(2,1)S(1)}, bf16[256,256]{1,0:T(8,128)(2,1)S(1)}, u32[]{:S(2)}, u32[]{:S(2)}) collective-permute-start(bf16[256,256]{1,0:T(8,128)(2,1)S(1)} %collective-permute-done.11.refs_12_), channel_id=1, source_target_pairs={{4,0},{5,1},{8,4},{9,5},{12,8},{13,9},{14,12},{15,13},{10,14},{11,... | collective-permute-start | bytes 393224 | tf_op jit(solution)/shard_map/ppermute | solution.py:209
  26.0 1.5 %collective-permute-done.8.refs_8_ = bf16[256,256]{1,0:T(8,128)(2,1)S(1)} collective-permute-done((bf16[256,256]{1,0:T(8,128)(2,1)S(1)}, bf16[256,256]{1,0:T(8,128)(2,1)S(1)}, u32[]{:S(2)}, u32[]{:S(2)}) %collective-permute-start.8) | collective-permute-done | bytes 131104 | tf_op jit(solution)/shard_map/ppermute | solution.py:209
  27.4 0.0 collective-permute-done.refs_1_.swapped
  27.4 0.9 %early.1 = (f32[256,256]{1,0:T(8,128)S(1)}, f32[256,256]{1,0:T(8,128)S(1)}, f32[256,256]{1,0:T(8,128)S(1)}, f32[256,256]{1,0:T(8,128)S(1)}, f32[256,256]{1,0:T(8...) custom-call(bf16[256,4096]{1,0:T(8,128)(2,1)S(1)} %get-tuple-element.38.refs_0_.window, ...), custom_call_target="tpu_custom_call" | custom-call | flops 872415232 | bytes 5636096 | tf_op jit(solution)/shard_map/early/pallas_call | solution.py:32
  28.4 0.0 collective-permute-done.12.rest_9_
  28.4 0.1 collective-permute-done.13.rest_10_
  28.5 0.8 %collective-permute-done.14.rest_11_ = bf16[256,256]{1,0:T(8,128)(2,1)S(1)} collective-permute-done((bf16[256,256]{1,0:T(8,128)(2,1)S(1)}, bf16[256,256]{1,0:T(8,128)(2,1)S(1)}, u32[]{:S(2)}, u32[]{:S(2)}) %collective-permute-start.14) | collective-permute-done | bytes 131104 | tf_op jit(solution)/shard_map/ppermute | solution.py:209
  29.4 1.0 %late.1 = (f32[256,256]{1,0:T(8,128)S(1)}, f32[256,256]{1,0:T(8,128)S(1)}, f32[256,256]{1,0:T(8,128)S(1)}, f32[256,256]{1,0:T(8,128)S(1)}, f32[136,256]{1,0:T(8,...) custom-call(bf16[256,4096]{1,0:T(8,128)(2,1)S(1)} %get-tuple-element.38.refs_0_.window, ...), custom_call_target="tpu_custom_call" | custom-call | flops 536870912 | bytes 7340032 | tf_op jit(solution)/shard_map/late/pallas_call | solution.py:32
  30.4 0.1 collective-permute-start.16
  30.5 0.5 collective-permute-start.23
  30.9 0.1 collective-permute-start.15
  31.0 0.8 %collective-permute-done.16 = f32[136,256]{1,0:T(8,128)S(1)} collective-permute-done((f32[136,256]{1,0:T(8,128)S(1)}, f32[136,256]{1,0:T(8,128)S(1)}, u32[]{:S(2)}, u32[]{:S(2)}) %collective-permute-start.16) | collective-permute-done | bytes 139296 | tf_op jit(solution)/shard_map/ppermute | solution.py:209
  31.8 1.6 %collective-permute-start.19 = (bf16[136,256]{1,0:T(8,128)(2,1)S(1)}, bf16[136,256]{1,0:T(8,128)(2,1)S(1)}, u32[]{:S(2)}, u32[]{:S(2)}) collective-permute-start(bf16[136,256]{1,0:T(8,128)(2,1)S(1)} %add.24), channel_id=1, source_target_pairs={{0,2},{1,3},{2,0},{3,1},{4,6},{5,7},{6,4},{7,5},{8,10},{9,11},{10,... | collective-permute-start | bytes 208904 | tf_op jit(solution)/shard_map/ppermute | solution.py:209
  33.5 0.0 collective-permute-done.23
  33.5 1.6 %collective-permute-start.24 = (bf16[128,256]{1,0:T(8,128)(2,1)S(1)}, bf16[128,256]{1,0:T(8,128)(2,1)S(1)}, u32[]{:S(2)}, u32[]{:S(2)}) collective-permute-start(bf16[128,256]{1,0:T(8,128)(2,1)S(1)} %add_convert_fusion.4), channel_id=1, source_target_pairs={{0,4},{1,5},{2,6},{3,7},{4,0},{5,1},{6,2},{7,3},{8,12},{9,13},{10,... | collective-permute-start | bytes 196616 | tf_op jit(solution)/shard_map/ppermute | solution.py:209
  35.1 0.4 collective-permute-start.17
  35.6 0.6 %collective-permute-done.19 = bf16[136,256]{1,0:T(8,128)(2,1)S(1)} collective-permute-done((bf16[136,256]{1,0:T(8,128)(2,1)S(1)}, bf16[136,256]{1,0:T(8,128)(2,1)S(1)}, u32[]{:S(2)}, u32[]{:S(2)}) %collective-permute-start.19) | collective-permute-done | bytes 69664 | tf_op jit(solution)/shard_map/ppermute | solution.py:209
  36.2 1.7 %collective-permute-start.20 = (bf16[136,256]{1,0:T(8,128)(2,1)S(1)}, bf16[136,256]{1,0:T(8,128)(2,1)S(1)}, u32[]{:S(2)}, u32[]{:S(2)}) collective-permute-start(bf16[136,256]{1,0:T(8,128)(2,1)S(1)} %add_convert_fusion.1), channel_id=1, source_target_pairs={{0,4},{1,5},{2,6},{3,7},{4,0},{5,1},{6,2},{7,3},{8,12},{9,13},{10,... | collective-permute-start | bytes 208904 | tf_op jit(solution)/shard_map/ppermute | solution.py:209
  37.9 0.0 collective-permute-done.24
  38.0 2.5 %collective-permute-start.25 = (bf16[128,256]{1,0:T(8,128)(2,1)S(1)}, bf16[128,256]{1,0:T(8,128)(2,1)S(1)}, u32[]{:S(2)}, u32[]{:S(2)}) collective-permute-start(bf16[128,256]{1,0:T(8,128)(2,1)S(1)} %add_convert_fusion.3), channel_id=1, source_target_pairs={{0,8},{1,9},{2,10},{3,11},{4,12},{5,13},{6,14},{7,15},{8,0},{9,1},... | collective-permute-start | bytes 196616 | tf_op jit(solution)/shard_map/ppermute | solution.py:209
  40.5 1.0 %collective-permute-done.20 = bf16[136,256]{1,0:T(8,128)(2,1)S(1)} collective-permute-done((bf16[136,256]{1,0:T(8,128)(2,1)S(1)}, bf16[136,256]{1,0:T(8,128)(2,1)S(1)}, u32[]{:S(2)}, u32[]{:S(2)}) %collective-permute-start.20) | collective-permute-done | bytes 69664 | tf_op jit(solution)/shard_map/ppermute | solution.py:209
  41.5 2.2 %collective-permute-start.21 = (bf16[136,256]{1,0:T(8,128)(2,1)S(1)}, bf16[136,256]{1,0:T(8,128)(2,1)S(1)}, u32[]{:S(2)}, u32[]{:S(2)}) collective-permute-start(bf16[136,256]{1,0:T(8,128)(2,1)S(1)} %add_convert_fusion), channel_id=1, source_target_pairs={{0,8},{1,9},{2,10},{3,11},{4,12},{5,13},{6,14},{7,15},{8,0},{9,1},... | collective-permute-start | bytes 208904 | tf_op jit(solution)/shard_map/ppermute | solution.py:209
  43.7 0.0 collective-permute-done.25
  43.7 2.3 %collective-permute-start.26 = (bf16[128,256]{1,0:T(8,128)(2,1)S(1)}, bf16[128,256]{1,0:T(8,128)(2,1)S(1)}, u32[]{:S(2)}, u32[]{:S(2)}) collective-permute-start(bf16[128,256]{1,0:T(8,128)(2,1)S(1)} %add_convert_fusion.2), channel_id=1, source_target_pairs={{0,2},{1,3},{2,0},{3,1},{4,6},{5,7},{6,4},{7,5},{8,10},{9,11},{10,... | collective-permute-start | bytes 196616 | tf_op jit(solution)/shard_map/ppermute | solution.py:209
  46.0 0.0 collective-permute-done.17.refs_6_
  46.0 0.4 rest.1
  46.4 0.1 collective-permute-start.18
  46.5 0.5 collective-permute-done.21
  47.0 0.1 collective-permute-start.22
  47.1 1.2 %collective-permute-done.26 = bf16[128,256]{1,0:T(8,128)(2,1)S(1)} collective-permute-done((bf16[128,256]{1,0:T(8,128)(2,1)S(1)}, bf16[128,256]{1,0:T(8,128)(2,1)S(1)}, u32[]{:S(2)}, u32[]{:S(2)}) %collective-permute-start.26) | collective-permute-done | bytes 65568 | tf_op jit(solution)/shard_map/ppermute | solution.py:209
  48.3 0.1 collective-permute-start.27
  48.3 0.0 collective-permute-done.15.received_one
  48.3 0.0 collective-permute-done.18.received_two
  48.4 0.0 copy-done
  48.4 1.0 %columns.1 = (bf16[256,256]{1,0:T(8,128)(2,1)}, bf16[256,256]{1,0:T(8,128)(2,1)}) custom-call(f32[256,256]{1,0:T(8,128)S(1)} %get-tuple-element.51.own_one, f32[256,256]{1,0:T(8,128)S(1)} %collective-permute-done.15.received_one, f32[256,256]{1,0:T(8,128)S(1)} %get-tuple-element.58.own_two, f32[256,256]{1,0:T(8,128)S(1)} %collective-permute-done.18.received_two, ...), custom_call_target="tpu_custom_call" | custom-call | bytes 1181696 | tf_op jit(solution)/shard_map/columns/pallas_call | solution.py:32
  49.4 0.0 collective-permute-done.22.pack_b
  49.4 0.3 collective-permute-done.27.cross_b
  49.7 0.0 copy-done.2
  49.7 1.3 %last.1 = (f32[256,256]{1,0:T(8,128)}, f32[256,256]{1,0:T(8,128)}, f32[256,256]{1,0:T(8,128)}) custom-call(f32[136,256]{1,0:T(8,128)S(1)} %convert_add_fusion.pack_a, f32[136,256]{1,0:T(8,128)S(1)} %collective-permute-done.22.pack_b, f32[128,256]{1,0:T(8,128)S(1)} %convert_add_fusion.1.cross_a, f32[128,256]{1,0:T(8,128)S(1)} %collective-permute-done.27.cross_b, ...), custom_call_target="tpu_custom_call" | custom-call | bytes 1196032 | tf_op jit(solution)/shard_map/last/pallas_call | solution.py:32
  (12 shorter events, 0.1 us)
Async XLA Ops:
  2.4 25.0 %collective-permute-start = (bf16[256,4096]{1,0:T(8,128)(2,1)S(1)}, bf16[256,4096]{1,0:T(8,128)(2,1)S(1)}, u32[]{:S(2)}, u32[]{:S(2)}) collective-permute-start(bf16[256,4096]{1,0:T(8,128)(2,1)S(1)} %get-tuple-element.38.refs_0_.window), channel_id=1, source_target_pairs={{0,1},{1,0},{2,3},{3,2},{4,5},{5,4},{6,7},{7,6},{8,9},{9,8},{10,11... | collective-permute-start | bytes 6291464 | tf_op jit(solution)/shard_map/ppermute | solution.py:209
  3.0 7.0 %collective-permute-start.6 = (bf16[256,256]{1,0:T(8,128)(2,1)S(1)}, bf16[256,256]{1,0:T(8,128)(2,1)S(1)}, u32[]{:S(2)}, u32[]{:S(2)}) collective-permute-start(bf16[256,256]{1,0:T(8,128)(2,1)S(1)} %get-tuple-element.39.refs_2_), channel_id=1, source_target_pairs={{4,0},{5,1},{8,4},{9,5},{12,8},{13,9},{14,12},{15,13},{10,14},{11,... | collective-permute-start | bytes 393224 | tf_op jit(solution)/shard_map/ppermute | solution.py:209
  5.5 6.3 %collective-permute-start.1 = (bf16[256,256]{1,0:T(8,128)(2,1)S(1)}, bf16[256,256]{1,0:T(8,128)(2,1)S(1)}, u32[]{:S(2)}, u32[]{:S(2)}) collective-permute-start(bf16[256,256]{1,0:T(8,128)(2,1)S(1)} %get-tuple-element.39.refs_2_), channel_id=1, source_target_pairs={{0,4},{1,5},{4,8},{5,9},{8,12},{9,13},{12,14},{13,15},{14,10},{15,... | collective-permute-start | bytes 393224 | tf_op jit(solution)/shard_map/ppermute | solution.py:209
  5.7 7.1 %collective-permute-start.9 = (bf16[256,256]{1,0:T(8,128)(2,1)S(1)}, bf16[256,256]{1,0:T(8,128)(2,1)S(1)}, u32[]{:S(2)}, u32[]{:S(2)}) collective-permute-start(bf16[256,256]{1,0:T(8,128)(2,1)S(1)} %get-tuple-element.40.refs_9_), channel_id=1, source_target_pairs={{4,0},{5,1},{8,4},{9,5},{12,8},{13,9},{14,12},{15,13},{10,14},{11,... | collective-permute-start | bytes 393224 | tf_op jit(solution)/shard_map/ppermute | solution.py:209
  7.6 7.1 %collective-permute-start.4 = (bf16[256,256]{1,0:T(8,128)(2,1)S(1)}, bf16[256,256]{1,0:T(8,128)(2,1)S(1)}, u32[]{:S(2)}, u32[]{:S(2)}) collective-permute-start(bf16[256,256]{1,0:T(8,128)(2,1)S(1)} %get-tuple-element.40.refs_9_), channel_id=1, source_target_pairs={{0,4},{1,5},{4,8},{5,9},{8,12},{9,13},{12,14},{13,15},{14,10},{15,... | collective-permute-start | bytes 393224 | tf_op jit(solution)/shard_map/ppermute | solution.py:209
  10.0 5.7 %collective-permute-start.7 = (bf16[256,256]{1,0:T(8,128)(2,1)S(1)}, bf16[256,256]{1,0:T(8,128)(2,1)S(1)}, u32[]{:S(2)}, u32[]{:S(2)}) collective-permute-start(bf16[256,256]{1,0:T(8,128)(2,1)S(1)} %collective-permute-done.6.refs_6_), channel_id=1, source_target_pairs={{4,0},{5,1},{8,4},{9,5},{12,8},{13,9},{14,12},{15,13},{10,14},{11,... | collective-permute-start | bytes 393224 | tf_op jit(solution)/shard_map/ppermute | solution.py:209
  11.9 5.7 %collective-permute-start.2 = (bf16[256,256]{1,0:T(8,128)(2,1)S(1)}, bf16[256,256]{1,0:T(8,128)(2,1)S(1)}, u32[]{:S(2)}, u32[]{:S(2)}) collective-permute-start(bf16[256,256]{1,0:T(8,128)(2,1)S(1)} %collective-permute-done.1.refs_3_), channel_id=1, source_target_pairs={{0,4},{1,5},{4,8},{5,9},{8,12},{9,13},{12,14},{13,15},{14,10},{15,... | collective-permute-start | bytes 393224 | tf_op jit(solution)/shard_map/ppermute | solution.py:209
  12.8 6.4 %collective-permute-start.10 = (bf16[256,256]{1,0:T(8,128)(2,1)S(1)}, bf16[256,256]{1,0:T(8,128)(2,1)S(1)}, u32[]{:S(2)}, u32[]{:S(2)}) collective-permute-start(bf16[256,256]{1,0:T(8,128)(2,1)S(1)} %collective-permute-done.9.refs_10_), channel_id=1, source_target_pairs={{4,0},{5,1},{8,4},{9,5},{12,8},{13,9},{14,12},{15,13},{10,14},{11,... | collective-permute-start | bytes 393224 | tf_op jit(solution)/shard_map/ppermute | solution.py:209
  14.7 13.7 %collective-permute-start.12 = (bf16[768,256]{1,0:T(8,128)(2,1)S(1)}, bf16[768,256]{1,0:T(8,128)(2,1)S(1)}, u32[]{:S(2)}, u32[]{:S(2)}) collective-permute-start(bf16[768,256]{1,0:T(8,128)(2,1)S(1)} %get-tuple-element.50.rest_8_), channel_id=1, source_target_pairs={{0,1},{1,0},{2,3},{3,2},{4,5},{5,4},{6,7},{7,6},{8,9},{9,8},{10,11... | collective-permute-start | bytes 1179656 | tf_op jit(solution)/shard_map/ppermute | solution.py:209
  15.6 6.4 %collective-permute-start.5 = (bf16[256,256]{1,0:T(8,128)(2,1)S(1)}, bf16[256,256]{1,0:T(8,128)(2,1)S(1)}, u32[]{:S(2)}, u32[]{:S(2)}) collective-permute-start(bf16[256,256]{1,0:T(8,128)(2,1)S(1)} %collective-permute-done.4.refs_4_), channel_id=1, source_target_pairs={{0,4},{1,5},{4,8},{5,9},{8,12},{9,13},{12,14},{13,15},{14,10},{15,... | collective-permute-start | bytes 393224 | tf_op jit(solution)/shard_map/ppermute | solution.py:209
  17.6 5.9 %collective-permute-start.3 = (bf16[256,256]{1,0:T(8,128)(2,1)S(1)}, bf16[256,256]{1,0:T(8,128)(2,1)S(1)}, u32[]{:S(2)}, u32[]{:S(2)}) collective-permute-start(bf16[256,256]{1,0:T(8,128)(2,1)S(1)} %collective-permute-done.2.refs_4_), channel_id=1, source_target_pairs={{0,4},{1,5},{4,8},{5,9},{8,12},{9,13},{12,14},{13,15},{14,10},{15,... | collective-permute-start | bytes 393224 | tf_op jit(solution)/shard_map/ppermute | solution.py:209
  19.2 5.2 %collective-permute-start.11 = (bf16[256,256]{1,0:T(8,128)(2,1)S(1)}, bf16[256,256]{1,0:T(8,128)(2,1)S(1)}, u32[]{:S(2)}, u32[]{:S(2)}) collective-permute-start(bf16[256,256]{1,0:T(8,128)(2,1)S(1)} %collective-permute-done.10.refs_11_), channel_id=1, source_target_pairs={{4,0},{5,1},{8,4},{9,5},{12,8},{13,9},{14,12},{15,13},{10,14},{11,... | collective-permute-start | bytes 393224 | tf_op jit(solution)/shard_map/ppermute | solution.py:209
  22.0 5.5 %collective-permute-start.8 = (bf16[256,256]{1,0:T(8,128)(2,1)S(1)}, bf16[256,256]{1,0:T(8,128)(2,1)S(1)}, u32[]{:S(2)}, u32[]{:S(2)}) collective-permute-start(bf16[256,256]{1,0:T(8,128)(2,1)S(1)} %collective-permute-done.7.refs_7_), channel_id=1, source_target_pairs={{4,0},{5,1},{8,4},{9,5},{12,8},{13,9},{14,12},{15,13},{10,14},{11,... | collective-permute-start | bytes 393224 | tf_op jit(solution)/shard_map/ppermute | solution.py:209
  23.6 5.0 %collective-permute-start.13 = (bf16[256,256]{1,0:T(8,128)(2,1)S(1)}, bf16[256,256]{1,0:T(8,128)(2,1)S(1)}, u32[]{:S(2)}, u32[]{:S(2)}) collective-permute-start(bf16[256,256]{1,0:T(8,128)(2,1)S(1)} %collective-permute-done.3.refs_5_), channel_id=1, source_target_pairs={{0,4},{1,5},{4,8},{5,9},{8,12},{9,13},{12,14},{13,15},{14,10},{15,... | collective-permute-start | bytes 393224 | tf_op jit(solution)/shard_map/ppermute | solution.py:209
  24.4 5.0 %collective-permute-start.14 = (bf16[256,256]{1,0:T(8,128)(2,1)S(1)}, bf16[256,256]{1,0:T(8,128)(2,1)S(1)}, u32[]{:S(2)}, u32[]{:S(2)}) collective-permute-start(bf16[256,256]{1,0:T(8,128)(2,1)S(1)} %collective-permute-done.11.refs_12_), channel_id=1, source_target_pairs={{4,0},{5,1},{8,4},{9,5},{12,8},{13,9},{14,12},{15,13},{10,14},{11,... | collective-permute-start | bytes 393224 | tf_op jit(solution)/shard_map/ppermute | solution.py:209
  30.4 1.4 %collective-permute-start.16 = (f32[136,256]{1,0:T(8,128)S(1)}, f32[136,256]{1,0:T(8,128)S(1)}, u32[]{:S(2)}, u32[]{:S(2)}) collective-permute-start(f32[136,256]{1,0:T(8,128)S(1)} %get-tuple-element.56), channel_id=1, source_target_pairs={{0,1},{1,0},{2,3},{3,2},{4,5},{5,4},{6,7},{7,6},{8,9},{9,8},{10,11... | collective-permute-start | bytes 417800 | tf_op jit(solution)/shard_map/ppermute | solution.py:209
  30.5 3.0 %collective-permute-start.23 = (f32[128,256]{1,0:T(8,128)S(1)}, f32[128,256]{1,0:T(8,128)S(1)}, u32[]{:S(2)}, u32[]{:S(2)}) collective-permute-start(f32[128,256]{1,0:T(8,128)S(1)} %get-tuple-element.66), channel_id=1, source_target_pairs={{0,1},{1,0},{2,3},{3,2},{4,5},{5,4},{6,7},{7,6},{8,9},{9,8},{10,11... | collective-permute-start | bytes 393224 | tf_op jit(solution)/shard_map/ppermute | solution.py:209
  30.9 17.4 %collective-permute-start.15 = (f32[256,256]{1,0:T(8,128)S(1)}, f32[256,256]{1,0:T(8,128)S(1)}, u32[]{:S(2)}, u32[]{:S(2)}) collective-permute-start(f32[256,256]{1,0:T(8,128)S(1)} %get-tuple-element.52), channel_id=1, source_target_pairs={{0,1},{1,0},{2,3},{3,2},{4,5},{5,4},{6,7},{7,6},{8,9},{9,8},{10,11... | collective-permute-start | bytes 786440 | tf_op jit(solution)/shard_map/ppermute | solution.py:209
  31.8 4.4 %collective-permute-start.19 = (bf16[136,256]{1,0:T(8,128)(2,1)S(1)}, bf16[136,256]{1,0:T(8,128)(2,1)S(1)}, u32[]{:S(2)}, u32[]{:S(2)}) collective-permute-start(bf16[136,256]{1,0:T(8,128)(2,1)S(1)} %add.24), channel_id=1, source_target_pairs={{0,2},{1,3},{2,0},{3,1},{4,6},{5,7},{6,4},{7,5},{8,10},{9,11},{10,... | collective-permute-start | bytes 208904 | tf_op jit(solution)/shard_map/ppermute | solution.py:209
  33.5 4.5 %collective-permute-start.24 = (bf16[128,256]{1,0:T(8,128)(2,1)S(1)}, bf16[128,256]{1,0:T(8,128)(2,1)S(1)}, u32[]{:S(2)}, u32[]{:S(2)}) collective-permute-start(bf16[128,256]{1,0:T(8,128)(2,1)S(1)} %add_convert_fusion.4), channel_id=1, source_target_pairs={{0,4},{1,5},{2,6},{3,7},{4,0},{5,1},{6,2},{7,3},{8,12},{9,13},{10,... | collective-permute-start | bytes 196616 | tf_op jit(solution)/shard_map/ppermute | solution.py:209
  35.1 10.9 %collective-permute-start.17 = (bf16[256,256]{1,0:T(8,128)(2,1)S(1)}, bf16[256,256]{1,0:T(8,128)(2,1)S(1)}, u32[]{:S(2)}, u32[]{:S(2)}) collective-permute-start(bf16[256,256]{1,0:T(8,128)(2,1)S(1)} %collective-permute-done.5.refs_5_), channel_id=1, source_target_pairs={{0,4},{1,5},{4,8},{5,9},{8,12},{9,13},{12,14},{13,15},{14,10},{15,... | collective-permute-start | bytes 393224 | tf_op jit(solution)/shard_map/ppermute | solution.py:209
  36.2 5.3 %collective-permute-start.20 = (bf16[136,256]{1,0:T(8,128)(2,1)S(1)}, bf16[136,256]{1,0:T(8,128)(2,1)S(1)}, u32[]{:S(2)}, u32[]{:S(2)}) collective-permute-start(bf16[136,256]{1,0:T(8,128)(2,1)S(1)} %add_convert_fusion.1), channel_id=1, source_target_pairs={{0,4},{1,5},{2,6},{3,7},{4,0},{5,1},{6,2},{7,3},{8,12},{9,13},{10,... | collective-permute-start | bytes 208904 | tf_op jit(solution)/shard_map/ppermute | solution.py:209
  38.0 5.7 %collective-permute-start.25 = (bf16[128,256]{1,0:T(8,128)(2,1)S(1)}, bf16[128,256]{1,0:T(8,128)(2,1)S(1)}, u32[]{:S(2)}, u32[]{:S(2)}) collective-permute-start(bf16[128,256]{1,0:T(8,128)(2,1)S(1)} %add_convert_fusion.3), channel_id=1, source_target_pairs={{0,8},{1,9},{2,10},{3,11},{4,12},{5,13},{6,14},{7,15},{8,0},{9,1},... | collective-permute-start | bytes 196616 | tf_op jit(solution)/shard_map/ppermute | solution.py:209
  41.5 5.4 %collective-permute-start.21 = (bf16[136,256]{1,0:T(8,128)(2,1)S(1)}, bf16[136,256]{1,0:T(8,128)(2,1)S(1)}, u32[]{:S(2)}, u32[]{:S(2)}) collective-permute-start(bf16[136,256]{1,0:T(8,128)(2,1)S(1)} %add_convert_fusion), channel_id=1, source_target_pairs={{0,8},{1,9},{2,10},{3,11},{4,12},{5,13},{6,14},{7,15},{8,0},{9,1},... | collective-permute-start | bytes 208904 | tf_op jit(solution)/shard_map/ppermute | solution.py:209
  43.7 4.5 %collective-permute-start.26 = (bf16[128,256]{1,0:T(8,128)(2,1)S(1)}, bf16[128,256]{1,0:T(8,128)(2,1)S(1)}, u32[]{:S(2)}, u32[]{:S(2)}) collective-permute-start(bf16[128,256]{1,0:T(8,128)(2,1)S(1)} %add_convert_fusion.2), channel_id=1, source_target_pairs={{0,2},{1,3},{2,0},{3,1},{4,6},{5,7},{6,4},{7,5},{8,10},{9,11},{10,... | collective-permute-start | bytes 196616 | tf_op jit(solution)/shard_map/ppermute | solution.py:209
  46.0 2.4 %copy-start = (bf16[256,256]{1,0:T(8,128)(2,1)S(1)}, bf16[256,256]{1,0:T(8,128)(2,1)}, u32[]{:S(2)}) copy-start(bf16[256,256]{1,0:T(8,128)(2,1)} %cross.3) | copy-start | bytes 393220
  46.0 3.7 %copy-start.1 = (f32[256,256]{1,0:T(8,128)S(1)}, f32[256,256]{1,0:T(8,128)}, u32[]{:S(2)}) copy-start(f32[256,256]{1,0:T(8,128)} %diag_one.1) | copy-start | bytes 786436
  46.0 3.7 %copy-start.2 = (f32[256,256]{1,0:T(8,128)S(1)}, f32[256,256]{1,0:T(8,128)}, u32[]{:S(2)}) copy-start(f32[256,256]{1,0:T(8,128)} %diag_two.1) | copy-start | bytes 786436
  46.4 2.0 %collective-permute-start.18 = (f32[256,256]{1,0:T(8,128)S(1)}, f32[256,256]{1,0:T(8,128)S(1)}, u32[]{:S(2)}, u32[]{:S(2)}) collective-permute-start(f32[256,256]{1,0:T(8,128)S(1)} %get-tuple-element.59), channel_id=1, source_target_pairs={{0,1},{1,0},{2,3},{3,2},{4,5},{5,4},{6,7},{7,6},{8,9},{9,8},{10,11... | collective-permute-start | bytes 786440 | tf_op jit(solution)/shard_map/ppermute | solution.py:209
  47.0 2.4 %collective-permute-start.22 = (f32[136,256]{1,0:T(8,128)S(1)}, f32[136,256]{1,0:T(8,128)S(1)}, u32[]{:S(2)}, u32[]{:S(2)}) collective-permute-start(f32[136,256]{1,0:T(8,128)S(1)} %convert_add_fusion.pack_a), channel_id=1, source_target_pairs={{0,1},{1,0},{2,3},{3,2},{4,5},{5,4},{6,7},{7,6},{8,9},{9,8},{10,11... | collective-permute-start | bytes 417800 | tf_op jit(solution)/shard_map/ppermute | solution.py:209
  48.3 1.4 %collective-permute-start.27 = (f32[128,256]{1,0:T(8,128)S(1)}, f32[128,256]{1,0:T(8,128)S(1)}, u32[]{:S(2)}, u32[]{:S(2)}) collective-permute-start(f32[128,256]{1,0:T(8,128)S(1)} %convert_add_fusion.1.cross_a), channel_id=1, source_target_pairs={{0,1},{1,0},{2,3},{3,2},{4,5},{5,4},{6,7},{7,6},{8,9},{9,8},{10,11... | collective-permute-start | bytes 393224 | tf_op jit(solution)/shard_map/ppermute | solution.py:209

commit v6 on v5

--- a/solution.py
+++ b/solution.py
@@ -27,14 +27,14 @@
     return high, (x - high.astype(F32)).astype(BF16)
 
 
-def call(body, name, outs, args, n_smem=0, flops=0, aliases=None, specs=None, scratch=()):
+def call(body, name, outs, args, n_smem=0, flops=0, aliases=None, specs=None, scratch=(), out_spec=VMEM):
     size = sum(a.size * a.dtype.itemsize for a in args)
     return pl.pallas_call(
         body,
         name=name,
         out_shape=tuple(jax.ShapeDtypeStruct(s, d) for s, d in outs),
         in_specs=specs or [SMEM] * n_smem + [VMEM] * (len(args) - n_smem),
-        out_specs=tuple(VMEM for _ in outs),
+        out_specs=tuple(out_spec for _ in outs),
         input_output_aliases=aliases or {},
         scratch_shapes=scratch,
         compiler_params=pltpu.CompilerParams(vmem_limit_bytes=16 << 20),
@@ -55,14 +55,20 @@
     return pltpu.with_memory_space_constraint(x, pltpu.HBM)
 
 
+def load_body(window, out, sem):
+    copy = pltpu.make_async_copy(window, out, sem)
+    copy.start()
+    copy.wait()
+
+
 def diagonal_of(weight):
     n = weight.shape[1]
     on = lax.broadcasted_iota(jnp.int32, (n, n), 0) == lax.broadcasted_iota(jnp.int32, (n, n), 1)
     return jnp.where(on, jnp.broadcast_to(weight, (n, n)), 0.0).astype(BF16)
 
 
-def mask_body(table, rows, one, two, window, m_one, m_two, stack, weights, window_v, table_v, rows_v, one_v, two_v, sems):
-    moves = (table, table_v), (rows, rows_v), (one, one_v), (two, two_v), (window, window_v)
+def mask_body(table, rows, one, two, m_one, m_two, stack, weights, table_v, rows_v, one_v, two_v, sems):
+    moves = (table, table_v), (rows, rows_v), (one, one_v), (two, two_v)
     copies = [pltpu.make_async_copy(src, dst, sems.at[i]) for i, (src, dst) in enumerate(moves)]
     for copy in copies:
         copy.start()
@@ -80,8 +86,7 @@
         value = dot(chosen, panel[...]).astype(BF16)
         masked[...] = value
         stack[which * n : (which + 1) * n] = value
-    stack[2 * n :] = dot(diagonal_of(weights[0:1]), m_two[...]).astype(BF16)
-    copies[4].wait()
+    stack[2 * n :] = jnp.broadcast_to(weights[0:1], (stack.shape[0] - 2 * n, n)).astype(BF16)
 
 
 def product(offset, window, swapped, piece):
@@ -103,7 +108,7 @@
     return total
 
 
-def early_body(window, swapped, one, up, down, two, back, *outs):
+def early_body(window, swapped, stack, sibling, one, up, down, two, back, *outs):
     zero = (jnp.zeros(one.shape, F32),) * 2
     own = product(0, window, swapped, one)
     side = plus(add_products(zero, up, window, swapped), own, 0.5)
@@ -111,31 +116,34 @@
     own = product(0, window, swapped, two)
     side_two = plus(add_products(zero, back, window, swapped), own, 0.5)
     whole_two = plus(side_two, own, 0.5)
-    for out, value in zip(outs, (*side, *whole, *side_two, *whole_two), strict=True):
+    for out, value in zip(outs[:8], (*side, *whole, *side_two, *whole_two), strict=True):
         out[...] = value
-
-
-def gram(stack, sibling, which, images):
+    n = one.shape[0]
+    for out, panel in zip(outs[8:], (stack, sibling), strict=True):
+        weight = panel[2 * n :][:1].astype(F32)
+        out[...] = dot(diagonal_of(weight), panel[n : 2 * n]).astype(BF16)
+
+
+def gram(panels, images):
     (a, b), (c, d) = halves(images[0]), halves(images[1])
-    n = images[0].shape[0]
-    mine, sibling = (x[which * n : (which + 1) * n] for x in (stack, sibling))
+    mine, sibling = panels
     return (dot_t(mine, a) + dot_t(sibling, c)) + (dot_t(mine, b) + dot_t(sibling, d))
 
 
 def late_body(steps, window, swapped, *rest):
-    sums, (stack, sibling, one, two), outs, parts = rest[:8], rest[8:12], rest[12:16], rest[16:]
+    sums, twice, (stack, sibling, one, two), outs, parts = rest[:8], rest[8:10], rest[10:14], rest[14:18], rest[18:]
     sums = [(sums[i][...], sums[i + 1][...]) for i in range(0, 8, 2)]
     far = product(-steps, window, swapped, one)
     image_one = plus(sums[1], far)
-    first = gram(stack, sibling, 0, plus(sums[0], far, 0.5))
+    n = stack.shape[1]
+    first = gram([x[:n] for x in (stack, sibling)], plus(sums[0], far, 0.5))
     far = product(steps, window, swapped, two)
     image_two = plus(sums[3], far)
-    second = gram(stack, sibling, 1, plus(sums[2], far, 0.5))
-    cross = -gram(stack, sibling, 2, image_one)
+    second = gram([x[n : 2 * n] for x in (stack, sibling)], plus(sums[2], far, 0.5))
+    cross = -gram([x[...] for x in twice], image_one)
     for out, value in zip(outs, (*image_one, *image_two), strict=True):
         out[...] = value
 
-    n = first.shape[0]
     half = n // 2
     row = lax.broadcasted_iota(jnp.int32, (n, n), 0)
     col = lax.broadcasted_iota(jnp.int32, (n, n), 1)
@@ -166,7 +174,7 @@
     column_two[...] = (-(row_weights(weights, 1) * (image + dot(rounded, cross[...])))).astype(BF16)
 
 
-def last_body(pack_a, pack_b, cross_a, cross_b, cross, diag_one, diag_two, block_one, edge, block_two):
+def last_body(pack_a, pack_b, cross_a, cross_b, cross, diag_one, diag_two, block_one, edge, block_two, *held):
     n = cross.shape[0]
     half = n // 2
     first = lax.axis_index(AXIS) % 2 == 0
@@ -182,16 +190,28 @@
     s_one = jnp.where(row <= col, packed, turned)
     s_two = jnp.where(row > col, packed, turned)
     s_two = jnp.where(row == col, jnp.broadcast_to(diagonal, (n, n)), s_two)
+    c = cross[...]
+    *values, sems = held
+    copies = [
+        pltpu.make_async_copy(value, out, sems.at[i])
+        for i, (value, out) in enumerate(zip(values, (block_one, edge, block_two), strict=True))
+    ]
+
+    one = diag_one[...] + s_one
+    values[0][...] = one
+    copies[0].start()
+    a, b = halves(one)
+    moved = dot(a, c) + dot(b, c)
     cross_sum = whole(cross_a[...], cross_b[...])
-    c = cross[...]
-    one = diag_one[...] + s_one
-    block_one[...] = one
-    a, b = halves(one)
-    out = -(cross_sum.T + (dot(a, c) + dot(b, c)))
-    edge[...] = out
-    a, b = halves(out)
+    values[1][...] = -(cross_sum.T + moved)
+    copies[1].start()
+    a, b = halves(moved)
     d, e = halves(cross_sum)
-    block_two[...] = diag_two[...] + s_two + (dot(d, c) + dot(e, c)) - (dot_t(c, a) + dot_t(c, b))
+    bent = dot(d, c) + dot(e, c)
+    values[2][...] = diag_two[...] + s_two + (bent + bent.T) + (dot_t(c, a) + dot_t(c, b))
+    copies[2].start()
+    for copy in copies:
+        copy.wait()
 
 
 def local(
@@ -210,18 +230,18 @@
 
     square = ((rows, width), F32)
     tile = ((rows, width), BF16)
-    m_one, m_two, stack, weights, window = call(
+    m_one, m_two, stack, weights = call(
         mask_body,
         "mask",
-        (tile, tile, ((3 * rows, width), BF16), ((2, rows), F32), (inverse_window.shape, BF16)),
-        tuple(map(in_hbm, (struct_mask, row_super.reshape(1, -1), panel_one, panel_two, inverse_window))),
-        specs=[HBM] * 5,
+        (tile, tile, ((2 * rows + 16, rows), BF16), ((2, rows), F32)),
+        tuple(map(in_hbm, (struct_mask, row_super.reshape(1, -1), panel_one, panel_two))),
+        specs=[HBM] * 4,
         scratch=[
             pltpu.SMEM(struct_mask.shape, jnp.int32),
             pltpu.VMEM((1, rows), jnp.int32),
             pltpu.VMEM((rows, width), BF16),
             pltpu.VMEM((rows, width), BF16),
-            pltpu.SemaphoreType.DMA((5,)),
+            pltpu.SemaphoreType.DMA((4,)),
         ],
     )
 
@@ -235,12 +255,21 @@
             two_up.append(send(two_up[-1], ahead))
     one_far = send(one_up[-1], ahead)
     two_far = send(two_down[-1], back)
-    swapped = send(window, flip[0])
+    late_window, *_ = lax.optimization_barrier((inverse_window, one_up[1], one_down[1], two_up[1], two_down[1]))
+    (window,) = call(
+        load_body,
+        "load",
+        ((inverse_window.shape, BF16),),
+        (in_hbm(late_window),),
+        specs=[HBM],
+        scratch=[pltpu.SemaphoreType.DMA(())],
+    )
+    swapped = send(inverse_window, flip[0])
     sibling = send(stack, flip[0])
 
     def early_refs(*refs):
         inputs, outs = refs[: len(early_in)], refs[len(early_in) :]
-        fixed, pieces = inputs[:2], inputs[2:]
+        fixed, pieces = inputs[:4], inputs[4:]
         n = steps - 1
         one, up, down = pieces[0], pieces[1 : 1 + n], pieces[1 + n : 1 + 2 * n]
         two, behind = pieces[1 + 2 * n], pieces[2 + 2 * n :]
@@ -256,13 +285,13 @@
 
     one_up[-1], *_ = lax.optimization_barrier((one_up[-1], *two_up))
     early_in = (
-        *(window, swapped),
+        *(window, swapped, stack, sibling),
         *one_up,
         *one_down[1:],
         *two_down,
     )
     block_flops = 4 * rows * width * width
-    early = call(early_refs, "early", (square,) * 8, early_in, flops=block_flops * (3 * steps + 1))
+    early = call(early_refs, "early", (square,) * 8 + (tile,) * 2, early_in, flops=block_flops * (3 * steps + 1))
     packed = ((half + 8, width), F32)
     crossed = ((half, width), F32)
     own_one, other_one, own_two, other_two, keep_p, away_p, keep_x, away_x = call(
@@ -310,6 +339,8 @@
         "last",
         (full, full, full),
         (pack_a, pack_b, cross_a, cross_b, cross_block, diag_one, diag_two),
+        scratch=[pltpu.VMEM((width, width), F32)] * 3 + [pltpu.SemaphoreType.DMA((3,))],
+        out_spec=HBM,
     )
     return column_one, block_one, column_two, edge_block, block_two
 

time: 51.1 us -> 50.7 us (level)
  waiting for transfers between devices: 13.2 us -> 11.3 us
  Pallas kernels: 6.41 us -> 7.67 us
    ppermute x28, waiting for transfers between devices: 13.2 us -> 11.3 us  [send(): return lax.ppermute(x, AXIS, perm)]
    pallas_call x6 -> x7, Pallas kernels: 6.41 us -> 7.67 us  [call(): pl.pallas_call(body, name=name, out_shape=tuple((jax.ShapeDtypeStruct(s,...]
  transfers between devices with their start and end apart: 28 -> 28, of which waited for: 14 -> 12; matrix products, arithmetic and copies ran while one was open for 0% -> 0% of each run, Pallas kernels for 5% -> 11%
where the time goes in v6:
time: 50.7 us; the launch traced here: 50.6 us
  starting transfers between devices  30.6 us (60%)
  waiting for transfers between devices  11.3 us (22%)
  Pallas kernels  7.67 us (15%)
  between operations  0.82 us (2%)
    ppermute x28, starting transfers between devices, send(): return lax.ppermute(x, AXIS, perm)  30.6 us
    ppermute x28, waiting for transfers between devices, send(): return lax.ppermute(x, AXIS, perm)  11.3 us
    pallas_call x7, Pallas kernels, call(): pl.pallas_call(body, name=name, out_shape=tuple((jax.ShapeDtypeStruct(s,...  7.67 us
  transfers between devices with their start and end apart: 28, of which 12 were waited for; matrix products, arithmetic and copies ran while one was open for 0% of the time, Pallas kernels for 11%

profile of v6, /device:TPU:0, one launch (start us, length us, event | category | flops | bytes accessed | tf_op | source)
XLA Modules:
  0.0 50.6 jit_solution(2101249531927423773)
XLA Ops:
  0.6 0.5 %collective-permute-start.4 = (bf16[256,4096]{1,0:T(8,128)(2,1)}, bf16[256,4096]{1,0:T(8,128)(2,1)S(1)}, u32[]{:S(2)}, u32[]{:S(2)}) collective-permute-start(bf16[256,4096]{1,0:T(8,128)(2,1)} %window), channel_id=1, source_target_pairs={{0,1},{1,0},{2,3},{3,2},{4,5},{5,4},{6,7},{7,6},{8,9},{9,8},{10,11... | collective-permute-start | bytes 6291464 | tf_op jit(solution)/shard_map/ppermute | solution.py:229
  1.2 1.4 %mask.1 = (bf16[256,256]{1,0:T(8,128)(2,1)S(1)}, bf16[256,256]{1,0:T(8,128)(2,1)S(1)}, bf16[528,256]{1,0:T(8,128)(2,1)S(1)}, f32[2,256]{1,0:T(2,128)S(1)}) custom-call(s32[2,16]{1,0:T(2,128)} %table.1, s32[1,256]{1,0:T(1,128)} %bitcast.1, bf16[256,256]{1,0:T(8,128)(2,1)} %one.1, bf16[256,256]{1,0:T(8,128)(2,1)} %two.1), custom_call_target="tpu_custom_call" | custom-call | bytes 263296 | tf_op jit(solution)/shard_map/mask/pallas_call | solution.py:32
  2.5 2.6 %collective-permute-start.1 = (bf16[256,256]{1,0:T(8,128)(2,1)S(1)}, bf16[256,256]{1,0:T(8,128)(2,1)S(1)}, u32[]{:S(2)}, u32[]{:S(2)}) collective-permute-start(bf16[256,256]{1,0:T(8,128)(2,1)S(1)} %get-tuple-element.40.refs_4_), channel_id=1, source_target_pairs={{4,0},{5,1},{8,4},{9,5},{12,8},{13,9},{14,12},{15,13},{10,14},{11,... | collective-permute-start | bytes 393224 | tf_op jit(solution)/shard_map/ppermute | solution.py:229
  5.1 0.1 collective-permute-start
  5.3 1.9 %collective-permute-start.3 = (bf16[256,256]{1,0:T(8,128)(2,1)S(1)}, bf16[256,256]{1,0:T(8,128)(2,1)S(1)}, u32[]{:S(2)}, u32[]{:S(2)}) collective-permute-start(bf16[256,256]{1,0:T(8,128)(2,1)S(1)} %get-tuple-element.41.refs_11_), channel_id=1, source_target_pairs={{4,0},{5,1},{8,4},{9,5},{12,8},{13,9},{14,12},{15,13},{10,14},{11,... | collective-permute-start | bytes 393224 | tf_op jit(solution)/shard_map/ppermute | solution.py:229
  7.2 0.1 collective-permute-start.2
  7.3 2.3 %collective-permute-done.1.refs_8_ = bf16[256,256]{1,0:T(8,128)(2,1)S(1)} collective-permute-done((bf16[256,256]{1,0:T(8,128)(2,1)S(1)}, bf16[256,256]{1,0:T(8,128)(2,1)S(1)}, u32[]{:S(2)}, u32[]{:S(2)}) %collective-permute-start.1) | collective-permute-done | bytes 131104 | tf_op jit(solution)/shard_map/ppermute | solution.py:229
  9.5 1.9 %collective-permute-start.9 = (bf16[256,256]{1,0:T(8,128)(2,1)S(1)}, bf16[256,256]{1,0:T(8,128)(2,1)S(1)}, u32[]{:S(2)}, u32[]{:S(2)}) collective-permute-start(bf16[256,256]{1,0:T(8,128)(2,1)S(1)} %collective-permute-done.1.refs_8_), channel_id=1, source_target_pairs={{4,0},{5,1},{8,4},{9,5},{12,8},{13,9},{14,12},{15,13},{10,14},{11,... | collective-permute-start | bytes 393224 | tf_op jit(solution)/shard_map/ppermute | solution.py:229
  11.4 0.0 collective-permute-done.refs_5_
  11.5 0.1 collective-permute-start.6
  11.6 0.8 %collective-permute-done.3.refs_12_ = bf16[256,256]{1,0:T(8,128)(2,1)S(1)} collective-permute-done((bf16[256,256]{1,0:T(8,128)(2,1)S(1)}, bf16[256,256]{1,0:T(8,128)(2,1)S(1)}, u32[]{:S(2)}, u32[]{:S(2)}) %collective-permute-start.3) | collective-permute-done | bytes 131104 | tf_op jit(solution)/shard_map/ppermute | solution.py:229
  12.3 1.9 %collective-permute-start.11 = (bf16[256,256]{1,0:T(8,128)(2,1)S(1)}, bf16[256,256]{1,0:T(8,128)(2,1)S(1)}, u32[]{:S(2)}, u32[]{:S(2)}) collective-permute-start(bf16[256,256]{1,0:T(8,128)(2,1)S(1)} %collective-permute-done.3.refs_12_), channel_id=1, source_target_pairs={{4,0},{5,1},{8,4},{9,5},{12,8},{13,9},{14,12},{15,13},{10,14},{11,... | collective-permute-start | bytes 393224 | tf_op jit(solution)/shard_map/ppermute | solution.py:229
  14.2 0.0 collective-permute-done.2.refs_4_
  14.2 0.0 collective-permute-start.5
  14.2 1.0 %collective-permute-done.9.refs_9_ = bf16[256,256]{1,0:T(8,128)(2,1)S(1)} collective-permute-done((bf16[256,256]{1,0:T(8,128)(2,1)S(1)}, bf16[256,256]{1,0:T(8,128)(2,1)S(1)}, u32[]{:S(2)}, u32[]{:S(2)}) %collective-permute-start.9) | collective-permute-done | bytes 131104 | tf_op jit(solution)/shard_map/ppermute | solution.py:229
  15.2 2.0 %collective-permute-start.8 = (bf16[256,256]{1,0:T(8,128)(2,1)S(1)}, bf16[256,256]{1,0:T(8,128)(2,1)S(1)}, u32[]{:S(2)}, u32[]{:S(2)}) collective-permute-start(bf16[256,256]{1,0:T(8,128)(2,1)S(1)} %collective-permute-done.2.refs_4_), channel_id=1, source_target_pairs={{0,4},{1,5},{4,8},{5,9},{8,12},{9,13},{12,14},{13,15},{14,10},{15,... | collective-permute-start | bytes 393224 | tf_op jit(solution)/shard_map/ppermute | solution.py:229
  17.2 0.0 collective-permute-done.6.refs_6_
  17.2 1.6 %collective-permute-start.7 = (bf16[256,256]{1,0:T(8,128)(2,1)S(1)}, bf16[256,256]{1,0:T(8,128)(2,1)S(1)}, u32[]{:S(2)}, u32[]{:S(2)}) collective-permute-start(bf16[256,256]{1,0:T(8,128)(2,1)S(1)} %collective-permute-done.6.refs_6_), channel_id=1, source_target_pairs={{0,4},{1,5},{4,8},{5,9},{8,12},{9,13},{12,14},{13,15},{14,10},{15,... | collective-permute-start | bytes 393224 | tf_op jit(solution)/shard_map/ppermute | solution.py:229
  18.8 0.0 collective-permute-done.11.refs_13_
  18.8 0.7 %collective-permute-start.12 = (bf16[256,256]{1,0:T(8,128)(2,1)S(1)}, bf16[256,256]{1,0:T(8,128)(2,1)S(1)}, u32[]{:S(2)}, u32[]{:S(2)}) collective-permute-start(bf16[256,256]{1,0:T(8,128)(2,1)S(1)} %collective-permute-done.11.refs_13_), channel_id=1, source_target_pairs={{4,0},{5,1},{8,4},{9,5},{12,8},{13,9},{14,12},{15,13},{10,14},{11,... | collective-permute-start | bytes 393224 | tf_op jit(solution)/shard_map/ppermute | solution.py:229
  19.5 2.1 %collective-permute-done.8.refs_5_ = bf16[256,256]{1,0:T(8,128)(2,1)S(1)} collective-permute-done((bf16[256,256]{1,0:T(8,128)(2,1)S(1)}, bf16[256,256]{1,0:T(8,128)(2,1)S(1)}, u32[]{:S(2)}, u32[]{:S(2)}) %collective-permute-start.8) | collective-permute-done | bytes 131104 | tf_op jit(solution)/shard_map/ppermute | solution.py:229
  21.6 1.6 %collective-permute-start.10 = (bf16[256,256]{1,0:T(8,128)(2,1)S(1)}, bf16[256,256]{1,0:T(8,128)(2,1)S(1)}, u32[]{:S(2)}, u32[]{:S(2)}) collective-permute-start(bf16[256,256]{1,0:T(8,128)(2,1)S(1)} %collective-permute-done.9.refs_9_), channel_id=1, source_target_pairs={{4,0},{5,1},{8,4},{9,5},{12,8},{13,9},{14,12},{15,13},{10,14},{11,... | collective-permute-start | bytes 393224 | tf_op jit(solution)/shard_map/ppermute | solution.py:229
  23.1 0.0 collective-permute-done.7.refs_7_
  23.1 0.7 %collective-permute-start.13 = (bf16[256,256]{1,0:T(8,128)(2,1)S(1)}, bf16[256,256]{1,0:T(8,128)(2,1)S(1)}, u32[]{:S(2)}, u32[]{:S(2)}) collective-permute-start(bf16[256,256]{1,0:T(8,128)(2,1)S(1)} %collective-permute-done.7.refs_7_), channel_id=1, source_target_pairs={{0,4},{1,5},{4,8},{5,9},{8,12},{9,13},{12,14},{13,15},{14,10},{15,... | collective-permute-start | bytes 393224 | tf_op jit(solution)/shard_map/ppermute | solution.py:229
  23.8 0.2 collective-permute-done.12.refs_14_
  24.0 1.6 %collective-permute-start.14 = (bf16[256,256]{1,0:T(8,128)(2,1)S(1)}, bf16[256,256]{1,0:T(8,128)(2,1)S(1)}, u32[]{:S(2)}, u32[]{:S(2)}) collective-permute-start(bf16[256,256]{1,0:T(8,128)(2,1)S(1)} %collective-permute-done.12.refs_14_), channel_id=1, source_target_pairs={{4,0},{5,1},{8,4},{9,5},{12,8},{13,9},{14,12},{15,13},{10,14},{11,... | collective-permute-start | bytes 393224 | tf_op jit(solution)/shard_map/ppermute | solution.py:229
  25.6 1.6 %load.1.refs_0_.window = bf16[256,4096]{1,0:T(8,128)(2,1)S(1)} custom-call(bf16[256,4096]{1,0:T(8,128)(2,1)} %window), custom_call_target="tpu_custom_call" | custom-call | bytes 2097152 | tf_op jit(solution)/shard_map/load/pallas_call | solution.py:32
  27.2 0.0 collective-permute-done.5.refs_3_.rest_11_
  27.2 0.0 collective-permute-done.10.refs_10_
  27.2 0.0 collective-permute-done.4.refs_1_.swapped
  27.2 1.0 %early.1 = (f32[256,256]{1,0:T(8,128)S(1)}, f32[256,256]{1,0:T(8,128)S(1)}, f32[256,256]{1,0:T(8,128)S(1)}, f32[256,256]{1,0:T(8,128)S(1)}, f32[256,256]{1,0:T(8...) custom-call(bf16[256,4096]{1,0:T(8,128)(2,1)S(1)} %load.1.refs_0_.wi, ...), custom_call_target="tpu_custom_call" | custom-call | flops 872415232 | bytes 6176768 | tf_op jit(solution)/shard_map/early/pallas_call | solution.py:32
  28.2 0.0 collective-permute-done.13.rest_12_
  28.2 0.7 %collective-permute-done.14.rest_13_ = bf16[256,256]{1,0:T(8,128)(2,1)S(1)} collective-permute-done((bf16[256,256]{1,0:T(8,128)(2,1)S(1)}, bf16[256,256]{1,0:T(8,128)(2,1)S(1)}, u32[]{:S(2)}, u32[]{:S(2)}) %collective-permute-start.14) | collective-permute-done | bytes 131104 | tf_op jit(solution)/shard_map/ppermute | solution.py:229
  28.9 1.0 %late.1 = (f32[256,256]{1,0:T(8,128)S(1)}, f32[256,256]{1,0:T(8,128)S(1)}, f32[256,256]{1,0:T(8,128)S(1)}, f32[256,256]{1,0:T(8,128)S(1)}, f32[136,256]{1,0:T(8,...) custom-call(bf16[256,4096]{1,0:T(8,128)(2,1)S(1)} %load.1.refs_0_.window, ...), custom_call_target="tpu_custom_call" | custom-call | flops 536870912 | bytes 7356416 | tf_op jit(solution)/shard_map/late/pallas_call | solution.py:32
  29.9 0.1 collective-permute-start.16
  30.0 0.5 collective-permute-start.23
  30.5 0.1 collective-permute-start.15
  30.6 0.8 %collective-permute-done.16 = f32[136,256]{1,0:T(8,128)S(1)} collective-permute-done((f32[136,256]{1,0:T(8,128)S(1)}, f32[136,256]{1,0:T(8,128)S(1)}, u32[]{:S(2)}, u32[]{:S(2)}) %collective-permute-start.16) | collective-permute-done | bytes 139296 | tf_op jit(solution)/shard_map/ppermute | solution.py:229
  31.4 1.6 %collective-permute-start.19 = (bf16[136,256]{1,0:T(8,128)(2,1)S(1)}, bf16[136,256]{1,0:T(8,128)(2,1)S(1)}, u32[]{:S(2)}, u32[]{:S(2)}) collective-permute-start(bf16[136,256]{1,0:T(8,128)(2,1)S(1)} %add.24), channel_id=1, source_target_pairs={{0,2},{1,3},{2,0},{3,1},{4,6},{5,7},{6,4},{7,5},{8,10},{9,11},{10,... | collective-permute-start | bytes 208904 | tf_op jit(solution)/shard_map/ppermute | solution.py:229
  33.0 0.0 collective-permute-done.23
  33.0 1.6 %collective-permute-start.24 = (bf16[128,256]{1,0:T(8,128)(2,1)S(1)}, bf16[128,256]{1,0:T(8,128)(2,1)S(1)}, u32[]{:S(2)}, u32[]{:S(2)}) collective-permute-start(bf16[128,256]{1,0:T(8,128)(2,1)S(1)} %add_convert_fusion.4), channel_id=1, source_target_pairs={{0,4},{1,5},{2,6},{3,7},{4,0},{5,1},{6,2},{7,3},{8,12},{9,13},{10,... | collective-permute-start | bytes 196616 | tf_op jit(solution)/shard_map/ppermute | solution.py:229
  34.7 0.5 collective-permute-start.17
  35.1 0.6 %collective-permute-done.19 = bf16[136,256]{1,0:T(8,128)(2,1)S(1)} collective-permute-done((bf16[136,256]{1,0:T(8,128)(2,1)S(1)}, bf16[136,256]{1,0:T(8,128)(2,1)S(1)}, u32[]{:S(2)}, u32[]{:S(2)}) %collective-permute-start.19) | collective-permute-done | bytes 69664 | tf_op jit(solution)/shard_map/ppermute | solution.py:229
  35.8 1.7 %collective-permute-start.20 = (bf16[136,256]{1,0:T(8,128)(2,1)S(1)}, bf16[136,256]{1,0:T(8,128)(2,1)S(1)}, u32[]{:S(2)}, u32[]{:S(2)}) collective-permute-start(bf16[136,256]{1,0:T(8,128)(2,1)S(1)} %add_convert_fusion.1), channel_id=1, source_target_pairs={{0,4},{1,5},{2,6},{3,7},{4,0},{5,1},{6,2},{7,3},{8,12},{9,13},{10,... | collective-permute-start | bytes 208904 | tf_op jit(solution)/shard_map/ppermute | solution.py:229
  37.5 0.0 collective-permute-done.24
  37.5 2.6 %collective-permute-start.25 = (bf16[128,256]{1,0:T(8,128)(2,1)S(1)}, bf16[128,256]{1,0:T(8,128)(2,1)S(1)}, u32[]{:S(2)}, u32[]{:S(2)}) collective-permute-start(bf16[128,256]{1,0:T(8,128)(2,1)S(1)} %add_convert_fusion.3), channel_id=1, source_target_pairs={{0,8},{1,9},{2,10},{3,11},{4,12},{5,13},{6,14},{7,15},{8,0},{9,1},... | collective-permute-start | bytes 196616 | tf_op jit(solution)/shard_map/ppermute | solution.py:229
  40.2 0.9 %collective-permute-done.20 = bf16[136,256]{1,0:T(8,128)(2,1)S(1)} collective-permute-done((bf16[136,256]{1,0:T(8,128)(2,1)S(1)}, bf16[136,256]{1,0:T(8,128)(2,1)S(1)}, u32[]{:S(2)}, u32[]{:S(2)}) %collective-permute-start.20) | collective-permute-done | bytes 69664 | tf_op jit(solution)/shard_map/ppermute | solution.py:229
  41.1 2.3 %collective-permute-start.21 = (bf16[136,256]{1,0:T(8,128)(2,1)S(1)}, bf16[136,256]{1,0:T(8,128)(2,1)S(1)}, u32[]{:S(2)}, u32[]{:S(2)}) collective-permute-start(bf16[136,256]{1,0:T(8,128)(2,1)S(1)} %add_convert_fusion), channel_id=1, source_target_pairs={{0,8},{1,9},{2,10},{3,11},{4,12},{5,13},{6,14},{7,15},{8,0},{9,1},... | collective-permute-start | bytes 208904 | tf_op jit(solution)/shard_map/ppermute | solution.py:229
  43.3 0.0 collective-permute-done.25
  43.4 2.2 %collective-permute-start.26 = (bf16[128,256]{1,0:T(8,128)(2,1)S(1)}, bf16[128,256]{1,0:T(8,128)(2,1)S(1)}, u32[]{:S(2)}, u32[]{:S(2)}) collective-permute-start(bf16[128,256]{1,0:T(8,128)(2,1)S(1)} %add_convert_fusion.2), channel_id=1, source_target_pairs={{0,2},{1,3},{2,0},{3,1},{4,6},{5,7},{6,4},{7,5},{8,10},{9,11},{10,... | collective-permute-start | bytes 196616 | tf_op jit(solution)/shard_map/ppermute | solution.py:229
  45.6 0.0 collective-permute-done.17.refs_6_
  45.6 0.4 rest.1
  46.0 0.1 collective-permute-start.18
  46.1 0.5 %collective-permute-done.21 = bf16[136,256]{1,0:T(8,128)(2,1)S(1)} collective-permute-done((bf16[136,256]{1,0:T(8,128)(2,1)S(1)}, bf16[136,256]{1,0:T(8,128)(2,1)S(1)}, u32[]{:S(2)}, u32[]{:S(2)}) %collective-permute-start.21) | collective-permute-done | bytes 69664 | tf_op jit(solution)/shard_map/ppermute | solution.py:229
  46.6 0.1 collective-permute-start.22
  46.7 1.1 %collective-permute-done.26 = bf16[128,256]{1,0:T(8,128)(2,1)S(1)} collective-permute-done((bf16[128,256]{1,0:T(8,128)(2,1)S(1)}, bf16[128,256]{1,0:T(8,128)(2,1)S(1)}, u32[]{:S(2)}, u32[]{:S(2)}) %collective-permute-start.26) | collective-permute-done | bytes 65568 | tf_op jit(solution)/shard_map/ppermute | solution.py:229
  47.9 0.1 collective-permute-start.27
  47.9 0.0 collective-permute-done.15.received_one
  47.9 0.0 collective-permute-done.18.received_two
  48.0 1.0 %columns.1 = (bf16[256,256]{1,0:T(8,128)(2,1)}, bf16[256,256]{1,0:T(8,128)(2,1)}) custom-call(f32[256,256]{1,0:T(8,128)S(1)} %get-tuple-element.55.own_one, f32[256,256]{1,0:T(8,128)S(1)} %collective-permute-done.15.received_one, f32[256,256]{1,0:T(8,128)S(1)} %get-tuple-element.62.own_two, f32[256,256]{1,0:T(8,128)S(1)} %collective-permute-done.18.received_two, ...), custom_call_target="tpu_custom_call" | custom-call | bytes 1181696 | tf_op jit(solution)/shard_map/columns/pallas_call | solution.py:32
  49.0 0.0 collective-permute-done.22.pack_b
  49.0 0.3 collective-permute-done.27.cross_b
  49.3 0.0 copy-done.2
  49.3 1.3 %last.1 = (f32[256,256]{1,0:T(8,128)}, f32[256,256]{1,0:T(8,128)}, f32[256,256]{1,0:T(8,128)}) custom-call(f32[136,256]{1,0:T(8,128)S(1)} %convert_add_fusion.pack_a, f32[136,256]{1,0:T(8,128)S(1)} %collective-permute-done.22.pack_b, f32[128,256]{1,0:T(8,128)S(1)} %convert_add_fusion.1.cross_a, f32[128,256]{1,0:T(8,128)S(1)} %collective-permute-done.27.cross_b, ...), custom_call_target="tpu_custom_call" | custom-call | bytes 1196032 | tf_op jit(solution)/shard_map/last/pallas_call | solution.py:32
  (13 shorter events, 0.2 us)
Async XLA Ops:
  0.6 26.6 %collective-permute-start.4 = (bf16[256,4096]{1,0:T(8,128)(2,1)}, bf16[256,4096]{1,0:T(8,128)(2,1)S(1)}, u32[]{:S(2)}, u32[]{:S(2)}) collective-permute-start(bf16[256,4096]{1,0:T(8,128)(2,1)} %window), channel_id=1, source_target_pairs={{0,1},{1,0},{2,3},{3,2},{4,5},{5,4},{6,7},{7,6},{8,9},{9,8},{10,11... | collective-permute-start | bytes 6291464 | tf_op jit(solution)/shard_map/ppermute | solution.py:229
  2.5 7.0 %collective-permute-start.1 = (bf16[256,256]{1,0:T(8,128)(2,1)S(1)}, bf16[256,256]{1,0:T(8,128)(2,1)S(1)}, u32[]{:S(2)}, u32[]{:S(2)}) collective-permute-start(bf16[256,256]{1,0:T(8,128)(2,1)S(1)} %get-tuple-element.40.refs_4_), channel_id=1, source_target_pairs={{4,0},{5,1},{8,4},{9,5},{12,8},{13,9},{14,12},{15,13},{10,14},{11,... | collective-permute-start | bytes 393224 | tf_op jit(solution)/shard_map/ppermute | solution.py:229
  5.1 6.3 %collective-permute-start = (bf16[256,256]{1,0:T(8,128)(2,1)S(1)}, bf16[256,256]{1,0:T(8,128)(2,1)S(1)}, u32[]{:S(2)}, u32[]{:S(2)}) collective-permute-start(bf16[256,256]{1,0:T(8,128)(2,1)S(1)} %get-tuple-element.40.refs_4_), channel_id=1, source_target_pairs={{0,4},{1,5},{4,8},{5,9},{8,12},{9,13},{12,14},{13,15},{14,10},{15,... | collective-permute-start | bytes 393224 | tf_op jit(solution)/shard_map/ppermute | solution.py:229
  5.3 7.1 %collective-permute-start.3 = (bf16[256,256]{1,0:T(8,128)(2,1)S(1)}, bf16[256,256]{1,0:T(8,128)(2,1)S(1)}, u32[]{:S(2)}, u32[]{:S(2)}) collective-permute-start(bf16[256,256]{1,0:T(8,128)(2,1)S(1)} %get-tuple-element.41.refs_11_), channel_id=1, source_target_pairs={{4,0},{5,1},{8,4},{9,5},{12,8},{13,9},{14,12},{15,13},{10,14},{11,... | collective-permute-start | bytes 393224 | tf_op jit(solution)/shard_map/ppermute | solution.py:229
  7.2 7.1 %collective-permute-start.2 = (bf16[256,256]{1,0:T(8,128)(2,1)S(1)}, bf16[256,256]{1,0:T(8,128)(2,1)S(1)}, u32[]{:S(2)}, u32[]{:S(2)}) collective-permute-start(bf16[256,256]{1,0:T(8,128)(2,1)S(1)} %get-tuple-element.41.refs_11_), channel_id=1, source_target_pairs={{0,4},{1,5},{4,8},{5,9},{8,12},{9,13},{12,14},{13,15},{14,10},{15,... | collective-permute-start | bytes 393224 | tf_op jit(solution)/shard_map/ppermute | solution.py:229
  9.5 5.7 %collective-permute-start.9 = (bf16[256,256]{1,0:T(8,128)(2,1)S(1)}, bf16[256,256]{1,0:T(8,128)(2,1)S(1)}, u32[]{:S(2)}, u32[]{:S(2)}) collective-permute-start(bf16[256,256]{1,0:T(8,128)(2,1)S(1)} %collective-permute-done.1.refs_8_), channel_id=1, source_target_pairs={{4,0},{5,1},{8,4},{9,5},{12,8},{13,9},{14,12},{15,13},{10,14},{11,... | collective-permute-start | bytes 393224 | tf_op jit(solution)/shard_map/ppermute | solution.py:229
  11.5 5.7 %collective-permute-start.6 = (bf16[256,256]{1,0:T(8,128)(2,1)S(1)}, bf16[256,256]{1,0:T(8,128)(2,1)S(1)}, u32[]{:S(2)}, u32[]{:S(2)}) collective-permute-start(bf16[256,256]{1,0:T(8,128)(2,1)S(1)} %collective-permute-done.refs_5_), channel_id=1, source_target_pairs={{0,4},{1,5},{4,8},{5,9},{8,12},{9,13},{12,14},{13,15},{14,10},{15,... | collective-permute-start | bytes 393224 | tf_op jit(solution)/shard_map/ppermute | solution.py:229
  12.3 6.4 %collective-permute-start.11 = (bf16[256,256]{1,0:T(8,128)(2,1)S(1)}, bf16[256,256]{1,0:T(8,128)(2,1)S(1)}, u32[]{:S(2)}, u32[]{:S(2)}) collective-permute-start(bf16[256,256]{1,0:T(8,128)(2,1)S(1)} %collective-permute-done.3.refs_12_), channel_id=1, source_target_pairs={{4,0},{5,1},{8,4},{9,5},{12,8},{13,9},{14,12},{15,13},{10,14},{11,... | collective-permute-start | bytes 393224 | tf_op jit(solution)/shard_map/ppermute | solution.py:229
  14.2 12.9 %collective-permute-start.5 = (bf16[528,256]{1,0:T(8,128)(2,1)S(1)}, bf16[528,256]{1,0:T(8,128)(2,1)S(1)}, u32[]{:S(2)}, u32[]{:S(2)}) collective-permute-start(bf16[528,256]{1,0:T(8,128)(2,1)S(1)} %get-tuple-element.43.refs_2_.rest_10_), channel_id=1, source_target_pairs={{0,1},{1,0},{2,3},{3,2},{4,5},{5,4},{6,7},{7,6},{8,9},{9,8},{10,11... | collective-permute-start | bytes 811016 | tf_op jit(solution)/shard_map/ppermute | solution.py:229
  15.2 6.4 %collective-permute-start.8 = (bf16[256,256]{1,0:T(8,128)(2,1)S(1)}, bf16[256,256]{1,0:T(8,128)(2,1)S(1)}, u32[]{:S(2)}, u32[]{:S(2)}) collective-permute-start(bf16[256,256]{1,0:T(8,128)(2,1)S(1)} %collective-permute-done.2.refs_4_), channel_id=1, source_target_pairs={{0,4},{1,5},{4,8},{5,9},{8,12},{9,13},{12,14},{13,15},{14,10},{15,... | collective-permute-start | bytes 393224 | tf_op jit(solution)/shard_map/ppermute | solution.py:229
  17.2 6.0 %collective-permute-start.7 = (bf16[256,256]{1,0:T(8,128)(2,1)S(1)}, bf16[256,256]{1,0:T(8,128)(2,1)S(1)}, u32[]{:S(2)}, u32[]{:S(2)}) collective-permute-start(bf16[256,256]{1,0:T(8,128)(2,1)S(1)} %collective-permute-done.6.refs_6_), channel_id=1, source_target_pairs={{0,4},{1,5},{4,8},{5,9},{8,12},{9,13},{12,14},{13,15},{14,10},{15,... | collective-permute-start | bytes 393224 | tf_op jit(solution)/shard_map/ppermute | solution.py:229
  18.8 5.2 %collective-permute-start.12 = (bf16[256,256]{1,0:T(8,128)(2,1)S(1)}, bf16[256,256]{1,0:T(8,128)(2,1)S(1)}, u32[]{:S(2)}, u32[]{:S(2)}) collective-permute-start(bf16[256,256]{1,0:T(8,128)(2,1)S(1)} %collective-permute-done.11.refs_13_), channel_id=1, source_target_pairs={{4,0},{5,1},{8,4},{9,5},{12,8},{13,9},{14,12},{15,13},{10,14},{11,... | collective-permute-start | bytes 393224 | tf_op jit(solution)/shard_map/ppermute | solution.py:229
  21.6 5.6 %collective-permute-start.10 = (bf16[256,256]{1,0:T(8,128)(2,1)S(1)}, bf16[256,256]{1,0:T(8,128)(2,1)S(1)}, u32[]{:S(2)}, u32[]{:S(2)}) collective-permute-start(bf16[256,256]{1,0:T(8,128)(2,1)S(1)} %collective-permute-done.9.refs_9_), channel_id=1, source_target_pairs={{4,0},{5,1},{8,4},{9,5},{12,8},{13,9},{14,12},{15,13},{10,14},{11,... | collective-permute-start | bytes 393224 | tf_op jit(solution)/shard_map/ppermute | solution.py:229
  23.1 5.1 %collective-permute-start.13 = (bf16[256,256]{1,0:T(8,128)(2,1)S(1)}, bf16[256,256]{1,0:T(8,128)(2,1)S(1)}, u32[]{:S(2)}, u32[]{:S(2)}) collective-permute-start(bf16[256,256]{1,0:T(8,128)(2,1)S(1)} %collective-permute-done.7.refs_7_), channel_id=1, source_target_pairs={{0,4},{1,5},{4,8},{5,9},{8,12},{9,13},{12,14},{13,15},{14,10},{15,... | collective-permute-start | bytes 393224 | tf_op jit(solution)/shard_map/ppermute | solution.py:229
  24.0 5.0 %collective-permute-start.14 = (bf16[256,256]{1,0:T(8,128)(2,1)S(1)}, bf16[256,256]{1,0:T(8,128)(2,1)S(1)}, u32[]{:S(2)}, u32[]{:S(2)}) collective-permute-start(bf16[256,256]{1,0:T(8,128)(2,1)S(1)} %collective-permute-done.12.refs_14_), channel_id=1, source_target_pairs={{4,0},{5,1},{8,4},{9,5},{12,8},{13,9},{14,12},{15,13},{10,14},{11,... | collective-permute-start | bytes 393224 | tf_op jit(solution)/shard_map/ppermute | solution.py:229
  29.9 1.4 %collective-permute-start.16 = (f32[136,256]{1,0:T(8,128)S(1)}, f32[136,256]{1,0:T(8,128)S(1)}, u32[]{:S(2)}, u32[]{:S(2)}) collective-permute-start(f32[136,256]{1,0:T(8,128)S(1)} %get-tuple-element.60), channel_id=1, source_target_pairs={{0,1},{1,0},{2,3},{3,2},{4,5},{5,4},{6,7},{7,6},{8,9},{9,8},{10,11... | collective-permute-start | bytes 417800 | tf_op jit(solution)/shard_map/ppermute | solution.py:229
  30.0 3.0 %collective-permute-start.23 = (f32[128,256]{1,0:T(8,128)S(1)}, f32[128,256]{1,0:T(8,128)S(1)}, u32[]{:S(2)}, u32[]{:S(2)}) collective-permute-start(f32[128,256]{1,0:T(8,128)S(1)} %get-tuple-element.70), channel_id=1, source_target_pairs={{0,1},{1,0},{2,3},{3,2},{4,5},{5,4},{6,7},{7,6},{8,9},{9,8},{10,11... | collective-permute-start | bytes 393224 | tf_op jit(solution)/shard_map/ppermute | solution.py:229
  30.5 17.4 %collective-permute-start.15 = (f32[256,256]{1,0:T(8,128)S(1)}, f32[256,256]{1,0:T(8,128)S(1)}, u32[]{:S(2)}, u32[]{:S(2)}) collective-permute-start(f32[256,256]{1,0:T(8,128)S(1)} %get-tuple-element.56), channel_id=1, source_target_pairs={{0,1},{1,0},{2,3},{3,2},{4,5},{5,4},{6,7},{7,6},{8,9},{9,8},{10,11... | collective-permute-start | bytes 786440 | tf_op jit(solution)/shard_map/ppermute | solution.py:229
  31.4 4.4 %collective-permute-start.19 = (bf16[136,256]{1,0:T(8,128)(2,1)S(1)}, bf16[136,256]{1,0:T(8,128)(2,1)S(1)}, u32[]{:S(2)}, u32[]{:S(2)}) collective-permute-start(bf16[136,256]{1,0:T(8,128)(2,1)S(1)} %add.24), channel_id=1, source_target_pairs={{0,2},{1,3},{2,0},{3,1},{4,6},{5,7},{6,4},{7,5},{8,10},{9,11},{10,... | collective-permute-start | bytes 208904 | tf_op jit(solution)/shard_map/ppermute | solution.py:229
  33.0 4.5 %collective-permute-start.24 = (bf16[128,256]{1,0:T(8,128)(2,1)S(1)}, bf16[128,256]{1,0:T(8,128)(2,1)S(1)}, u32[]{:S(2)}, u32[]{:S(2)}) collective-permute-start(bf16[128,256]{1,0:T(8,128)(2,1)S(1)} %add_convert_fusion.4), channel_id=1, source_target_pairs={{0,4},{1,5},{2,6},{3,7},{4,0},{5,1},{6,2},{7,3},{8,12},{9,13},{10,... | collective-permute-start | bytes 196616 | tf_op jit(solution)/shard_map/ppermute | solution.py:229
  34.7 10.9 %collective-permute-start.17 = (bf16[256,256]{1,0:T(8,128)(2,1)S(1)}, bf16[256,256]{1,0:T(8,128)(2,1)S(1)}, u32[]{:S(2)}, u32[]{:S(2)}) collective-permute-start(bf16[256,256]{1,0:T(8,128)(2,1)S(1)} %collective-permute-done.8.refs_5_), channel_id=1, source_target_pairs={{0,4},{1,5},{4,8},{5,9},{8,12},{9,13},{12,14},{13,15},{14,10},{15,... | collective-permute-start | bytes 393224 | tf_op jit(solution)/shard_map/ppermute | solution.py:229
  35.8 5.3 %collective-permute-start.20 = (bf16[136,256]{1,0:T(8,128)(2,1)S(1)}, bf16[136,256]{1,0:T(8,128)(2,1)S(1)}, u32[]{:S(2)}, u32[]{:S(2)}) collective-permute-start(bf16[136,256]{1,0:T(8,128)(2,1)S(1)} %add_convert_fusion.1), channel_id=1, source_target_pairs={{0,4},{1,5},{2,6},{3,7},{4,0},{5,1},{6,2},{7,3},{8,12},{9,13},{10,... | collective-permute-start | bytes 208904 | tf_op jit(solution)/shard_map/ppermute | solution.py:229
  37.5 5.8 %collective-permute-start.25 = (bf16[128,256]{1,0:T(8,128)(2,1)S(1)}, bf16[128,256]{1,0:T(8,128)(2,1)S(1)}, u32[]{:S(2)}, u32[]{:S(2)}) collective-permute-start(bf16[128,256]{1,0:T(8,128)(2,1)S(1)} %add_convert_fusion.3), channel_id=1, source_target_pairs={{0,8},{1,9},{2,10},{3,11},{4,12},{5,13},{6,14},{7,15},{8,0},{9,1},... | collective-permute-start | bytes 196616 | tf_op jit(solution)/shard_map/ppermute | solution.py:229
  41.1 5.5 %collective-permute-start.21 = (bf16[136,256]{1,0:T(8,128)(2,1)S(1)}, bf16[136,256]{1,0:T(8,128)(2,1)S(1)}, u32[]{:S(2)}, u32[]{:S(2)}) collective-permute-start(bf16[136,256]{1,0:T(8,128)(2,1)S(1)} %add_convert_fusion), channel_id=1, source_target_pairs={{0,8},{1,9},{2,10},{3,11},{4,12},{5,13},{6,14},{7,15},{8,0},{9,1},... | collective-permute-start | bytes 208904 | tf_op jit(solution)/shard_map/ppermute | solution.py:229
  43.4 4.5 %collective-permute-start.26 = (bf16[128,256]{1,0:T(8,128)(2,1)S(1)}, bf16[128,256]{1,0:T(8,128)(2,1)S(1)}, u32[]{:S(2)}, u32[]{:S(2)}) collective-permute-start(bf16[128,256]{1,0:T(8,128)(2,1)S(1)} %add_convert_fusion.2), channel_id=1, source_target_pairs={{0,2},{1,3},{2,0},{3,1},{4,6},{5,7},{6,4},{7,5},{8,10},{9,11},{10,... | collective-permute-start | bytes 196616 | tf_op jit(solution)/shard_map/ppermute | solution.py:229
  45.6 2.4 %copy-start = (bf16[256,256]{1,0:T(8,128)(2,1)S(1)}, bf16[256,256]{1,0:T(8,128)(2,1)}, u32[]{:S(2)}) copy-start(bf16[256,256]{1,0:T(8,128)(2,1)} %cross.3) | copy-start | bytes 393220
  45.6 3.7 %copy-start.1 = (f32[256,256]{1,0:T(8,128)S(1)}, f32[256,256]{1,0:T(8,128)}, u32[]{:S(2)}) copy-start(f32[256,256]{1,0:T(8,128)} %diag_one.1) | copy-start | bytes 786436
  45.6 3.7 %copy-start.2 = (f32[256,256]{1,0:T(8,128)S(1)}, f32[256,256]{1,0:T(8,128)}, u32[]{:S(2)}) copy-start(f32[256,256]{1,0:T(8,128)} %diag_two.1) | copy-start | bytes 786436
  46.0 2.0 %collective-permute-start.18 = (f32[256,256]{1,0:T(8,128)S(1)}, f32[256,256]{1,0:T(8,128)S(1)}, u32[]{:S(2)}, u32[]{:S(2)}) collective-permute-start(f32[256,256]{1,0:T(8,128)S(1)} %get-tuple-element.63), channel_id=1, source_target_pairs={{0,1},{1,0},{2,3},{3,2},{4,5},{5,4},{6,7},{7,6},{8,9},{9,8},{10,11... | collective-permute-start | bytes 786440 | tf_op jit(solution)/shard_map/ppermute | solution.py:229
  46.6 2.4 %collective-permute-start.22 = (f32[136,256]{1,0:T(8,128)S(1)}, f32[136,256]{1,0:T(8,128)S(1)}, u32[]{:S(2)}, u32[]{:S(2)}) collective-permute-start(f32[136,256]{1,0:T(8,128)S(1)} %convert_add_fusion.pack_a), channel_id=1, source_target_pairs={{0,1},{1,0},{2,3},{3,2},{4,5},{5,4},{6,7},{7,6},{8,9},{9,8},{10,11... | collective-permute-start | bytes 417800 | tf_op jit(solution)/shard_map/ppermute | solution.py:229
  47.9 1.4 %collective-permute-start.27 = (f32[128,256]{1,0:T(8,128)S(1)}, f32[128,256]{1,0:T(8,128)S(1)}, u32[]{:S(2)}, u32[]{:S(2)}) collective-permute-start(f32[128,256]{1,0:T(8,128)S(1)} %convert_add_fusion.1.cross_a), channel_id=1, source_target_pairs={{0,1},{1,0},{2,3},{3,2},{4,5},{5,4},{6,7},{7,6},{8,9},{9,8},{10,11... | collective-permute-start | bytes 393224 | tf_op jit(solution)/shard_map/ppermute | solution.py:229

commit v7 on v6

--- a/solution.py
+++ b/solution.py
@@ -125,9 +125,9 @@
 
 
 def gram(panels, images):
-    (a, b), (c, d) = halves(images[0]), halves(images[1])
-    mine, sibling = panels
-    return (dot_t(mine, a) + dot_t(sibling, c)) + (dot_t(mine, b) + dot_t(sibling, d))
+    both = jnp.concatenate(panels, axis=0)
+    high, low = halves(jnp.concatenate(images, axis=0))
+    return dot_t(both, high) + dot_t(both, low)
 
 
 def late_body(steps, window, swapped, *rest):

time: 50.7 us -> 50.7 us (level)
  no operation moved by 1% of the time
where the time goes in v7:
time: 50.7 us; the launch traced here: 50.5 us
  starting transfers between devices  30.7 us (61%)
  waiting for transfers between devices  11.3 us (22%)
  Pallas kernels  7.62 us (15%)
  between operations  0.82 us (2%)
    ppermute x28, starting transfers between devices, send(): return lax.ppermute(x, AXIS, perm)  30.7 us
    ppermute x28, waiting for transfers between devices, send(): return lax.ppermute(x, AXIS, perm)  11.3 us
    pallas_call x7, Pallas kernels, call(): pl.pallas_call(body, name=name, out_shape=tuple((jax.ShapeDtypeStruct(s,...  7.62 us
  transfers between devices with their start and end apart: 28, of which 12 were waited for; matrix products, arithmetic and copies ran while one was open for 0% of the time, Pallas kernels for 11%

profile of v7, /device:TPU:0, one launch (start us, length us, event | category | flops | bytes accessed | tf_op | source)
XLA Modules:
  0.0 50.5 jit_solution(9618395025672673464)
XLA Ops:
  0.6 0.5 %collective-permute-start.4 = (bf16[256,4096]{1,0:T(8,128)(2,1)}, bf16[256,4096]{1,0:T(8,128)(2,1)S(1)}, u32[]{:S(2)}, u32[]{:S(2)}) collective-permute-start(bf16[256,4096]{1,0:T(8,128)(2,1)} %window), channel_id=1, source_target_pairs={{0,1},{1,0},{2,3},{3,2},{4,5},{5,4},{6,7},{7,6},{8,9},{9,8},{10,11... | collective-permute-start | bytes 6291464 | tf_op jit(solution)/shard_map/ppermute | solution.py:229
  1.2 1.4 %mask.1 = (bf16[256,256]{1,0:T(8,128)(2,1)S(1)}, bf16[256,256]{1,0:T(8,128)(2,1)S(1)}, bf16[528,256]{1,0:T(8,128)(2,1)S(1)}, f32[2,256]{1,0:T(2,128)S(1)}) custom-call(s32[2,16]{1,0:T(2,128)} %table.1, s32[1,256]{1,0:T(1,128)} %bitcast.1, bf16[256,256]{1,0:T(8,128)(2,1)} %one.1, bf16[256,256]{1,0:T(8,128)(2,1)} %two.1), custom_call_target="tpu_custom_call" | custom-call | bytes 263296 | tf_op jit(solution)/shard_map/mask/pallas_call | solution.py:32
  2.5 2.6 %collective-permute-start.1 = (bf16[256,256]{1,0:T(8,128)(2,1)S(1)}, bf16[256,256]{1,0:T(8,128)(2,1)S(1)}, u32[]{:S(2)}, u32[]{:S(2)}) collective-permute-start(bf16[256,256]{1,0:T(8,128)(2,1)S(1)} %get-tuple-element.40.refs_4_), channel_id=1, source_target_pairs={{4,0},{5,1},{8,4},{9,5},{12,8},{13,9},{14,12},{15,13},{10,14},{11,... | collective-permute-start | bytes 393224 | tf_op jit(solution)/shard_map/ppermute | solution.py:229
  5.1 0.1 collective-permute-start
  5.3 1.9 %collective-permute-start.3 = (bf16[256,256]{1,0:T(8,128)(2,1)S(1)}, bf16[256,256]{1,0:T(8,128)(2,1)S(1)}, u32[]{:S(2)}, u32[]{:S(2)}) collective-permute-start(bf16[256,256]{1,0:T(8,128)(2,1)S(1)} %get-tuple-element.41.refs_11_), channel_id=1, source_target_pairs={{4,0},{5,1},{8,4},{9,5},{12,8},{13,9},{14,12},{15,13},{10,14},{11,... | collective-permute-start | bytes 393224 | tf_op jit(solution)/shard_map/ppermute | solution.py:229
  7.2 0.1 collective-permute-start.2
  7.3 2.3 %collective-permute-done.1.refs_8_ = bf16[256,256]{1,0:T(8,128)(2,1)S(1)} collective-permute-done((bf16[256,256]{1,0:T(8,128)(2,1)S(1)}, bf16[256,256]{1,0:T(8,128)(2,1)S(1)}, u32[]{:S(2)}, u32[]{:S(2)}) %collective-permute-start.1) | collective-permute-done | bytes 131104 | tf_op jit(solution)/shard_map/ppermute | solution.py:229
  9.5 1.9 %collective-permute-start.9 = (bf16[256,256]{1,0:T(8,128)(2,1)S(1)}, bf16[256,256]{1,0:T(8,128)(2,1)S(1)}, u32[]{:S(2)}, u32[]{:S(2)}) collective-permute-start(bf16[256,256]{1,0:T(8,128)(2,1)S(1)} %collective-permute-done.1.refs_8_), channel_id=1, source_target_pairs={{4,0},{5,1},{8,4},{9,5},{12,8},{13,9},{14,12},{15,13},{10,14},{11,... | collective-permute-start | bytes 393224 | tf_op jit(solution)/shard_map/ppermute | solution.py:229
  11.4 0.0 collective-permute-done.refs_5_
  11.5 0.1 collective-permute-start.6
  11.6 0.8 %collective-permute-done.3.refs_12_ = bf16[256,256]{1,0:T(8,128)(2,1)S(1)} collective-permute-done((bf16[256,256]{1,0:T(8,128)(2,1)S(1)}, bf16[256,256]{1,0:T(8,128)(2,1)S(1)}, u32[]{:S(2)}, u32[]{:S(2)}) %collective-permute-start.3) | collective-permute-done | bytes 131104 | tf_op jit(solution)/shard_map/ppermute | solution.py:229
  12.3 1.9 %collective-permute-start.11 = (bf16[256,256]{1,0:T(8,128)(2,1)S(1)}, bf16[256,256]{1,0:T(8,128)(2,1)S(1)}, u32[]{:S(2)}, u32[]{:S(2)}) collective-permute-start(bf16[256,256]{1,0:T(8,128)(2,1)S(1)} %collective-permute-done.3.refs_12_), channel_id=1, source_target_pairs={{4,0},{5,1},{8,4},{9,5},{12,8},{13,9},{14,12},{15,13},{10,14},{11,... | collective-permute-start | bytes 393224 | tf_op jit(solution)/shard_map/ppermute | solution.py:229
  14.2 0.0 collective-permute-done.2.refs_4_
  14.2 0.0 collective-permute-start.5
  14.2 1.0 %collective-permute-done.9.refs_9_ = bf16[256,256]{1,0:T(8,128)(2,1)S(1)} collective-permute-done((bf16[256,256]{1,0:T(8,128)(2,1)S(1)}, bf16[256,256]{1,0:T(8,128)(2,1)S(1)}, u32[]{:S(2)}, u32[]{:S(2)}) %collective-permute-start.9) | collective-permute-done | bytes 131104 | tf_op jit(solution)/shard_map/ppermute | solution.py:229
  15.2 2.0 %collective-permute-start.8 = (bf16[256,256]{1,0:T(8,128)(2,1)S(1)}, bf16[256,256]{1,0:T(8,128)(2,1)S(1)}, u32[]{:S(2)}, u32[]{:S(2)}) collective-permute-start(bf16[256,256]{1,0:T(8,128)(2,1)S(1)} %collective-permute-done.2.refs_4_), channel_id=1, source_target_pairs={{0,4},{1,5},{4,8},{5,9},{8,12},{9,13},{12,14},{13,15},{14,10},{15,... | collective-permute-start | bytes 393224 | tf_op jit(solution)/shard_map/ppermute | solution.py:229
  17.2 0.0 collective-permute-done.6.refs_6_
  17.2 1.6 %collective-permute-start.7 = (bf16[256,256]{1,0:T(8,128)(2,1)S(1)}, bf16[256,256]{1,0:T(8,128)(2,1)S(1)}, u32[]{:S(2)}, u32[]{:S(2)}) collective-permute-start(bf16[256,256]{1,0:T(8,128)(2,1)S(1)} %collective-permute-done.6.refs_6_), channel_id=1, source_target_pairs={{0,4},{1,5},{4,8},{5,9},{8,12},{9,13},{12,14},{13,15},{14,10},{15,... | collective-permute-start | bytes 393224 | tf_op jit(solution)/shard_map/ppermute | solution.py:229
  18.8 0.0 collective-permute-done.11.refs_13_
  18.8 0.7 %collective-permute-start.12 = (bf16[256,256]{1,0:T(8,128)(2,1)S(1)}, bf16[256,256]{1,0:T(8,128)(2,1)S(1)}, u32[]{:S(2)}, u32[]{:S(2)}) collective-permute-start(bf16[256,256]{1,0:T(8,128)(2,1)S(1)} %collective-permute-done.11.refs_13_), channel_id=1, source_target_pairs={{4,0},{5,1},{8,4},{9,5},{12,8},{13,9},{14,12},{15,13},{10,14},{11,... | collective-permute-start | bytes 393224 | tf_op jit(solution)/shard_map/ppermute | solution.py:229
  19.5 2.1 %collective-permute-done.8.refs_5_ = bf16[256,256]{1,0:T(8,128)(2,1)S(1)} collective-permute-done((bf16[256,256]{1,0:T(8,128)(2,1)S(1)}, bf16[256,256]{1,0:T(8,128)(2,1)S(1)}, u32[]{:S(2)}, u32[]{:S(2)}) %collective-permute-start.8) | collective-permute-done | bytes 131104 | tf_op jit(solution)/shard_map/ppermute | solution.py:229
  21.6 1.6 %collective-permute-start.10 = (bf16[256,256]{1,0:T(8,128)(2,1)S(1)}, bf16[256,256]{1,0:T(8,128)(2,1)S(1)}, u32[]{:S(2)}, u32[]{:S(2)}) collective-permute-start(bf16[256,256]{1,0:T(8,128)(2,1)S(1)} %collective-permute-done.9.refs_9_), channel_id=1, source_target_pairs={{4,0},{5,1},{8,4},{9,5},{12,8},{13,9},{14,12},{15,13},{10,14},{11,... | collective-permute-start | bytes 393224 | tf_op jit(solution)/shard_map/ppermute | solution.py:229
  23.1 0.0 collective-permute-done.7.refs_7_
  23.1 0.7 %collective-permute-start.13 = (bf16[256,256]{1,0:T(8,128)(2,1)S(1)}, bf16[256,256]{1,0:T(8,128)(2,1)S(1)}, u32[]{:S(2)}, u32[]{:S(2)}) collective-permute-start(bf16[256,256]{1,0:T(8,128)(2,1)S(1)} %collective-permute-done.7.refs_7_), channel_id=1, source_target_pairs={{0,4},{1,5},{4,8},{5,9},{8,12},{9,13},{12,14},{13,15},{14,10},{15,... | collective-permute-start | bytes 393224 | tf_op jit(solution)/shard_map/ppermute | solution.py:229
  23.8 0.2 collective-permute-done.12.refs_14_
  24.0 1.6 %collective-permute-start.14 = (bf16[256,256]{1,0:T(8,128)(2,1)S(1)}, bf16[256,256]{1,0:T(8,128)(2,1)S(1)}, u32[]{:S(2)}, u32[]{:S(2)}) collective-permute-start(bf16[256,256]{1,0:T(8,128)(2,1)S(1)} %collective-permute-done.12.refs_14_), channel_id=1, source_target_pairs={{4,0},{5,1},{8,4},{9,5},{12,8},{13,9},{14,12},{15,13},{10,14},{11,... | collective-permute-start | bytes 393224 | tf_op jit(solution)/shard_map/ppermute | solution.py:229
  25.6 1.6 %load.1.refs_0_.window = bf16[256,4096]{1,0:T(8,128)(2,1)S(1)} custom-call(bf16[256,4096]{1,0:T(8,128)(2,1)} %window), custom_call_target="tpu_custom_call" | custom-call | bytes 2097152 | tf_op jit(solution)/shard_map/load/pallas_call | solution.py:32
  27.2 0.0 collective-permute-done.5.refs_3_.rest_11_
  27.2 0.0 collective-permute-done.10.refs_10_
  27.2 0.0 collective-permute-done.4.refs_1_.swapped
  27.2 1.0 %early.1 = (f32[256,256]{1,0:T(8,128)S(1)}, f32[256,256]{1,0:T(8,128)S(1)}, f32[256,256]{1,0:T(8,128)S(1)}, f32[256,256]{1,0:T(8,128)S(1)}, f32[256,256]{1,0:T(8...) custom-call(bf16[256,4096]{1,0:T(8,128)(2,1)S(1)} %load.1.refs_0_.wi, ...), custom_call_target="tpu_custom_call" | custom-call | flops 872415232 | bytes 6176768 | tf_op jit(solution)/shard_map/early/pallas_call | solution.py:32
  28.2 0.0 collective-permute-done.13.rest_12_
  28.2 0.7 %collective-permute-done.14.rest_13_ = bf16[256,256]{1,0:T(8,128)(2,1)S(1)} collective-permute-done((bf16[256,256]{1,0:T(8,128)(2,1)S(1)}, bf16[256,256]{1,0:T(8,128)(2,1)S(1)}, u32[]{:S(2)}, u32[]{:S(2)}) %collective-permute-start.14) | collective-permute-done | bytes 131104 | tf_op jit(solution)/shard_map/ppermute | solution.py:229
  28.9 0.9 %late.1 = (f32[256,256]{1,0:T(8,128)S(1)}, f32[256,256]{1,0:T(8,128)S(1)}, f32[256,256]{1,0:T(8,128)S(1)}, f32[256,256]{1,0:T(8,128)S(1)}, f32[136,256]{1,0:T(8,...) custom-call(bf16[256,4096]{1,0:T(8,128)(2,1)S(1)} %load.1.refs_0_.window, ...), custom_call_target="tpu_custom_call" | custom-call | flops 536870912 | bytes 7356416 | tf_op jit(solution)/shard_map/late/pallas_call | solution.py:32
  29.9 0.1 collective-permute-start.16
  30.0 0.5 collective-permute-start.23
  30.5 0.1 collective-permute-start.15
  30.5 0.8 %collective-permute-done.16 = f32[136,256]{1,0:T(8,128)S(1)} collective-permute-done((f32[136,256]{1,0:T(8,128)S(1)}, f32[136,256]{1,0:T(8,128)S(1)}, u32[]{:S(2)}, u32[]{:S(2)}) %collective-permute-start.16) | collective-permute-done | bytes 139296 | tf_op jit(solution)/shard_map/ppermute | solution.py:229
  31.3 1.6 %collective-permute-start.19 = (bf16[136,256]{1,0:T(8,128)(2,1)S(1)}, bf16[136,256]{1,0:T(8,128)(2,1)S(1)}, u32[]{:S(2)}, u32[]{:S(2)}) collective-permute-start(bf16[136,256]{1,0:T(8,128)(2,1)S(1)} %add.24), channel_id=1, source_target_pairs={{0,2},{1,3},{2,0},{3,1},{4,6},{5,7},{6,4},{7,5},{8,10},{9,11},{10,... | collective-permute-start | bytes 208904 | tf_op jit(solution)/shard_map/ppermute | solution.py:229
  33.0 0.0 collective-permute-done.23
  33.0 1.6 %collective-permute-start.24 = (bf16[128,256]{1,0:T(8,128)(2,1)S(1)}, bf16[128,256]{1,0:T(8,128)(2,1)S(1)}, u32[]{:S(2)}, u32[]{:S(2)}) collective-permute-start(bf16[128,256]{1,0:T(8,128)(2,1)S(1)} %add_convert_fusion.4), channel_id=1, source_target_pairs={{0,4},{1,5},{2,6},{3,7},{4,0},{5,1},{6,2},{7,3},{8,12},{9,13},{10,... | collective-permute-start | bytes 196616 | tf_op jit(solution)/shard_map/ppermute | solution.py:229
  34.6 0.4 collective-permute-start.17
  35.1 0.6 %collective-permute-done.19 = bf16[136,256]{1,0:T(8,128)(2,1)S(1)} collective-permute-done((bf16[136,256]{1,0:T(8,128)(2,1)S(1)}, bf16[136,256]{1,0:T(8,128)(2,1)S(1)}, u32[]{:S(2)}, u32[]{:S(2)}) %collective-permute-start.19) | collective-permute-done | bytes 69664 | tf_op jit(solution)/shard_map/ppermute | solution.py:229
  35.7 1.8 %collective-permute-start.20 = (bf16[136,256]{1,0:T(8,128)(2,1)S(1)}, bf16[136,256]{1,0:T(8,128)(2,1)S(1)}, u32[]{:S(2)}, u32[]{:S(2)}) collective-permute-start(bf16[136,256]{1,0:T(8,128)(2,1)S(1)} %add_convert_fusion.1), channel_id=1, source_target_pairs={{0,4},{1,5},{2,6},{3,7},{4,0},{5,1},{6,2},{7,3},{8,12},{9,13},{10,... | collective-permute-start | bytes 208904 | tf_op jit(solution)/shard_map/ppermute | solution.py:229
  37.5 0.0 collective-permute-done.24
  37.5 2.7 %collective-permute-start.25 = (bf16[128,256]{1,0:T(8,128)(2,1)S(1)}, bf16[128,256]{1,0:T(8,128)(2,1)S(1)}, u32[]{:S(2)}, u32[]{:S(2)}) collective-permute-start(bf16[128,256]{1,0:T(8,128)(2,1)S(1)} %add_convert_fusion.3), channel_id=1, source_target_pairs={{0,8},{1,9},{2,10},{3,11},{4,12},{5,13},{6,14},{7,15},{8,0},{9,1},... | collective-permute-start | bytes 196616 | tf_op jit(solution)/shard_map/ppermute | solution.py:229
  40.1 0.9 %collective-permute-done.20 = bf16[136,256]{1,0:T(8,128)(2,1)S(1)} collective-permute-done((bf16[136,256]{1,0:T(8,128)(2,1)S(1)}, bf16[136,256]{1,0:T(8,128)(2,1)S(1)}, u32[]{:S(2)}, u32[]{:S(2)}) %collective-permute-start.20) | collective-permute-done | bytes 69664 | tf_op jit(solution)/shard_map/ppermute | solution.py:229
  41.0 2.3 %collective-permute-start.21 = (bf16[136,256]{1,0:T(8,128)(2,1)S(1)}, bf16[136,256]{1,0:T(8,128)(2,1)S(1)}, u32[]{:S(2)}, u32[]{:S(2)}) collective-permute-start(bf16[136,256]{1,0:T(8,128)(2,1)S(1)} %add_convert_fusion), channel_id=1, source_target_pairs={{0,8},{1,9},{2,10},{3,11},{4,12},{5,13},{6,14},{7,15},{8,0},{9,1},... | collective-permute-start | bytes 208904 | tf_op jit(solution)/shard_map/ppermute | solution.py:229
  43.3 0.0 collective-permute-done.25
  43.3 2.2 %collective-permute-start.26 = (bf16[128,256]{1,0:T(8,128)(2,1)S(1)}, bf16[128,256]{1,0:T(8,128)(2,1)S(1)}, u32[]{:S(2)}, u32[]{:S(2)}) collective-permute-start(bf16[128,256]{1,0:T(8,128)(2,1)S(1)} %add_convert_fusion.2), channel_id=1, source_target_pairs={{0,2},{1,3},{2,0},{3,1},{4,6},{5,7},{6,4},{7,5},{8,10},{9,11},{10,... | collective-permute-start | bytes 196616 | tf_op jit(solution)/shard_map/ppermute | solution.py:229
  45.5 0.0 collective-permute-done.17.refs_6_
  45.5 0.4 rest.1
  45.9 0.1 collective-permute-start.18
  46.0 0.5 %collective-permute-done.21 = bf16[136,256]{1,0:T(8,128)(2,1)S(1)} collective-permute-done((bf16[136,256]{1,0:T(8,128)(2,1)S(1)}, bf16[136,256]{1,0:T(8,128)(2,1)S(1)}, u32[]{:S(2)}, u32[]{:S(2)}) %collective-permute-start.21) | collective-permute-done | bytes 69664 | tf_op jit(solution)/shard_map/ppermute | solution.py:229
  46.6 0.1 collective-permute-start.22
  46.7 1.1 %collective-permute-done.26 = bf16[128,256]{1,0:T(8,128)(2,1)S(1)} collective-permute-done((bf16[128,256]{1,0:T(8,128)(2,1)S(1)}, bf16[128,256]{1,0:T(8,128)(2,1)S(1)}, u32[]{:S(2)}, u32[]{:S(2)}) %collective-permute-start.26) | collective-permute-done | bytes 65568 | tf_op jit(solution)/shard_map/ppermute | solution.py:229
  47.8 0.1 collective-permute-start.27
  47.9 0.0 collective-permute-done.15.received_one
  47.9 0.0 collective-permute-done.18.received_two
  47.9 1.0 %columns.1 = (bf16[256,256]{1,0:T(8,128)(2,1)}, bf16[256,256]{1,0:T(8,128)(2,1)}) custom-call(f32[256,256]{1,0:T(8,128)S(1)} %get-tuple-element.55.own_one, f32[256,256]{1,0:T(8,128)S(1)} %collective-permute-done.15.received_one, f32[256,256]{1,0:T(8,128)S(1)} %get-tuple-element.62.own_two, f32[256,256]{1,0:T(8,128)S(1)} %collective-permute-done.18.received_two, ...), custom_call_target="tpu_custom_call" | custom-call | bytes 1181696 | tf_op jit(solution)/shard_map/columns/pallas_call | solution.py:32
  48.9 0.0 collective-permute-done.22.pack_b
  48.9 0.3 collective-permute-done.27.cross_b
  49.2 0.0 copy-done.1
  49.2 1.3 %last.1 = (f32[256,256]{1,0:T(8,128)}, f32[256,256]{1,0:T(8,128)}, f32[256,256]{1,0:T(8,128)}) custom-call(f32[136,256]{1,0:T(8,128)S(1)} %convert_add_fusion.pack_a, f32[136,256]{1,0:T(8,128)S(1)} %collective-permute-done.22.pack_b, f32[128,256]{1,0:T(8,128)S(1)} %convert_add_fusion.1.cross_a, f32[128,256]{1,0:T(8,128)S(1)} %collective-permute-done.27.cross_b, ...), custom_call_target="tpu_custom_call" | custom-call | bytes 1196032 | tf_op jit(solution)/shard_map/last/pallas_call | solution.py:32
  (13 shorter events, 0.2 us)
Async XLA Ops:
  0.6 26.6 %collective-permute-start.4 = (bf16[256,4096]{1,0:T(8,128)(2,1)}, bf16[256,4096]{1,0:T(8,128)(2,1)S(1)}, u32[]{:S(2)}, u32[]{:S(2)}) collective-permute-start(bf16[256,4096]{1,0:T(8,128)(2,1)} %window), channel_id=1, source_target_pairs={{0,1},{1,0},{2,3},{3,2},{4,5},{5,4},{6,7},{7,6},{8,9},{9,8},{10,11... | collective-permute-start | bytes 6291464 | tf_op jit(solution)/shard_map/ppermute | solution.py:229
  2.5 7.0 %collective-permute-start.1 = (bf16[256,256]{1,0:T(8,128)(2,1)S(1)}, bf16[256,256]{1,0:T(8,128)(2,1)S(1)}, u32[]{:S(2)}, u32[]{:S(2)}) collective-permute-start(bf16[256,256]{1,0:T(8,128)(2,1)S(1)} %get-tuple-element.40.refs_4_), channel_id=1, source_target_pairs={{4,0},{5,1},{8,4},{9,5},{12,8},{13,9},{14,12},{15,13},{10,14},{11,... | collective-permute-start | bytes 393224 | tf_op jit(solution)/shard_map/ppermute | solution.py:229
  5.1 6.3 %collective-permute-start = (bf16[256,256]{1,0:T(8,128)(2,1)S(1)}, bf16[256,256]{1,0:T(8,128)(2,1)S(1)}, u32[]{:S(2)}, u32[]{:S(2)}) collective-permute-start(bf16[256,256]{1,0:T(8,128)(2,1)S(1)} %get-tuple-element.40.refs_4_), channel_id=1, source_target_pairs={{0,4},{1,5},{4,8},{5,9},{8,12},{9,13},{12,14},{13,15},{14,10},{15,... | collective-permute-start | bytes 393224 | tf_op jit(solution)/shard_map/ppermute | solution.py:229
  5.3 7.1 %collective-permute-start.3 = (bf16[256,256]{1,0:T(8,128)(2,1)S(1)}, bf16[256,256]{1,0:T(8,128)(2,1)S(1)}, u32[]{:S(2)}, u32[]{:S(2)}) collective-permute-start(bf16[256,256]{1,0:T(8,128)(2,1)S(1)} %get-tuple-element.41.refs_11_), channel_id=1, source_target_pairs={{4,0},{5,1},{8,4},{9,5},{12,8},{13,9},{14,12},{15,13},{10,14},{11,... | collective-permute-start | bytes 393224 | tf_op jit(solution)/shard_map/ppermute | solution.py:229
  7.2 7.1 %collective-permute-start.2 = (bf16[256,256]{1,0:T(8,128)(2,1)S(1)}, bf16[256,256]{1,0:T(8,128)(2,1)S(1)}, u32[]{:S(2)}, u32[]{:S(2)}) collective-permute-start(bf16[256,256]{1,0:T(8,128)(2,1)S(1)} %get-tuple-element.41.refs_11_), channel_id=1, source_target_pairs={{0,4},{1,5},{4,8},{5,9},{8,12},{9,13},{12,14},{13,15},{14,10},{15,... | collective-permute-start | bytes 393224 | tf_op jit(solution)/shard_map/ppermute | solution.py:229
  9.5 5.7 %collective-permute-start.9 = (bf16[256,256]{1,0:T(8,128)(2,1)S(1)}, bf16[256,256]{1,0:T(8,128)(2,1)S(1)}, u32[]{:S(2)}, u32[]{:S(2)}) collective-permute-start(bf16[256,256]{1,0:T(8,128)(2,1)S(1)} %collective-permute-done.1.refs_8_), channel_id=1, source_target_pairs={{4,0},{5,1},{8,4},{9,5},{12,8},{13,9},{14,12},{15,13},{10,14},{11,... | collective-permute-start | bytes 393224 | tf_op jit(solution)/shard_map/ppermute | solution.py:229
  11.5 5.7 %collective-permute-start.6 = (bf16[256,256]{1,0:T(8,128)(2,1)S(1)}, bf16[256,256]{1,0:T(8,128)(2,1)S(1)}, u32[]{:S(2)}, u32[]{:S(2)}) collective-permute-start(bf16[256,256]{1,0:T(8,128)(2,1)S(1)} %collective-permute-done.refs_5_), channel_id=1, source_target_pairs={{0,4},{1,5},{4,8},{5,9},{8,12},{9,13},{12,14},{13,15},{14,10},{15,... | collective-permute-start | bytes 393224 | tf_op jit(solution)/shard_map/ppermute | solution.py:229
  12.3 6.4 %collective-permute-start.11 = (bf16[256,256]{1,0:T(8,128)(2,1)S(1)}, bf16[256,256]{1,0:T(8,128)(2,1)S(1)}, u32[]{:S(2)}, u32[]{:S(2)}) collective-permute-start(bf16[256,256]{1,0:T(8,128)(2,1)S(1)} %collective-permute-done.3.refs_12_), channel_id=1, source_target_pairs={{4,0},{5,1},{8,4},{9,5},{12,8},{13,9},{14,12},{15,13},{10,14},{11,... | collective-permute-start | bytes 393224 | tf_op jit(solution)/shard_map/ppermute | solution.py:229
  14.2 12.9 %collective-permute-start.5 = (bf16[528,256]{1,0:T(8,128)(2,1)S(1)}, bf16[528,256]{1,0:T(8,128)(2,1)S(1)}, u32[]{:S(2)}, u32[]{:S(2)}) collective-permute-start(bf16[528,256]{1,0:T(8,128)(2,1)S(1)} %get-tuple-element.43.refs_2_.rest_10_), channel_id=1, source_target_pairs={{0,1},{1,0},{2,3},{3,2},{4,5},{5,4},{6,7},{7,6},{8,9},{9,8},{10,11... | collective-permute-start | bytes 811016 | tf_op jit(solution)/shard_map/ppermute | solution.py:229
  15.2 6.4 %collective-permute-start.8 = (bf16[256,256]{1,0:T(8,128)(2,1)S(1)}, bf16[256,256]{1,0:T(8,128)(2,1)S(1)}, u32[]{:S(2)}, u32[]{:S(2)}) collective-permute-start(bf16[256,256]{1,0:T(8,128)(2,1)S(1)} %collective-permute-done.2.refs_4_), channel_id=1, source_target_pairs={{0,4},{1,5},{4,8},{5,9},{8,12},{9,13},{12,14},{13,15},{14,10},{15,... | collective-permute-start | bytes 393224 | tf_op jit(solution)/shard_map/ppermute | solution.py:229
  17.2 6.0 %collective-permute-start.7 = (bf16[256,256]{1,0:T(8,128)(2,1)S(1)}, bf16[256,256]{1,0:T(8,128)(2,1)S(1)}, u32[]{:S(2)}, u32[]{:S(2)}) collective-permute-start(bf16[256,256]{1,0:T(8,128)(2,1)S(1)} %collective-permute-done.6.refs_6_), channel_id=1, source_target_pairs={{0,4},{1,5},{4,8},{5,9},{8,12},{9,13},{12,14},{13,15},{14,10},{15,... | collective-permute-start | bytes 393224 | tf_op jit(solution)/shard_map/ppermute | solution.py:229
  18.8 5.2 %collective-permute-start.12 = (bf16[256,256]{1,0:T(8,128)(2,1)S(1)}, bf16[256,256]{1,0:T(8,128)(2,1)S(1)}, u32[]{:S(2)}, u32[]{:S(2)}) collective-permute-start(bf16[256,256]{1,0:T(8,128)(2,1)S(1)} %collective-permute-done.11.refs_13_), channel_id=1, source_target_pairs={{4,0},{5,1},{8,4},{9,5},{12,8},{13,9},{14,12},{15,13},{10,14},{11,... | collective-permute-start | bytes 393224 | tf_op jit(solution)/shard_map/ppermute | solution.py:229
  21.6 5.6 %collective-permute-start.10 = (bf16[256,256]{1,0:T(8,128)(2,1)S(1)}, bf16[256,256]{1,0:T(8,128)(2,1)S(1)}, u32[]{:S(2)}, u32[]{:S(2)}) collective-permute-start(bf16[256,256]{1,0:T(8,128)(2,1)S(1)} %collective-permute-done.9.refs_9_), channel_id=1, source_target_pairs={{4,0},{5,1},{8,4},{9,5},{12,8},{13,9},{14,12},{15,13},{10,14},{11,... | collective-permute-start | bytes 393224 | tf_op jit(solution)/shard_map/ppermute | solution.py:229
  23.1 5.1 %collective-permute-start.13 = (bf16[256,256]{1,0:T(8,128)(2,1)S(1)}, bf16[256,256]{1,0:T(8,128)(2,1)S(1)}, u32[]{:S(2)}, u32[]{:S(2)}) collective-permute-start(bf16[256,256]{1,0:T(8,128)(2,1)S(1)} %collective-permute-done.7.refs_7_), channel_id=1, source_target_pairs={{0,4},{1,5},{4,8},{5,9},{8,12},{9,13},{12,14},{13,15},{14,10},{15,... | collective-permute-start | bytes 393224 | tf_op jit(solution)/shard_map/ppermute | solution.py:229
  24.0 5.0 %collective-permute-start.14 = (bf16[256,256]{1,0:T(8,128)(2,1)S(1)}, bf16[256,256]{1,0:T(8,128)(2,1)S(1)}, u32[]{:S(2)}, u32[]{:S(2)}) collective-permute-start(bf16[256,256]{1,0:T(8,128)(2,1)S(1)} %collective-permute-done.12.refs_14_), channel_id=1, source_target_pairs={{4,0},{5,1},{8,4},{9,5},{12,8},{13,9},{14,12},{15,13},{10,14},{11,... | collective-permute-start | bytes 393224 | tf_op jit(solution)/shard_map/ppermute | solution.py:229
  29.9 1.4 %collective-permute-start.16 = (f32[136,256]{1,0:T(8,128)S(1)}, f32[136,256]{1,0:T(8,128)S(1)}, u32[]{:S(2)}, u32[]{:S(2)}) collective-permute-start(f32[136,256]{1,0:T(8,128)S(1)} %get-tuple-element.60), channel_id=1, source_target_pairs={{0,1},{1,0},{2,3},{3,2},{4,5},{5,4},{6,7},{7,6},{8,9},{9,8},{10,11... | collective-permute-start | bytes 417800 | tf_op jit(solution)/shard_map/ppermute | solution.py:229
  30.0 3.0 %collective-permute-start.23 = (f32[128,256]{1,0:T(8,128)S(1)}, f32[128,256]{1,0:T(8,128)S(1)}, u32[]{:S(2)}, u32[]{:S(2)}) collective-permute-start(f32[128,256]{1,0:T(8,128)S(1)} %get-tuple-element.70), channel_id=1, source_target_pairs={{0,1},{1,0},{2,3},{3,2},{4,5},{5,4},{6,7},{7,6},{8,9},{9,8},{10,11... | collective-permute-start | bytes 393224 | tf_op jit(solution)/shard_map/ppermute | solution.py:229
  30.5 17.4 %collective-permute-start.15 = (f32[256,256]{1,0:T(8,128)S(1)}, f32[256,256]{1,0:T(8,128)S(1)}, u32[]{:S(2)}, u32[]{:S(2)}) collective-permute-start(f32[256,256]{1,0:T(8,128)S(1)} %get-tuple-element.56), channel_id=1, source_target_pairs={{0,1},{1,0},{2,3},{3,2},{4,5},{5,4},{6,7},{7,6},{8,9},{9,8},{10,11... | collective-permute-start | bytes 786440 | tf_op jit(solution)/shard_map/ppermute | solution.py:229
  31.3 4.4 %collective-permute-start.19 = (bf16[136,256]{1,0:T(8,128)(2,1)S(1)}, bf16[136,256]{1,0:T(8,128)(2,1)S(1)}, u32[]{:S(2)}, u32[]{:S(2)}) collective-permute-start(bf16[136,256]{1,0:T(8,128)(2,1)S(1)} %add.24), channel_id=1, source_target_pairs={{0,2},{1,3},{2,0},{3,1},{4,6},{5,7},{6,4},{7,5},{8,10},{9,11},{10,... | collective-permute-start | bytes 208904 | tf_op jit(solution)/shard_map/ppermute | solution.py:229
  33.0 4.5 %collective-permute-start.24 = (bf16[128,256]{1,0:T(8,128)(2,1)S(1)}, bf16[128,256]{1,0:T(8,128)(2,1)S(1)}, u32[]{:S(2)}, u32[]{:S(2)}) collective-permute-start(bf16[128,256]{1,0:T(8,128)(2,1)S(1)} %add_convert_fusion.4), channel_id=1, source_target_pairs={{0,4},{1,5},{2,6},{3,7},{4,0},{5,1},{6,2},{7,3},{8,12},{9,13},{10,... | collective-permute-start | bytes 196616 | tf_op jit(solution)/shard_map/ppermute | solution.py:229
  34.6 10.9 %collective-permute-start.17 = (bf16[256,256]{1,0:T(8,128)(2,1)S(1)}, bf16[256,256]{1,0:T(8,128)(2,1)S(1)}, u32[]{:S(2)}, u32[]{:S(2)}) collective-permute-start(bf16[256,256]{1,0:T(8,128)(2,1)S(1)} %collective-permute-done.8.refs_5_), channel_id=1, source_target_pairs={{0,4},{1,5},{4,8},{5,9},{8,12},{9,13},{12,14},{13,15},{14,10},{15,... | collective-permute-start | bytes 393224 | tf_op jit(solution)/shard_map/ppermute | solution.py:229
  35.7 5.3 %collective-permute-start.20 = (bf16[136,256]{1,0:T(8,128)(2,1)S(1)}, bf16[136,256]{1,0:T(8,128)(2,1)S(1)}, u32[]{:S(2)}, u32[]{:S(2)}) collective-permute-start(bf16[136,256]{1,0:T(8,128)(2,1)S(1)} %add_convert_fusion.1), channel_id=1, source_target_pairs={{0,4},{1,5},{2,6},{3,7},{4,0},{5,1},{6,2},{7,3},{8,12},{9,13},{10,... | collective-permute-start | bytes 208904 | tf_op jit(solution)/shard_map/ppermute | solution.py:229
  37.5 5.8 %collective-permute-start.25 = (bf16[128,256]{1,0:T(8,128)(2,1)S(1)}, bf16[128,256]{1,0:T(8,128)(2,1)S(1)}, u32[]{:S(2)}, u32[]{:S(2)}) collective-permute-start(bf16[128,256]{1,0:T(8,128)(2,1)S(1)} %add_convert_fusion.3), channel_id=1, source_target_pairs={{0,8},{1,9},{2,10},{3,11},{4,12},{5,13},{6,14},{7,15},{8,0},{9,1},... | collective-permute-start | bytes 196616 | tf_op jit(solution)/shard_map/ppermute | solution.py:229
  41.0 5.5 %collective-permute-start.21 = (bf16[136,256]{1,0:T(8,128)(2,1)S(1)}, bf16[136,256]{1,0:T(8,128)(2,1)S(1)}, u32[]{:S(2)}, u32[]{:S(2)}) collective-permute-start(bf16[136,256]{1,0:T(8,128)(2,1)S(1)} %add_convert_fusion), channel_id=1, source_target_pairs={{0,8},{1,9},{2,10},{3,11},{4,12},{5,13},{6,14},{7,15},{8,0},{9,1},... | collective-permute-start | bytes 208904 | tf_op jit(solution)/shard_map/ppermute | solution.py:229
  43.3 4.5 %collective-permute-start.26 = (bf16[128,256]{1,0:T(8,128)(2,1)S(1)}, bf16[128,256]{1,0:T(8,128)(2,1)S(1)}, u32[]{:S(2)}, u32[]{:S(2)}) collective-permute-start(bf16[128,256]{1,0:T(8,128)(2,1)S(1)} %add_convert_fusion.2), channel_id=1, source_target_pairs={{0,2},{1,3},{2,0},{3,1},{4,6},{5,7},{6,4},{7,5},{8,10},{9,11},{10,... | collective-permute-start | bytes 196616 | tf_op jit(solution)/shard_map/ppermute | solution.py:229
  45.5 2.4 %copy-start = (bf16[256,256]{1,0:T(8,128)(2,1)S(1)}, bf16[256,256]{1,0:T(8,128)(2,1)}, u32[]{:S(2)}) copy-start(bf16[256,256]{1,0:T(8,128)(2,1)} %cross.3) | copy-start | bytes 393220
  45.5 3.7 %copy-start.1 = (f32[256,256]{1,0:T(8,128)S(1)}, f32[256,256]{1,0:T(8,128)}, u32[]{:S(2)}) copy-start(f32[256,256]{1,0:T(8,128)} %diag_one.1) | copy-start | bytes 786436
  45.5 3.7 %copy-start.2 = (f32[256,256]{1,0:T(8,128)S(1)}, f32[256,256]{1,0:T(8,128)}, u32[]{:S(2)}) copy-start(f32[256,256]{1,0:T(8,128)} %diag_two.1) | copy-start | bytes 786436
  45.9 2.0 %collective-permute-start.18 = (f32[256,256]{1,0:T(8,128)S(1)}, f32[256,256]{1,0:T(8,128)S(1)}, u32[]{:S(2)}, u32[]{:S(2)}) collective-permute-start(f32[256,256]{1,0:T(8,128)S(1)} %get-tuple-element.63), channel_id=1, source_target_pairs={{0,1},{1,0},{2,3},{3,2},{4,5},{5,4},{6,7},{7,6},{8,9},{9,8},{10,11... | collective-permute-start | bytes 786440 | tf_op jit(solution)/shard_map/ppermute | solution.py:229
  46.6 2.4 %collective-permute-start.22 = (f32[136,256]{1,0:T(8,128)S(1)}, f32[136,256]{1,0:T(8,128)S(1)}, u32[]{:S(2)}, u32[]{:S(2)}) collective-permute-start(f32[136,256]{1,0:T(8,128)S(1)} %convert_add_fusion.pack_a), channel_id=1, source_target_pairs={{0,1},{1,0},{2,3},{3,2},{4,5},{5,4},{6,7},{7,6},{8,9},{9,8},{10,11... | collective-permute-start | bytes 417800 | tf_op jit(solution)/shard_map/ppermute | solution.py:229
  47.8 1.4 %collective-permute-start.27 = (f32[128,256]{1,0:T(8,128)S(1)}, f32[128,256]{1,0:T(8,128)S(1)}, u32[]{:S(2)}, u32[]{:S(2)}) collective-permute-start(f32[128,256]{1,0:T(8,128)S(1)} %convert_add_fusion.1.cross_a), channel_id=1, source_target_pairs={{0,1},{1,0},{2,3},{3,2},{4,5},{5,4},{6,7},{7,6},{8,9},{9,8},{10,11... | collective-permute-start | bytes 393224 | tf_op jit(solution)/shard_map/ppermute | solution.py:229
